TPU v7x, 32 devices: a whole 2x2x4 slice. The times are simulated.
32 devices in a mesh: date: 4 (over x, core), tile: 4 (over z), col: 2 (over y).
Axes of the slice: x: 2, y: 2, z: 4, core: 2. Of those that a mesh axis runs over, the one named last changes fastest.
Arguments:
- arrivals: bfloat16 [1, 16, 2, 4, 16, 16, 1280], P(None, None, 'col', 'date', 'tile'), may hold values from -24 to 24
- owner_map: int32 [1, 16], replicated, may hold values from 0 to 15, each once within a row
- block_ids: int32 [1, 16, 2], P(None, ('date', 'tile'), 'col'), may hold values from 0 to 15
- tile_valid: int32 [1, 16, 2], P(None, ('date', 'tile'), 'col'), may hold values 0 or 1
- blend_weights: int32 [1, 16, 2, 2, 224], P(None, ('date', 'tile'), 'col'), may hold values from 1 to 8
- location_table: bfloat16 [16, 1280], replicated, may hold values from -3 to 3
- norm_gain: bfloat16 [1280], replicated, may hold values from 0.099609375 to 1.8984375
- qkv_weight: bfloat16 [1280, 3840], replicated, may hold values from -4 to 4
- out_weight: bfloat16 [1280, 1280], replicated, may hold values from -0.3125 to 0.3125
- final_gain: bfloat16 [1280], replicated, may hold values from 0.099609375 to 1.8984375
- reduce_weight: bfloat16 [5120, 256], replicated, may hold values from -0.078125 to 0.078125
- reduce_bias: bfloat16 [256], replicated, may hold values from -3 to 3
- upsample_weight: bfloat16 [256, 3136], replicated, may hold values from -0.375 to 0.375
- class_weight: bfloat16 [9, 13, 16], replicated, may hold values from -1.5 to 1.5
- class_bias: bfloat16 [13], replicated, may hold values from -3 to 3
Outputs:
- composite: float32 [1, 13, 3072, 384], P(None, None, ('date', 'tile'), 'col')
Inputs may be any that keep to these rules, and one draw needn't show every extreme that they name: `owner_map`: each scene's row names every tile row of the composite once.
All inputs are finite; a program needn't handle non-finite values. No bound on the sum of `tile_valid` on one device may be relied on, other than what follows from the above.
Results may differ from a plain program's by a relative error of at most 0.009.
Values may be sent and summed in bfloat16 or wider, within the bound.
No kernel may reach another device: no remote copies, remote signals or barrier semaphores. Data moves between devices by JAX's collectives and lax.ppermute only.
A program may use at most 256 MiB of HBM per device.

v0:
```python
import math

import jax
import jax.numpy as jnp
from jax import lax
from jax.sharding import PartitionSpec as P

HEADS = 16
DATES = 4
TILE_PX = 224
PATCH = 14
INTERSECTION = 32
FEAT = 16
NBLOCK = 16
PATCHES = 16
N_TOK = 1024
RIM = 16
STRIDE = 192


norm_eps = 1e-06


def with_halo(value, sides, width):
    for axis, dim in sides:
        size, length = (lax.axis_size(axis), value.shape[dim])
        up = [(i, (i + 1) % size) for i in range(size - 1)]
        down = [(j, i) for i, j in up]
        last = lax.slice_in_dim(value, length - width, length, axis=dim)
        initial = lax.slice_in_dim(value, 0, width, axis=dim)
        before = lax.ppermute(last, axis, up)
        after = lax.ppermute(initial, axis, down)
        value = jnp.concatenate([before, value, after], axis=dim)
    return value


def layer_norm(values, gain_row):
    average = jnp.mean(values, axis=-1, keepdims=True)
    centered = values - average
    spread = jnp.mean(centered * centered, axis=-1, keepdims=True)
    return centered * lax.rsqrt(spread + norm_eps) * gain_row.astype(jnp.float32)


def encode_tile(tokens, location, norm_gain, qkv_weight, out_weight, final_gain):
    token_count = tokens.shape[0]
    model_width = tokens.shape[1]
    head_width = model_width // HEADS
    residual = tokens.astype(jnp.float32) + location[None, :]
    normed = layer_norm(residual, norm_gain).astype(jnp.bfloat16)
    qkv_heads = qkv_weight.reshape(model_width, 3, HEADS, head_width)
    packed = jnp.einsum(
        "nd,dthe->thne", normed, qkv_heads, preferred_element_type=jnp.float32
    ).astype(jnp.bfloat16)
    queries = packed[0]
    key_rows = packed[1]
    value_rows = packed[2]
    block_rows = min(512, token_count)
    score_scale = 1.0 / math.sqrt(head_width)
    mixed_blocks = []
    for first_row in range(0, token_count, block_rows):
        query_block = queries[:, first_row : first_row + block_rows]
        scores = (
            jnp.einsum("hqd,hkd->hqk", query_block, key_rows, preferred_element_type=jnp.float32)
            * score_scale
        )
        highest = jnp.max(scores, axis=-1, keepdims=True)
        lifted = jnp.exp(scores - highest)
        attention = (lifted / jnp.sum(lifted, axis=-1, keepdims=True)).astype(jnp.bfloat16)
        mixed_blocks.append(
            jnp.einsum(
                "hqk,hkd->hqd", attention, value_rows, preferred_element_type=jnp.float32
            ).astype(jnp.bfloat16)
        )
    mixed_heads = jnp.concatenate(mixed_blocks, axis=1)
    out_heads = out_weight.reshape(HEADS, head_width, model_width)
    updated = residual + jnp.einsum(
        "hqd,hde->qe", mixed_heads, out_heads, preferred_element_type=jnp.float32
    )
    return layer_norm(updated, final_gain).astype(jnp.bfloat16)


def decode_tile(encoded, reduce_weight, reduce_bias, upsample_weight):
    model_width = encoded.shape[1]
    by_date = encoded.reshape(DATES, PATCHES * PATCHES, model_width)
    weight_by_date = reduce_weight.reshape(DATES, model_width, reduce_weight.shape[1])
    summed = jnp.einsum("tpd,tdc->pc", by_date, weight_by_date, preferred_element_type=jnp.float32)
    reduced = jax.nn.gelu(summed + reduce_bias.astype(jnp.float32), approximate=False).astype(
        jnp.bfloat16
    )
    upsampled = jnp.dot(reduced, upsample_weight, preferred_element_type=jnp.float32).astype(
        jnp.bfloat16
    )
    pixels = upsampled.reshape(PATCHES, PATCHES, FEAT, PATCH, PATCH).transpose(2, 0, 3, 1, 4)
    return pixels.reshape(FEAT, TILE_PX, TILE_PX)


def frame_edges(features, axis):
    far_edge = TILE_PX - INTERSECTION - 1
    first_row = lax.slice_in_dim(features, INTERSECTION, INTERSECTION + 1, axis=axis)
    last_row = lax.slice_in_dim(features, far_edge, far_edge + 1, axis=axis)
    return jnp.concatenate([first_row, features, last_row], axis=axis)


def keep_outer(widened, axis):
    upper_cell = lax.slice_in_dim(widened, 0, 1, axis=axis)
    inner_cells = lax.slice_in_dim(widened, 2, TILE_PX + 2, axis=axis)
    lower_cell = lax.slice_in_dim(widened, TILE_PX + 3, TILE_PX + 4, axis=axis)
    return jnp.concatenate([upper_cell, inner_cells, lower_cell], axis=axis)


def classify(padded, class_weight, class_bias):
    total = class_bias.astype(jnp.float32)[None, :, None, None]
    for offset in range(9):
        row_off = offset // 3
        col_off = offset % 3
        window = padded[:, :, row_off : row_off + TILE_PX, col_off : col_off + TILE_PX]
        total = total + jnp.einsum(
            "kf,bfhw->bkhw", class_weight[offset], window, preferred_element_type=jnp.float32
        )
    return total


def fold_rims(extended, axis):
    main_part = lax.slice_in_dim(extended, 2 * RIM, 2 * RIM + STRIDE, axis=axis)
    upper_rim = lax.slice_in_dim(extended, 0, RIM, axis=axis)
    lower_rim = lax.slice_in_dim(extended, TILE_PX + RIM, TILE_PX + 2 * RIM, axis=axis)
    filler = jnp.zeros_like(lax.slice_in_dim(main_part, 0, STRIDE - RIM, axis=axis))
    return (
        main_part
        + jnp.concatenate([upper_rim, filler], axis=axis)
        + jnp.concatenate([filler, lower_rim], axis=axis)
    )


def local(
    arrivals,
    owner_map,
    block_ids,
    tile_valid,
    blend_weights,
    location_table,
    norm_gain,
    qkv_weight,
    out_weight,
    final_gain,
    reduce_weight,
    reduce_bias,
    upsample_weight,
    class_weight,
    class_bias,
):
    arrival_order = jnp.argsort(owner_map, axis=1)
    ordered = jax.vmap(lambda scene_rows, scene_order: jnp.take(scene_rows, scene_order, axis=0))(
        arrivals, arrival_order
    )
    scenes = ordered.shape[0]
    strip_rows = ordered.shape[4]
    model_width = ordered.shape[6]
    merged = ordered.reshape(
        scenes, ordered.shape[1], ordered.shape[2], strip_rows, PATCHES, model_width
    )
    arrived = lax.all_to_all(merged, ("date", "tile"), split_axis=1, concat_axis=3, tiled=True)
    tile_tokens = arrived.reshape(-1, N_TOK, model_width)
    codes = block_ids.reshape(-1)
    one_hot = (codes[:, None] == jnp.arange(NBLOCK, dtype=jnp.int32)[None, :]).astype(jnp.bfloat16)
    locations = jnp.dot(one_hot, location_table, preferred_element_type=jnp.float32)

    def per_tile(inputs):
        tokens, location = inputs
        encoded = encode_tile(tokens, location, norm_gain, qkv_weight, out_weight, final_gain)
        return decode_tile(encoded, reduce_weight, reduce_bias, upsample_weight)

    features = lax.map(per_tile, (tile_tokens, locations))
    framed = frame_edges(frame_edges(features, 2), 3)
    widened = with_halo(framed, ((("date", "tile"), 2), ("col", 3)), 1)
    padded = keep_outer(keep_outer(widened, 2), 3)
    logits = classify(padded, class_weight, class_bias)
    profiles = blend_weights.reshape(scenes, 2, TILE_PX).astype(jnp.float32)
    valid_float = tile_valid.reshape(scenes).astype(jnp.float32)
    plane = valid_float[:, None, None] * profiles[:, 0, :, None] * profiles[:, 1, None, :]
    weighted = logits * plane[:, None]
    near_weighted, near_plane = (
        with_halo(weighted.astype(jnp.bfloat16), ((("date", "tile"), 2), ("col", 3)), RIM).astype(
            weighted.dtype
        ),
        with_halo(
            plane[:, None].astype(jnp.bfloat16), ((("date", "tile"), 2), ("col", 3)), RIM
        ).astype(jnp.float32),
    )
    numerator = fold_rims(fold_rims(near_weighted, 2), 3)
    denominator = fold_rims(fold_rims(near_plane, 2), 3)
    return numerator / jnp.maximum(denominator, 1.0)


def solution(mesh):
    placed = (
        P(None, None, "col", "date", "tile", None, None),
        P(),
        P(None, ("date", "tile"), "col"),
        P(None, ("date", "tile"), "col"),
        P(None, ("date", "tile"), "col", None, None),
        P(),
        P(),
        P(),
        P(),
        P(),
        P(),
        P(),
        P(),
        P(),
        P(),
    )
    return jax.shard_map(
        local,
        mesh=mesh,
        in_specs=placed,
        out_specs=P(None, None, ("date", "tile"), "col"),
        check_vma=False,
    )
```

profile of v0, /device:TPU:0, one launch (start us, length us, event | category | flops | bytes accessed | tf_op | source)
XLA Modules:
  0.0 390.8 jit_solution(16630025080000331534)
XLA Ops:
  1.8 4.0 %gather_fusion = bf16[16,4,16,1280]{3,2,1,0:T(8,128)(2,1)} fusion(bf16[1,16,4,16,1280]{4,3,2,1,0:T(8,128)(2,1)} %bitcast.214, s32[16]{0:T(128)S(1)} %or_bitcast_fusion), kind=kCustom, calls=%fused_computation | custom fusion | bytes 5243008 | tf_op jit(solution)/shard_map/vmap(jit(_take))/gather | solution.py:153
  5.8 3.5 bitcast_select_fusion
  9.4 7.5 %all-to-all-start = ((bf16[1,16,1,4,16,1280]{5,4,3,2,0,1:T(8,128)(2,1)}), bf16[1,16,1,4,16,1280]{5,4,3,2,0,1:T(8,128)(2,1)}, u32[]{:S(2)}, u32[]{:S(2)}) async-start(bf16[1,16,1,4,16,1280]{5,4,3,2,0,1:T(8,128)(2,1)} %bitcast_select_fusion), calls=%async_computation | async-start | bytes 5242880 | tf_op jit(solution)/shard_map/all_to_all | solution.py:162
  17.7 3.8 collective-permute-start.8
  24.3 36.3 %collective-permute-done.8 = bf16[1,1,16,224]{3,2,1,0:T(8,128)(2,1)S(1)} collective-permute-done((bf16[1,1,16,224]{3,2,1,0:T(8,128)(2,1)S(1)}, bf16[1,1,16,224]{3,2,1,0:T(8,128)(2,1)S(1)}, u32[]{:S(2)}, u32[]{:S(2)}) %collective-permute-start.8) | collective-permute-done | bytes 7200 | tf_op jit(solution)/shard_map/ppermute | solution.py:31
  60.7 3.4 collective-permute-start.10
  66.3 4.0 %collective-permute-done.11 = bf16[1,1,256,16]{3,2,1,0:T(8,128)(2,1)S(1)} collective-permute-done((bf16[1,1,256,16]{3,2,1,0:T(8,128)(2,1)S(1)}, bf16[1,1,256,16]{3,2,1,0:T(8,128)(2,1)S(1)}, u32[]{:S(2)}, u32[]{:S(2)}) %collective-permute-start.11) | collective-permute-done | bytes 8224 | tf_op jit(solution)/shard_map/ppermute | solution.py:32
  71.8 6.0 %all-to-all-done = bf16[1,16,1,4,16,1280]{5,4,3,2,0,1:T(8,128)(2,1)} async-done(((bf16[1,16,1,4,16,1280]{5,4,3,2,0,1:T(8,128)(2,1)}), bf16[1,16,1,4,16,1280]{5,4,3,2,0,1:T(8,128)(2,1)}, u32[]{:S(2)}, u32[]{:S(2)}) %all-to-all-start) | async-done | bytes 2621472 | tf_op jit(solution)/shard_map/all_to_all | solution.py:162
  77.8 2.3 add_reduce_fusion
  80.1 2.7 multiply_reduce_fusion.3
  82.9 2.7 multiply_convert_fusion.1
  85.6 16.5 %fusion.214 = f32[1024,3840]{0,1} fusion(bf16[1024,1280]{1,0:T(8,128)(2,1)S(1)} %bitcast.215, bf16[1280,3840]{1,0:T(8,128)(2,1)} %param.22), kind=kOutput, calls=%fused_computation.265 | convolution fusion | flops 10066329600 | bytes 28180480
  102.0 9.8 %convert_bitcast_fusion = bf16[3,16,1024,80]{2,3,1,0:T(8,128)(2,1)} fusion(f32[1024,3,16,80]{0,3,2,1:T(8,128)} %bitcast.213), kind=kLoop, calls=%fused_computation.15 | loop fusion | flops 3932160 | bytes 23592960 | tf_op jit(solution)/shard_map/while/body/eval_jaxpr/convert_element_type | solution.py:53
  111.8 3.7 slice_bitcast_fusion.2
  115.5 17.5 %fusion.208 = (f32[16,512]{1,0:T(8,128)S(1)}, f32[16,512,1024]{2,1,0:T(8,128)}) fusion(bf16[3,16,1024,80]{2,3,1,0:T(8,128)(2,1)} %convert_bitcast_fusion, bf16[16,1024,80]{1,2,0:T(8,128)(2,1)} %slice_bitcast_fusion.2), kind=kOutput, calls=%fused_computation.263 | convolution fusion | flops 1367344128 | bytes 37519360 | tf_op jit(solution)/shard_map/while/body/eval_jaxpr/sub | solution.py:67
  133.0 18.0 %fusion.203 = (f32[16,512]{1,0:T(8,128)S(1)}, f32[16,512,1024]{2,1,0:T(8,128)}) fusion(bf16[3,16,1024,80]{2,3,1,0:T(8,128)(2,1)} %convert_bitcast_fusion, bf16[16,1024,80]{1,2,0:T(8,128)(2,1)} %slice_bitcast_fusion.2), kind=kOutput, calls=%fused_computation.262 | convolution fusion | flops 1367344128 | bytes 37519360 | tf_op jit(solution)/shard_map/while/body/eval_jaxpr/sub | solution.py:67
  151.0 15.2 %fusion.70 = bf16[16,512,80]{1,2,0:T(8,128)(2,1)} fusion(bf16[3,16,1024,80]{2,3,1,0:T(8,128)(2,1)} %convert_bitcast_fusion, f32[16,512,1024]{2,1,0:T(8,128)} %get-tuple-element.65, f32[16,512]{1,0:T(8,128)S(1)} %get-tuple-element.64), kind=kOutput, calls=%fused_computation.101 | convolution fusion | flops 1359609856 | bytes 37519360 | tf_op jit(solution)/shard_map/while/body/eval_jaxpr/hqk,hkd->hqd/dot_general | solution.py:70
  166.2 15.3 %fusion.69 = bf16[16,512,80]{1,2,0:T(8,128)(2,1)} fusion(bf16[3,16,1024,80]{2,3,1,0:T(8,128)(2,1)} %convert_bitcast_fusion, f32[16,512,1024]{2,1,0:T(8,128)} %get-tuple-element.63, f32[16,512]{1,0:T(8,128)S(1)} %get-tuple-element.62), kind=kOutput, calls=%fused_computation.100 | convolution fusion | flops 1359609856 | bytes 37519360 | tf_op jit(solution)/shard_map/while/body/eval_jaxpr/hqk,hkd->hqd/dot_general | solution.py:70
  181.5 6.7 %fusion.213 = (f32[1024]{0:T(1024)S(1)}, f32[1024,1280]{1,0:T(8,128)S(1)}) fusion(bf16[16,80,1280]{2,1,0:T(8,128)(2,1)S(1)} %bitcast.210, bf16[16,512,80]{1,2,0:T(8,128)(2,1)} %fusion.69, bf16[16,512,80]{1,2,0:T(8,128)(2,1)} %fusion.70, f32[1280]{0:T(1024)S(1)} %convolution_reduce_fusion, bf16[1,16,1,4,16,1280]{5,4,3,2,0,1:T(8,128)(2,1)} %all-to-all-done), kind=kOutput, calls=%fused_computation.264 | convolution fusion | flops 3365927936 | bytes 13771776 | tf_op jit(solution)/shard_map/while/body/eval_jaxpr/hqd,hde->qe/dot_general | solution.py:76
  189.7 6.1 %convolution_convert_fusion = bf16[256,3136]{0,1:T(8,128)(2,1)} fusion(bf16[256,3136]{0,1:T(8,128)(2,1)} %param.27, bf16[4,256,1280]{2,1,0:T(8,128)(2,1)S(1)} %bitcast.216, bf16[4,1280,256]{2,1,0:T(8,128)(2,1)} %bitcast.222, f32[256]{0:T(256)S(1)} %convert_element_type.151), kind=kOutput, calls=%fused_computation.22 | convolution fusion | flops 1087258624 | bytes 8455168 | tf_op jit(solution)/shard_map/while/body/eval_jaxpr/dot_general | solution.py:90
  195.7 13.7 %reshape.427 = bf16[16,16,16,14,14]{1,0,4,3,2:T(8,128)(2,1)} reshape(bf16[256,3136]{0,1:T(8,128)(2,1)} %convolution_convert_fusion) | data formatting | bytes 3211264 | tf_op jit(solution)/shard_map/while/body/eval_jaxpr/reshape | solution.py:93
  209.4 27.6 %copy.38 = bf16[16,16,16,14,14]{4,1,3,0,2:T(8,128)(2,1)} copy(bf16[16,16,16,14,14]{1,0,4,3,2:T(8,128)(2,1)} %reshape.427) | data formatting | bytes 3211264 | tf_op jit(solution)/shard_map/while/body/eval_jaxpr/reshape | solution.py:93
  237.1 19.3 %broadcast_in_dim.53 = bf16[1,16,224,224]{3,2,1,0:T(8,128)(2,1)} reshape(bf16[16,16,14,16,14]{4,3,2,1,0:T(8,128)(2,1)} %bitcast.211) | data formatting | bytes 3211264 | tf_op jit(solution)/shard_map/while/body/jit(dynamic_update_index_in_dim)/broadcast_in_dim | solution.py:173
  256.4 2.5 copy.39
  260.9 13.4 %collective-permute-start = (bf16[1,16,1,226]{3,1,2,0:T(8,128)(2,1)S(1)}, bf16[1,16,1,226]{3,1,2,0:T(8,128)(2,1)S(1)}, u32[]{:S(2)}, u32[]{:S(2)}) collective-permute-start(bf16[1,16,1,226]{3,1,2,0:T(8,128)(2,1)S(1)} %get-tuple-element.27), channel_id=1, source_target_pairs={{0,2},{2,4},{4,6},{6,8},{8,10},{10,12},{12,14},{14,16},{16,18},{18... | collective-permute-start | bytes 21704 | tf_op jit(solution)/shard_map/ppermute | solution.py:31
  275.8 19.1 %reshape.432 = bf16[16,224,224]{2,1,0:T(8,128)(2,1)} reshape(bf16[16,16,14,16,14]{4,3,2,1,0:T(8,128)(2,1)} %bitcast.212) | data formatting | bytes 3211264 | tf_op jit(solution)/shard_map/reshape.36
  294.9 3.2 pad_maximum_fusion.1
  299.8 1.9 copy.42
  303.3 1.9 copy.43
  306.5 4.5 %fusion.61 = f32[224,224,13]{1,2,0:T(8,128)} fusion(bf16[16,224,224]{2,1,0:T(8,128)(2,1)} %reshape.432, bf16[9,13,16]{2,1,0:T(8,128)(2,1)S(1)} %copy-done.21), kind=kOutput, calls=%fused_computation.92 | convolution fusion | flops 20873216 | bytes 4218880 | tf_op jit(solution)/shard_map/kf,bfhw->bkhw/dot_general | solution.py:117
  311.0 1.8 copy.44
  314.6 5.3 %pad_maximum_fusion.2 = bf16[1,16,228,228]{3,1,2,0:T(8,128)(2,1)S(1)} fusion(bf16[1,16,228,1]{3,1,2,0:T(8,128)(2,1)} %copy.45, bf16[1,16,1,226]{3,1,2,0:T(8,128)(2,1)S(1)} %collective-permute-done.1, bf16[1,16,226,1]{3,1,2,0:T(8,128)(2,1)} %copy-done.4, bf16[1,16,1,224]{3,1,2,0:T(8,128)(2,1)S(1)} %get-tuple-element.55, ...), kind=kLoop, calls=%fused_computation.58 | loop fusion | flops 14971392 | bytes 3326976 | tf_op jit(solution)/shard_map/concatenate | solution.py:33
  322.5 2.8 fusion.40
  325.4 2.8 fusion.36
  328.1 2.9 fusion.32
  331.0 2.9 fusion.28
  334.0 2.9 fusion.50
  336.8 2.6 fusion.46
  339.8 8.8 %fusion.71 = bf16[1,13,224,224]{3,1,2,0:T(8,128)(2,1)S(1)} fusion(f32[224,224]{1,0:T(8,128)S(1)} %copy-done.10, bf16[1,16,226,1]{3,1,2,0:T(8,128)(2,1)S(1)} %get-tuple-element.49, bf16[1,16,226,224]{3,1,2,0:T(8,128)(2,1)S(1)} %slice.275, f32[224,224,13]{1,2,0:T(8,128)} %fusion.46, f32[224,224,13]{1,2,0:T(8,128)} %fusion.50, f32[224,224,13]{1,2,0:T(8,128)} %fusion.28, ...), kind=kOutput, calls=%fused_computation.102 | convolution fusion | flops 31259648 | bytes 27310592 | tf_op jit(solution)/shard_map/kf,bfhw->bkhw/dot_general | solution.py:117
  348.6 4.6 %collective-permute-start.4 = (bf16[1,13,16,224]{3,1,2,0:T(8,128)(2,1)S(1)}, bf16[1,13,16,224]{3,1,2,0:T(8,128)(2,1)S(1)}, u32[]{:S(2)}, u32[]{:S(2)}) collective-permute-start(bf16[1,13,16,224]{3,1,2,0:T(8,128)(2,1)S(1)} %get-tuple-element.52), channel_id=1, source_target_pairs={{0,2},{2,4},{4,6},{6,8},{8,10},{10,12},{12,14},{14,16},{16,18},{18... | collective-permute-start | bytes 279560 | tf_op jit(solution)/shard_map/ppermute | solution.py:31
  356.6 3.5 collective-permute-done.5
  362.0 2.6 copy.47
  364.6 5.2 %collective-permute-start.6 = (bf16[1,13,256,16]{2,3,1,0:T(8,128)(2,1)}, bf16[1,13,256,16]{2,3,1,0:T(8,128)(2,1)}, u32[]{:S(2)}, u32[]{:S(2)}) collective-permute-start(bf16[1,13,256,16]{2,3,1,0:T(8,128)(2,1)} %copy.47), channel_id=1, source_target_pairs={{0,1},{2,3},{4,5},{6,7},{8,9},{10,11},{12,13},{14,15},{16,17},{18,... | collective-permute-start | bytes 319496 | tf_op jit(solution)/shard_map/ppermute | solution.py:31
  373.3 1.8 copy.49
  375.2 2.9 collective-permute-done.7
  378.1 2.8 copy.50
  382.1 2.0 maximum_convert_fusion
  387.7 3.0 copy.51
  (123 shorter events, 35.4 us)
Async XLA Ops:
  0.0 181.5 %copy-start = (bf16[1280,1280]{1,0:T(8,128)(2,1)S(1)}, bf16[1280,1280]{1,0:T(8,128)(2,1)}, u32[]{:S(2)}) copy-start(bf16[1280,1280]{1,0:T(8,128)(2,1)} %param.23) | copy-start | bytes 9830404
  9.3 8.2 %copy-start.25 = (s32[1,1,1,2,224]{4,3,2,1,0:T(2,128)S(1)}, s32[1,1,1,2,224]{4,3,2,1,0:T(2,128)}, u32[]{:S(2)}) copy-start(s32[1,1,1,2,224]{4,3,2,1,0:T(2,128)} %param.19) | copy-start | bytes 5380
  9.4 56.1 %copy-start.20 = (bf16[16,1280]{1,0:T(8,128)(2,1)S(1)}, bf16[16,1280]{1,0:T(8,128)(2,1)}, u32[]{:S(2)}) copy-start(bf16[16,1280]{1,0:T(8,128)(2,1)} %param.20) | copy-start | bytes 122884
  9.4 56.2 %copy-start.23 = (bf16[1280]{0:T(1024)(128)(2,1)S(1)}, bf16[1280]{0:T(1024)(128)(2,1)}, u32[]{:S(2)}) copy-start(bf16[1280]{0:T(1024)(128)(2,1)} %param.21) | copy-start | bytes 7684
  9.4 56.3 %copy-start.24 = (bf16[1280]{0:T(1024)(128)(2,1)S(1)}, bf16[1280]{0:T(1024)(128)(2,1)}, u32[]{:S(2)}) copy-start(bf16[1280]{0:T(1024)(128)(2,1)} %param.24) | copy-start | bytes 7684
  9.4 56.3 %copy-start.27 = (bf16[256]{0:T(256)(128)(2,1)S(1)}, bf16[256]{0:T(256)(128)(2,1)}, u32[]{:S(2)}) copy-start(bf16[256]{0:T(256)(128)(2,1)} %param.26) | copy-start | bytes 1540
  9.4 56.3 %copy-start.28 = (bf16[13]{0:T(256)(128)(2,1)S(1)}, bf16[13]{0:T(256)(128)(2,1)}, u32[]{:S(2)}) copy-start(bf16[13]{0:T(256)(128)(2,1)} %param.29) | copy-start | bytes 82
  9.4 68.4 %all-to-all-start = ((bf16[1,16,1,4,16,1280]{5,4,3,2,0,1:T(8,128)(2,1)}), bf16[1,16,1,4,16,1280]{5,4,3,2,0,1:T(8,128)(2,1)}, u32[]{:S(2)}, u32[]{:S(2)}) async-start(bf16[1,16,1,4,16,1280]{5,4,3,2,0,1:T(8,128)(2,1)} %bitcast_select_fusion), calls=%async_computation | async-start | bytes 5242880 | tf_op jit(solution)/shard_map/all_to_all | solution.py:162
  17.7 52.6 %copy-start.7 = (bf16[1,1,224,224]{3,2,1,0:T(8,128)(2,1)}, bf16[1,1,224,224]{3,2,1,0:T(8,128)(2,1)S(1)}, u32[]{:S(2)}) copy-start(bf16[1,1,224,224]{3,2,1,0:T(8,128)(2,1)S(1)} %multiply_convert_fusion.2) | copy-start | bytes 301060
  17.7 42.8 %collective-permute-start.8 = (bf16[1,1,16,224]{3,2,1,0:T(8,128)(2,1)S(1)}, bf16[1,1,16,224]{3,2,1,0:T(8,128)(2,1)S(1)}, u32[]{:S(2)}, u32[]{:S(2)}) collective-permute-start(bf16[1,1,16,224]{3,2,1,0:T(8,128)(2,1)S(1)} %get-tuple-element.58), channel_id=1, source_target_pairs={{0,2},{2,4},{4,6},{6,8},{8,10},{10,12},{12,14},{14,16},{16,18},{18... | collective-permute-start | bytes 21512 | tf_op jit(solution)/shard_map/ppermute | solution.py:31
  21.5 39.0 %collective-permute-start.9 = (bf16[1,1,16,224]{3,2,1,0:T(8,128)(2,1)S(1)}, bf16[1,1,16,224]{3,2,1,0:T(8,128)(2,1)S(1)}, u32[]{:S(2)}, u32[]{:S(2)}) collective-permute-start(bf16[1,1,16,224]{3,2,1,0:T(8,128)(2,1)S(1)} %get-tuple-element.59), channel_id=1, source_target_pairs={{2,0},{4,2},{6,4},{8,6},{10,8},{12,10},{14,12},{16,14},{18,16},{20... | collective-permute-start | bytes 21512 | tf_op jit(solution)/shard_map/ppermute | solution.py:32
  60.6 9.7 %copy-start.16 = (bf16[1,1,16,224]{3,2,1,0:T(8,128)(2,1)}, bf16[1,1,16,224]{3,2,1,0:T(8,128)(2,1)S(1)}, u32[]{:S(2)}) copy-start(bf16[1,1,16,224]{3,2,1,0:T(8,128)(2,1)S(1)} %collective-permute-done.8) | copy-start | bytes 21508
  60.6 9.7 %copy-start.18 = (bf16[1,1,16,224]{3,2,1,0:T(8,128)(2,1)}, bf16[1,1,16,224]{3,2,1,0:T(8,128)(2,1)S(1)}, u32[]{:S(2)}) copy-start(bf16[1,1,16,224]{3,2,1,0:T(8,128)(2,1)S(1)} %collective-permute-done.9) | copy-start | bytes 21508
  60.7 5.5 %collective-permute-start.10 = (bf16[1,1,256,16]{3,2,1,0:T(8,128)(2,1)S(1)}, bf16[1,1,256,16]{3,2,1,0:T(8,128)(2,1)S(1)}, u32[]{:S(2)}, u32[]{:S(2)}) collective-permute-start(bf16[1,1,256,16]{3,2,1,0:T(8,128)(2,1)S(1)} %get-tuple-element.56), channel_id=1, source_target_pairs={{0,1},{2,3},{4,5},{6,7},{8,9},{10,11},{12,13},{14,15},{16,17},{18,... | collective-permute-start | bytes 24584 | tf_op jit(solution)/shard_map/ppermute | solution.py:31
  64.1 6.2 %collective-permute-start.11 = (bf16[1,1,256,16]{3,2,1,0:T(8,128)(2,1)S(1)}, bf16[1,1,256,16]{3,2,1,0:T(8,128)(2,1)S(1)}, u32[]{:S(2)}, u32[]{:S(2)}) collective-permute-start(bf16[1,1,256,16]{3,2,1,0:T(8,128)(2,1)S(1)} %get-tuple-element.57), channel_id=1, source_target_pairs={{1,0},{3,2},{5,4},{7,6},{9,8},{11,10},{13,12},{15,14},{17,16},{19,... | collective-permute-start | bytes 24584 | tf_op jit(solution)/shard_map/ppermute | solution.py:32
  66.3 4.1 %copy-start.12 = (bf16[1,1,256,16]{3,2,1,0:T(8,128)(2,1)}, bf16[1,1,256,16]{3,2,1,0:T(8,128)(2,1)S(1)}, u32[]{:S(2)}) copy-start(bf16[1,1,256,16]{3,2,1,0:T(8,128)(2,1)S(1)} %collective-permute-done.10) | copy-start | bytes 24580
  70.3 0.6 copy-start.14
  259.3 16.4 %copy-start.8 = (bf16[1,1,224,224]{3,2,1,0:T(8,128)(2,1)S(1)}, bf16[1,1,224,224]{3,2,1,0:T(8,128)(2,1)}, u32[]{:S(2)}) copy-start(bf16[1,1,224,224]{3,2,1,0:T(8,128)(2,1)} %copy-done.7) | copy-start | bytes 301060
  259.3 16.4 %copy-start.13 = (bf16[1,1,256,16]{3,2,1,0:T(8,128)(2,1)S(1)}, bf16[1,1,256,16]{3,2,1,0:T(8,128)(2,1)}, u32[]{:S(2)}) copy-start(bf16[1,1,256,16]{3,2,1,0:T(8,128)(2,1)} %copy-done.12) | copy-start | bytes 24580
  259.3 16.4 %copy-start.15 = (bf16[1,1,256,16]{3,2,1,0:T(8,128)(2,1)S(1)}, bf16[1,1,256,16]{3,2,1,0:T(8,128)(2,1)}, u32[]{:S(2)}) copy-start(bf16[1,1,256,16]{3,2,1,0:T(8,128)(2,1)} %copy-done.14) | copy-start | bytes 24580
  259.3 16.4 %copy-start.17 = (bf16[1,1,16,224]{3,2,1,0:T(8,128)(2,1)S(1)}, bf16[1,1,16,224]{3,2,1,0:T(8,128)(2,1)}, u32[]{:S(2)}) copy-start(bf16[1,1,16,224]{3,2,1,0:T(8,128)(2,1)} %copy-done.16) | copy-start | bytes 21508
  259.3 16.4 %copy-start.19 = (bf16[1,1,16,224]{3,2,1,0:T(8,128)(2,1)S(1)}, bf16[1,1,16,224]{3,2,1,0:T(8,128)(2,1)}, u32[]{:S(2)}) copy-start(bf16[1,1,16,224]{3,2,1,0:T(8,128)(2,1)} %copy-done.18) | copy-start | bytes 21508
  259.9 0.9 copy-start.4
  260.9 34.0 %collective-permute-start = (bf16[1,16,1,226]{3,1,2,0:T(8,128)(2,1)S(1)}, bf16[1,16,1,226]{3,1,2,0:T(8,128)(2,1)S(1)}, u32[]{:S(2)}, u32[]{:S(2)}) collective-permute-start(bf16[1,16,1,226]{3,1,2,0:T(8,128)(2,1)S(1)} %get-tuple-element.27), channel_id=1, source_target_pairs={{0,2},{2,4},{4,6},{6,8},{8,10},{10,12},{12,14},{14,16},{16,18},{18... | collective-permute-start | bytes 21704 | tf_op jit(solution)/shard_map/ppermute | solution.py:31
  274.3 20.6 %collective-permute-start.1 = (bf16[1,16,1,226]{3,1,2,0:T(8,128)(2,1)S(1)}, bf16[1,16,1,226]{3,1,2,0:T(8,128)(2,1)S(1)}, u32[]{:S(2)}, u32[]{:S(2)}) collective-permute-start(bf16[1,16,1,226]{3,1,2,0:T(8,128)(2,1)S(1)} %get-tuple-element.28), channel_id=1, source_target_pairs={{2,0},{4,2},{6,4},{8,6},{10,8},{12,10},{14,12},{16,14},{18,16},{20... | collective-permute-start | bytes 21704 | tf_op jit(solution)/shard_map/ppermute | solution.py:32
  298.1 8.4 %copy-start.21 = (bf16[9,13,16]{2,1,0:T(8,128)(2,1)S(1)}, bf16[9,13,16]{2,1,0:T(8,128)(2,1)}, u32[]{:S(2)}) copy-start(bf16[9,13,16]{2,1,0:T(8,128)(2,1)} %param.28) | copy-start | bytes 11236
  301.7 9.3 %collective-permute-start.2 = (bf16[1,16,228,1]{2,1,3,0:T(8,128)(2,1)S(1)}, bf16[1,16,228,1]{2,1,3,0:T(8,128)(2,1)S(1)}, u32[]{:S(2)}, u32[]{:S(2)}) collective-permute-start(bf16[1,16,228,1]{2,1,3,0:T(8,128)(2,1)S(1)} %copy.42), channel_id=1, source_target_pairs={{0,1},{2,3},{4,5},{6,7},{8,9},{10,11},{12,13},{14,15},{16,17},{18,... | collective-permute-start | bytes 21896 | tf_op jit(solution)/shard_map/ppermute | solution.py:31
  305.2 7.6 %collective-permute-start.3 = (bf16[1,16,228,1]{2,1,3,0:T(8,128)(2,1)S(1)}, bf16[1,16,228,1]{2,1,3,0:T(8,128)(2,1)S(1)}, u32[]{:S(2)}, u32[]{:S(2)}) collective-permute-start(bf16[1,16,228,1]{2,1,3,0:T(8,128)(2,1)S(1)} %copy.43), channel_id=1, source_target_pairs={{1,0},{3,2},{5,4},{7,6},{9,8},{11,10},{13,12},{15,14},{17,16},{19,... | collective-permute-start | bytes 21896 | tf_op jit(solution)/shard_map/ppermute | solution.py:32
  336.8 2.7 copy-start.5
  336.8 2.9 copy-start.10
  336.8 2.9 copy-start.26
  339.8 14.9 %copy-start.9 = (f32[1,1,256,256]{3,2,1,0:T(8,128)S(1)}, f32[1,1,256,256]{3,2,1,0:T(8,128)}, u32[]{:S(2)}) copy-start(f32[1,1,256,256]{3,2,1,0:T(8,128)} %maximum_convert_fusion.2) | copy-start | bytes 786436
  339.8 14.9 %copy-start.22 = (pred[192]{0:T(512)(128)(4,1)S(1)}, pred[192]{0:T(512)(128)(4,1)}, u32[]{:S(2)}) copy-start(pred[192]{0:T(512)(128)(4,1)} %constant.144.clone.1) | copy-start | bytes 580
  348.6 13.4 %copy-start.2 = (bf16[1,13,224,224]{3,1,2,0:T(8,128)(2,1)}, bf16[1,13,224,224]{3,1,2,0:T(8,128)(2,1)S(1)}, u32[]{:S(2)}) copy-start(bf16[1,13,224,224]{3,1,2,0:T(8,128)(2,1)S(1)} %fusion.71) | copy-start | bytes 3913732
  348.6 8.0 %collective-permute-start.4 = (bf16[1,13,16,224]{3,1,2,0:T(8,128)(2,1)S(1)}, bf16[1,13,16,224]{3,1,2,0:T(8,128)(2,1)S(1)}, u32[]{:S(2)}, u32[]{:S(2)}) collective-permute-start(bf16[1,13,16,224]{3,1,2,0:T(8,128)(2,1)S(1)} %get-tuple-element.52), channel_id=1, source_target_pairs={{0,2},{2,4},{4,6},{6,8},{8,10},{10,12},{12,14},{14,16},{16,18},{18... | collective-permute-start | bytes 279560 | tf_op jit(solution)/shard_map/ppermute | solution.py:31
  353.2 6.9 %collective-permute-start.5 = (bf16[1,13,16,224]{3,1,2,0:T(8,128)(2,1)S(1)}, bf16[1,13,16,224]{3,1,2,0:T(8,128)(2,1)S(1)}, u32[]{:S(2)}, u32[]{:S(2)}) collective-permute-start(bf16[1,13,16,224]{3,1,2,0:T(8,128)(2,1)S(1)} %get-tuple-element.53), channel_id=1, source_target_pairs={{2,0},{4,2},{6,4},{8,6},{10,8},{12,10},{14,12},{16,14},{18,16},{20... | collective-permute-start | bytes 279560 | tf_op jit(solution)/shard_map/ppermute | solution.py:32
  362.0 18.9 %copy-start.3 = (bf16[1,13,224,224]{3,1,2,0:T(8,128)(2,1)S(1)}, bf16[1,13,224,224]{3,1,2,0:T(8,128)(2,1)}, u32[]{:S(2)}) copy-start(bf16[1,13,224,224]{3,1,2,0:T(8,128)(2,1)} %copy-done.2) | copy-start | bytes 3913732
  364.6 8.7 %collective-permute-start.6 = (bf16[1,13,256,16]{2,3,1,0:T(8,128)(2,1)}, bf16[1,13,256,16]{2,3,1,0:T(8,128)(2,1)}, u32[]{:S(2)}, u32[]{:S(2)}) collective-permute-start(bf16[1,13,256,16]{2,3,1,0:T(8,128)(2,1)} %copy.47), channel_id=1, source_target_pairs={{0,1},{2,3},{4,5},{6,7},{8,9},{10,11},{12,13},{14,15},{16,17},{18,... | collective-permute-start | bytes 319496 | tf_op jit(solution)/shard_map/ppermute | solution.py:31
  371.2 6.9 %collective-permute-start.7 = (bf16[1,13,256,16]{2,3,1,0:T(8,128)(2,1)}, bf16[1,13,256,16]{2,3,1,0:T(8,128)(2,1)}, u32[]{:S(2)}, u32[]{:S(2)}) collective-permute-start(bf16[1,13,256,16]{2,3,1,0:T(8,128)(2,1)} %copy.48), channel_id=1, source_target_pairs={{1,0},{3,2},{5,4},{7,6},{9,8},{11,10},{13,12},{15,14},{17,16},{19,... | collective-permute-start | bytes 319496 | tf_op jit(solution)/shard_map/ppermute | solution.py:32
  380.8 1.3 copy-start.6
  385.4 0.9 copy-start.11
  386.3 4.3 %copy-start.1 = (bf16[1280,1280]{1,0:T(8,128)(2,1)S(1)}, bf16[1280,1280]{1,0:T(8,128)(2,1)}, u32[]{:S(2)}) copy-start(bf16[1280,1280]{1,0:T(8,128)(2,1)} %param.23) | copy-start | bytes 9830404
where the time goes:
time: 397 us; the launch traced here: 391 us
  matrix products  126 us (32%)
  local copies, waits for them, and re-layouts  118 us (30%)
  waiting for transfers between devices  54.4 us (14%)
  starting transfers between devices  47.3 us (12%)
  other arithmetic  42.3 us (11%)
    reshape x2, local copies, waits for them, and re-layouts, decode_tile(): upsampled.reshape(PATCHES, PATCHES, FEAT, PATCH, PATCH)  41.3 us
    ppermute x6, waiting for transfers between devices, with_halo(): before = lax.ppermute(last, axis, up)  38 us
    sub x2, matrix products, encode_tile(): lifted = jnp.exp(scores - highest)  35.6 us
    ppermute x6, starting transfers between devices, with_halo(): before = lax.ppermute(last, axis, up)  31.9 us
    dot_general x9, matrix products, classify(): jnp.einsum('kf,bfhw->bkhw', class_weight[offset], window, preferred_eleme...  30.9 us
    dot_general x2, matrix products, encode_tile(): jnp.einsum('hqk,hkd->hqd', attention, value_rows, preferred_element_type=...  30.5 us
    broadcast_in_dim x2, local copies, waits for them, and re-layouts, local(): features = lax.map(per_tile, (tile_tokens, locations))  21.9 us
    another operation x1, local copies, waits for them, and re-layouts  19.1 us
  transfers between devices with their start and end apart: 13, of which 6 were waited for; matrix products, arithmetic and copies ran while one was open for 9% of the time, Pallas kernels for 0%

commit v1 on v0

v1 whole, which is shorter than its diff:
```python
import functools
import math

import jax
import jax.numpy as jnp
import numpy as np
from jax import lax
from jax.experimental import pallas as pl
from jax.experimental.pallas import tpu as pltpu
from jax.sharding import PartitionSpec as P

HEADS = 16
DATES = 4
PATCH = 14
INTERSECTION = 32
FEAT = 16
PATCHES = 16
RIM = 16
TILE_PX = PATCH * PATCHES
STRIDE = TILE_PX - INTERSECTION
SPAN = PATCH + 2
FAR_PATCH, FAR_PIXEL = divmod(STRIDE - 1, PATCH)
NEAR_PATCH, NEAR_PIXEL = divmod(INTERSECTION, PATCH)
LANES = 256
VMEM = 56 * 2**20

norm_eps = 1e-06
bf16 = jnp.bfloat16
f32 = jnp.float32

NN = (((1,), (0,)), ((), ()))
NT = (((1,), (1,)), ((), ()))
TN = (((0,), (0,)), ((), ()))


def mm(left, right, dims=NN):
    return lax.dot_general(left, right, dims, preferred_element_type=f32)


def layer_norm(values, gain_row):
    average = jnp.mean(values, axis=-1, keepdims=True)
    centered = values - average
    spread = jnp.mean(centered * centered, axis=-1, keepdims=True)
    return centered * lax.rsqrt(spread + norm_eps) * gain_row


def qkv_kernel(query_blocks, scale, x_ref, loc_ref, gain_ref, w_ref, o_ref, normed_ref):
    step = pl.program_id(0)
    rows = min(128, x_ref.shape[0])

    @pl.when(step == 0)
    def _():
        def body(t, carry):
            s = pl.ds(pl.multiple_of(t * rows, rows), rows)
            residual = x_ref[s, :].astype(f32) + loc_ref[...]
            normed_ref[s, :] = layer_norm(residual, gain_ref[...].astype(f32)).astype(bf16)
            return carry

        lax.fori_loop(0, x_ref.shape[0] // rows, body, 0)

    packed = mm(w_ref[...], normed_ref[...], NT)
    o_ref[...] = (packed * jnp.where(step < query_blocks, scale, 1.0)).astype(bf16)


def project(x, location, gain, w_t):
    tokens, width = x.shape
    block = width // 2
    scale = math.log2(math.e) / math.sqrt(width // HEADS)
    return pl.pallas_call(
        functools.partial(qkv_kernel, width // block, scale),
        grid=(w_t.shape[0] // block,),
        in_specs=[
            pl.BlockSpec((tokens, width), lambda i: (0, 0)),
            pl.BlockSpec((1, width), lambda i: (0, 0)),
            pl.BlockSpec((1, width), lambda i: (0, 0)),
            pl.BlockSpec((block, width), lambda i: (i, 0)),
        ],
        out_specs=pl.BlockSpec((block, tokens), lambda i: (i, 0)),
        out_shape=jax.ShapeDtypeStruct((w_t.shape[0], tokens), bf16),
        scratch_shapes=[pltpu.VMEM((tokens, width), bf16)],
        compiler_params=pltpu.CompilerParams(vmem_limit_bytes=VMEM),
        name="project",
    )(x, location, gain, w_t)


def attention_kernel(block, q_ref, k_ref, v_ref, o_ref):
    head_width, tokens = q_ref.shape
    keys = k_ref[...]
    values = jnp.concatenate([v_ref[...], jnp.ones((16, tokens), bf16)], axis=0)
    for first in range(0, tokens, block):
        scores = mm(keys, q_ref[:, first : first + block], TN)
        highest = jnp.max(scores, axis=0, keepdims=True)
        lifted = jnp.exp2(scores - highest).astype(bf16)
        mixed = mm(values, lifted)
        o_ref[:, first : first + block] = (
            mixed[:head_width] * (1.0 / mixed[head_width : head_width + 1])
        ).astype(bf16)


def attend(packed):
    width, tokens = packed.shape[0] // 3, packed.shape[1]
    head = width // HEADS
    return pl.pallas_call(
        functools.partial(attention_kernel, min(512, tokens)),
        grid=(HEADS,),
        in_specs=[
            pl.BlockSpec((head, tokens), lambda h: (h, 0)),
            pl.BlockSpec((head, tokens), lambda h: (h + HEADS, 0)),
            pl.BlockSpec((head, tokens), lambda h: (h + 2 * HEADS, 0)),
        ],
        out_specs=pl.BlockSpec((head, tokens), lambda h: (h, 0)),
        out_shape=jax.ShapeDtypeStruct((width, tokens), bf16),
        compiler_params=pltpu.CompilerParams(vmem_limit_bytes=VMEM),
        name="attend",
    )(packed, packed, packed)


def reduce_kernel(m_ref, w_ref, x_ref, loc_ref, gain_ref, wr_ref, bias_ref, o_ref, sum_ref):
    date = pl.program_id(0)
    updated = x_ref[...].astype(f32) + loc_ref[...] + mm(m_ref[...], w_ref[...], TN)
    encoded = layer_norm(updated, gain_ref[...].astype(f32)).astype(bf16)
    part = mm(encoded, wr_ref[...])

    @pl.when(date == 0)
    def _():
        sum_ref[...] = part

    @pl.when(date > 0)
    def _():
        sum_ref[...] += part

    @pl.when(date == pl.num_programs(0) - 1)
    def _():
        v = sum_ref[...] + bias_ref[...].astype(f32)
        o_ref[...] = (0.5 * v * (1.0 + lax.erf(v * math.sqrt(0.5)))).astype(bf16)


def reduce_dates(mixed, out_weight, x, location, gain, reduce_weight, reduce_bias):
    width, tokens = mixed.shape
    patches = tokens // DATES
    dec = reduce_weight.shape[1]
    return pl.pallas_call(
        reduce_kernel,
        grid=(DATES,),
        in_specs=[
            pl.BlockSpec((width, patches), lambda t: (0, t)),
            pl.BlockSpec((width, width), lambda t: (0, 0)),
            pl.BlockSpec((patches, width), lambda t: (t, 0)),
            pl.BlockSpec((1, width), lambda t: (0, 0)),
            pl.BlockSpec((1, width), lambda t: (0, 0)),
            pl.BlockSpec((width, dec), lambda t: (t, 0)),
            pl.BlockSpec((1, dec), lambda t: (0, 0)),
        ],
        out_specs=pl.BlockSpec((patches, dec), lambda t: (0, 0)),
        out_shape=jax.ShapeDtypeStruct((patches, dec), bf16),
        scratch_shapes=[pltpu.VMEM((patches, dec), f32)],
        compiler_params=pltpu.CompilerParams(vmem_limit_bytes=VMEM),
        name="reduce_dates",
    )(mixed, out_weight, x, location, gain, reduce_weight, reduce_bias)


FIRST_OWN = RIM // PATCH
LAST_OWN = PATCHES - 1 - FIRST_OWN
UPPER = [a for a in range(PATCHES) if PATCH * a + PATCH >= TILE_PX - RIM]
LOWER = [a for a in range(PATCHES) if PATCH * a - 1 < RIM]
ENTRIES = (
    [(0, a) for a in UPPER]
    + [(0, None)]
    + [(1, a) for a in range(FIRST_OWN, LAST_OWN + 1)]
    + [(2, a) for a in LOWER]
    + [(2, None)]
)
SIDE = 16


def decoder_kernels(upsample_weight, class_weight):
    channels = upsample_weight.shape[0]
    classes = class_weight.shape[1]
    taps = class_weight.reshape(3, 3, classes, FEAT)
    reach = np.zeros((3, PATCH, SPAN), np.float32)
    for dy in range(3):
        for i in range(PATCH):
            reach[dy, i, i + 2 - dy] = 1.0
    main = jnp.einsum("yxkf,yiI->xfikI", taps, jnp.asarray(reach, bf16), preferred_element_type=f32)
    main = main.reshape(3, FEAT, PATCH, classes * SPAN)
    far = np.arange(PATCH)[None, None, :, None] == FAR_PIXEL
    near = np.arange(PATCH)[None, None, :, None] == NEAR_PIXEL
    above = jnp.where(far, taps[0].transpose(0, 2, 1)[:, :, None, :], 0).astype(f32)
    below = jnp.where(near, taps[2].transpose(0, 2, 1)[:, :, None, :], 0).astype(f32)
    spare = jnp.zeros((3, FEAT, PATCH, LANES - classes * (SPAN + 2)), f32)
    spread = jnp.concatenate([main, above, below, spare], axis=-1).astype(bf16)
    spread = spread.reshape(3, FEAT * PATCH, LANES)
    columns = upsample_weight.reshape(channels, FEAT * PATCH, PATCH).transpose(2, 0, 1)
    columns = jnp.pad(columns, ((2, 2), (0, 0), (0, 0)))

    def kernel(first_ref, second_ref, third_ref, spread_ref, o_ref):
        total = mm(first_ref[0], spread_ref[0])
        total += mm(second_ref[0], spread_ref[1])
        total += mm(third_ref[0], spread_ref[2])
        o_ref[0] = total.astype(bf16)

    block = (1, channels, FEAT * PATCH)
    kernels = pl.pallas_call(
        kernel,
        grid=(SPAN,),
        in_specs=[
            pl.BlockSpec(block, lambda j: (j, 0, 0)),
            pl.BlockSpec(block, lambda j: (j + 1, 0, 0)),
            pl.BlockSpec(block, lambda j: (j + 2, 0, 0)),
            pl.BlockSpec((3, FEAT * PATCH, LANES), lambda j: (0, 0, 0)),
        ],
        out_specs=pl.BlockSpec((1, channels, LANES), lambda j: (j, 0, 0)),
        out_shape=jax.ShapeDtypeStruct((SPAN, channels, LANES), bf16),
        name="decoder_kernels",
    )(columns, columns, columns, spread)
    near_column = mm(columns[NEAR_PIXEL + 2], spread[2]).astype(bf16)
    far_column = mm(columns[FAR_PIXEL + 2], spread[0]).astype(bf16)
    return kernels, jnp.stack([near_column, far_column])


def neighbour_profiles(blend_weights, tile_valid):
    profiles = blend_weights.reshape(2, TILE_PX).astype(bf16)
    valid = tile_valid.reshape(1).astype(bf16)
    own = jnp.concatenate([profiles[:1] * valid, profiles[1:]], axis=0)
    before, after = neighbours((own, own), "col", lax.axis_size("col"))
    wide = jnp.stack([before, own, after])
    rows = lax.axis_size("date") * lax.axis_size("tile")
    above, below = neighbours((wide, wide), ("date", "tile"), rows)
    return jnp.stack([above, wide, below])


def rim_profile(profiles, position):
    blank = jnp.zeros(profiles.shape[:-1] + (STRIDE - RIM,), profiles.dtype)
    if position == 0:
        return jnp.concatenate([profiles[..., TILE_PX - RIM :], blank], axis=-1)
    if position == 2:
        return jnp.concatenate([blank, profiles[..., :RIM]], axis=-1)
    return profiles[..., RIM : RIM + STRIDE]


def placement():
    main = np.zeros((3, SPAN, PATCHES, STRIDE), np.float32)
    side = np.zeros((3, SIDE, STRIDE), np.float32)
    for j in range(SPAN):
        for slot in range(PATCHES):
            if slot == 0:
                which, x = 0, PATCH * (PATCHES - 1) + j - 1
            elif slot == PATCHES - 1:
                which, x = 2, j - 1
            else:
                which, x = 1, PATCH * slot + j - 1
            column = x + (0, 1, 2)[which] * STRIDE - STRIDE - RIM
            if 0 <= x < TILE_PX and 0 <= column < STRIDE:
                main[which, j, slot, column] = 1.0
    rows = []
    for j in range(SPAN):
        x = PATCH * (PATCHES - 2) + j - 1
        if TILE_PX - RIM <= x < TILE_PX:
            side[0, len(rows), x - (TILE_PX - RIM)] = 1.0
            rows.append((0, j))
    for j in range(SPAN):
        x = PATCH + j - 1
        if 0 <= x < RIM:
            side[2, len(rows), STRIDE - RIM + x] = 1.0
            rows.append((2, j))
    side[0, len(rows), RIM - 1] = 1.0
    side[2, len(rows) + 1, STRIDE - RIM] = 1.0
    return main.reshape(3, SPAN * PATCHES, STRIDE), side, rows


PLACE_MAIN, PLACE_SIDE, SIDE_ROWS = placement()


def entry_weights(row_profiles, classes):
    padded = jnp.pad(row_profiles, ((0, 0), (0, 0), (1, 1)))
    lines = []
    for tile_row, a in ENTRIES:
        if a is None:
            lines.append(jnp.zeros((3, SPAN), f32))
        else:
            lines.append(padded[tile_row, :, PATCH * a : PATCH * a + SPAN])
    lines = jnp.stack(lines)
    main = jnp.broadcast_to(lines[:, :, None, :], (len(ENTRIES), 3, classes, SPAN))
    main = main.reshape(len(ENTRIES), 3, classes * SPAN)
    halo = []
    for tile_row, a in ENTRIES:
        above = row_profiles[tile_row, :, :1] if a is None and tile_row == 2 else jnp.zeros((3, 1), f32)
        below = row_profiles[tile_row, :, -1:] if a is None and tile_row == 0 else jnp.zeros((3, 1), f32)
        halo.append(
            jnp.concatenate(
                [
                    jnp.broadcast_to(above, (3, classes)),
                    jnp.broadcast_to(below, (3, classes)),
                    jnp.zeros((3, LANES - classes * (SPAN + 2)), f32),
                ],
                axis=-1,
            )
        )
    return jnp.concatenate([main, jnp.stack(halo)], axis=-1)


def blend_tables(profiles, classes):
    row_profiles, col_profiles = profiles[:, :, 0], profiles[:, :, 1]
    weights = entry_weights(row_profiles, classes)
    before, own, after = (weights[:, i : i + 1].astype(bf16) for i in range(3))
    count = len(ENTRIES)
    main = jnp.concatenate([before, jnp.broadcast_to(own, (count, PATCHES - 2, LANES)), after], axis=1)
    side_parts = [before if which == 0 else after for which, _ in SIDE_ROWS] + [before, after]
    side_parts.append(jnp.zeros((count, SIDE - len(side_parts), LANES), bf16))
    side = jnp.concatenate(side_parts, axis=1)
    columns = jnp.stack([rim_profile(col_profiles[:, i], i) for i in range(3)], axis=1)
    rows = jnp.stack([rim_profile(row_profiles[i], i) for i in range(3)], axis=0)
    spots = sum(PLACE_MAIN[i][None] * columns[:, i, None, :] for i in range(3)).astype(bf16)
    side_spots = sum(PLACE_SIDE[i][None] * columns[:, i, None, :] for i in range(3)).astype(bf16)
    total = 0.0
    for i in range(3):
        for j in range(3):
            total = total + rows[i, j, :, None] * columns[i, j, None, :]
    return main.reshape(-1, LANES), side.reshape(-1, LANES), spots, side_spots, total


def compose_kernel(
    classes, a_ref, b_ref, rwa_ref, rwb_ref, m_ref, edge_ref, e_ref, e2_ref, den_ref, bias_ref, o_ref, z_ref, z2_ref, acc_ref
):
    count = len(ENTRIES)

    def column(j, carry):
        z = mm(a_ref[...], m_ref[j]) * rwa_ref[...].astype(f32)
        z_ref[:, j] = z.astype(bf16).reshape(count, PATCHES, LANES)
        return carry

    lax.fori_loop(0, SPAN, column, 0)
    slot = lax.broadcasted_iota(jnp.int32, b_ref.shape, 0) % SIDE
    b = b_ref[...].astype(f32)
    total = None
    for i in range(len(SIDE_ROWS) + 2):
        weights = m_ref[SIDE_ROWS[i][1]] if i < len(SIDE_ROWS) else edge_ref[i - len(SIDE_ROWS)]
        part = mm(jnp.where(slot == i, b, 0.0).astype(bf16), weights)
        total = part if total is None else total + part
    z2_ref[...] = (total * rwb_ref[...].astype(f32)).astype(bf16).reshape(count, SIDE, LANES)
    acc_ref[...] = jnp.zeros_like(acc_ref)
    for n, (tile_row, a) in enumerate(ENTRIES):
        part = mm(z_ref[n].reshape(SPAN * PATCHES, LANES), e_ref[tile_row], TN)
        part += mm(z2_ref[n], e2_ref[tile_row], TN)
        if a is None:
            first = classes * SPAN + (classes if tile_row == 0 else 0)
            y = 2 * RIM - 1 if tile_row == 0 else STRIDE
            for k in range(classes):
                acc_ref[k, y : y + 1, :] += part[first + k : first + k + 1]
            continue
        y = PATCH * a - 1 + (tile_row - 1) * STRIDE
        low, high = 0, SPAN
        if tile_row == 0:
            high = min(SPAN, TILE_PX - (PATCH * a - 1))
        if tile_row == 2:
            low = max(0, 1 - PATCH * a)
        for k in range(classes):
            acc_ref[k, y + low : y + high, :] += part[k * SPAN + low : k * SPAN + high]
    den = den_ref[...]
    inverse = 1.0 / jnp.maximum(den, 1.0)
    for k in range(classes):
        o_ref[k] = (acc_ref[k, RIM : RIM + STRIDE, :] + bias_ref[k] * den) * inverse


def neighbours(value, axis, size):
    forward = [(i, i + 1) for i in range(size - 1)]
    backward = [(i + 1, i) for i in range(size - 1)]
    return lax.ppermute(value[0], axis, forward), lax.ppermute(value[1], axis, backward)


def compose(reduced, kernels, edges, tables, class_bias, classes):
    channels = reduced.shape[1]
    own = reduced.reshape(PATCHES, PATCHES, channels)
    edge = len(UPPER)
    before, after = neighbours((own[:, -2:], own[:, :2]), "col", lax.axis_size("col"))
    wide = jnp.concatenate([own, before, after], axis=1)
    rows = lax.axis_size("date") * lax.axis_size("tile")
    above, below = neighbours((wide[-edge:], wide[: len(LOWER)]), ("date", "tile"), rows)
    lines = jnp.concatenate(
        [
            above,
            wide[NEAR_PATCH : NEAR_PATCH + 1],
            wide[FIRST_OWN : LAST_OWN + 1],
            below,
            wide[FAR_PATCH : FAR_PATCH + 1],
        ],
        axis=0,
    )
    count = len(ENTRIES)
    main = jnp.concatenate([lines[:, PATCHES + 1 : PATCHES + 2], lines[:, 1 : PATCHES - 1], lines[:, PATCHES + 2 : PATCHES + 3]], axis=1)
    parts = [lines[:, PATCHES : PATCHES + 1] if which == 0 else lines[:, PATCHES + 3 : PATCHES + 4] for which, _ in SIDE_ROWS]
    parts += [lines[:, NEAR_PATCH : NEAR_PATCH + 1], lines[:, FAR_PATCH : FAR_PATCH + 1]]
    parts.append(jnp.zeros((count, SIDE - len(parts), channels), bf16))
    side = jnp.concatenate(parts, axis=1)
    main_weights, side_weights, spots, side_spots, total = tables
    whole = pl.BlockSpec(memory_space=pltpu.VMEM)
    return pl.pallas_call(
        functools.partial(compose_kernel, classes),
        in_specs=[whole] * 9 + [pl.BlockSpec(memory_space=pltpu.SMEM)],
        out_specs=whole,
        out_shape=jax.ShapeDtypeStruct((classes, STRIDE, STRIDE), f32),
        scratch_shapes=[
            pltpu.VMEM((count, SPAN, PATCHES, LANES), bf16),
            pltpu.VMEM((count, SIDE, LANES), bf16),
            pltpu.VMEM((classes, TILE_PX, STRIDE), f32),
        ],
        compiler_params=pltpu.CompilerParams(vmem_limit_bytes=VMEM),
        name="compose",
    )(
        main.reshape(-1, channels),
        side.reshape(-1, channels),
        main_weights,
        side_weights,
        kernels,
        edges,
        spots,
        side_spots,
        total,
        class_bias.astype(f32),
    )


def local(
    arrivals,
    owner_map,
    block_ids,
    tile_valid,
    blend_weights,
    location_table,
    norm_gain,
    qkv_weight,
    out_weight,
    final_gain,
    reduce_weight,
    reduce_bias,
    upsample_weight,
    class_weight,
    class_bias,
):
    width = arrivals.shape[-1]
    classes = class_weight.shape[1]
    profiles = neighbour_profiles(blend_weights, tile_valid).astype(f32)
    order = jnp.argsort(owner_map[0])
    ordered = jnp.take(arrivals[0], order, axis=0, mode="clip")
    strip = ordered.shape[3] * ordered.shape[4]
    ordered = ordered.reshape(ordered.shape[0], strip, width)
    ordered, profiles, qkv_weight, upsample_weight, class_weight = lax.optimization_barrier(
        (ordered, profiles, qkv_weight, upsample_weight, class_weight)
    )
    x = lax.all_to_all(ordered, ("date", "tile"), split_axis=0, concat_axis=0, tiled=True)
    codes = block_ids.reshape(1, 1)
    one_hot = (codes == jnp.arange(location_table.shape[0], dtype=jnp.int32)[None, :]).astype(bf16)
    location = jnp.dot(one_hot, location_table, preferred_element_type=f32)

    qkv_t = qkv_weight.T
    kernels, edges = decoder_kernels(upsample_weight, class_weight)
    tables = blend_tables(profiles, classes)
    x, location, qkv_t, kernels, edges, tables = lax.optimization_barrier((x, location, qkv_t, kernels, edges, tables))
    x = x.reshape(-1, width)

    packed = project(x, location, norm_gain[None], qkv_t)
    mixed = attend(packed)
    reduced = reduce_dates(mixed, out_weight, x, location, final_gain[None], reduce_weight, reduce_bias[None])
    return compose(reduced, kernels, edges, tables, class_bias, classes)[None]


def solution(mesh):
    placed = (
        P(None, None, "col", "date", "tile", None, None),
        P(),
        P(None, ("date", "tile"), "col"),
        P(None, ("date", "tile"), "col"),
        P(None, ("date", "tile"), "col", None, None),
    ) + (P(),) * 10
    return jax.shard_map(
        local,
        mesh=mesh,
        in_specs=placed,
        out_specs=P(None, None, ("date", "tile"), "col"),
        check_vma=False,
    )
```

time: 397 us -> 202 us (0.51)
  matrix products: 126 us -> 4.52 us
  Pallas kernels: 0 us -> 83.8 us
  local copies, waits for them, and re-layouts: 118 us -> 54.8 us
  waiting for transfers between devices: 54.4 us -> 10.8 us
  other arithmetic: 42.3 us -> 13.8 us
  starting transfers between devices: 47.3 us -> 28.4 us
    pallas_call x0 -> x5, Pallas kernels: none -> 83.8 us  [the longest x1 33.2 us: attend(): pl.pallas_call(functools.partial(attention_kernel, min(512, tokens)), gri...]
    dot_general x14 -> x4, matrix products: 74.3 us -> 4.52 us  [the longest x2 2.17 us: mm(): return lax.dot_general(left, right, dims, preferred_element_type=f32)]
    ppermute x12 -> x8, waiting for transfers between devices: 48.4 us -> 7.72 us  [the longest x4 6.44 us: neighbours(): lax.ppermute(value[1], axis, backward)]
    sub x2 -> x0, matrix products: 35.6 us -> none  [encode_tile(): lifted = jnp.exp(scores - highest)]
    reshape x2 -> x4, local copies, waits for them, and re-layouts: 41.3 us -> 11.8 us  [the longest x2 7.8 us: decoder_kernels(): upsample_weight.reshape(channels, FEAT * PATCH, PATCH).transpose(2, 0, 1)]
    ppermute x12 -> x8, starting transfers between devices: 39.8 us -> 20.4 us  [the longest x4 15 us: neighbours(): lax.ppermute(value[0], axis, forward)]
    unnamed x1 -> x0, matrix products: 16.5 us -> none
    another operation x1 -> x15, local copies, waits for them, and re-layouts: 19.1 us -> 2.88 us
  transfers between devices with their start and end apart: 13 -> 9, of which waited for: 6 -> 4; matrix products, arithmetic and copies ran while one was open for 9% -> 29% of each run, Pallas kernels for 0% -> 6%
where the time goes in v1:
time: 202 us; the launch traced here: 198 us
  Pallas kernels  83.8 us (41%)
  local copies, waits for them, and re-layouts  54.8 us (27%)
  starting transfers between devices  28.4 us (14%)
  other arithmetic  13.8 us (7%)
  waiting for transfers between devices  10.8 us (5%)
  matrix products  4.52 us (2%)
    pallas_call x1, Pallas kernels, attend(): pl.pallas_call(functools.partial(attention_kernel, min(512, tokens)), gri...  33.2 us
    pallas_call x1, Pallas kernels, project(): pl.pallas_call(functools.partial(qkv_kernel, width // block, scale), grid...  16.9 us
    ppermute x4, starting transfers between devices, neighbours(): lax.ppermute(value[0], axis, forward)  15 us
    optimization_barrier x1, local copies, waits for them, and re-layouts, local(): lax.optimization_barrier((ordered, profiles, qkv_weight, upsample_weight,...  13.7 us
    pallas_call x1, Pallas kernels, decoder_kernels(): pl.pallas_call(kernel, grid=(SPAN,), in_specs=[pl.BlockSpec(block, lambda...  12.4 us
    pallas_call x1, Pallas kernels, reduce_dates(): pl.pallas_call(reduce_kernel, grid=(DATES,), in_specs=[pl.BlockSpec((widt...  11.2 us
    pallas_call x1, Pallas kernels, compose(): pl.pallas_call(functools.partial(compose_kernel, classes), in_specs=[whol...  10.1 us
    all_to_all x1, starting transfers between devices, local(): lax.all_to_all(ordered, ('date', 'tile'), split_axis=0, concat_axis=0, ti...  7.99 us
  transfers between devices with their start and end apart: 9, of which 4 were waited for; matrix products, arithmetic and copies ran while one was open for 29% of the time, Pallas kernels for 6%

profile of v1, /device:TPU:0, one launch (start us, length us, event | category | flops | bytes accessed | tf_op | source)
XLA Modules:
  0.0 198.1 jit_solution(17332919915627369566)
XLA Ops:
  1.5 4.9 %collective-permute-start = (bf16[2,224]{1,0:T(2,128)(2,1)S(1)}, bf16[2,224]{1,0:T(2,128)(2,1)S(1)}, u32[]{:S(2)}, u32[]{:S(2)}) collective-permute-start(bf16[2,224]{1,0:T(2,128)(2,1)S(1)} %pad_maximum_fusion.7), channel_id=1, source_target_pairs={{0,1},{2,3},{4,5},{6,7},{8,9},{10,11},{12,13},{14,15},{16,17},{18,... | collective-permute-start | bytes 2696 | tf_op jit(solution)/shard_map/ppermute | solution.py:368
  6.4 1.3 collective-permute-start.1
  7.7 1.9 sort.17
  10.5 1.5 fusion.3.loc_ref
  13.6 1.3 broadcast_in_dim.131.gain_ref
  14.9 1.3 broadcast_in_dim.132.gain_ref
  16.2 1.2 broadcast_in_dim.133.bias_ref
  17.4 2.2 %gather_fusion = bf16[16,4,16,1280]{3,2,1,0:T(8,128)(2,1)} fusion(bf16[16,4,16,1280]{3,2,1,0:T(8,128)(2,1)S(1)} %bitcast.110, s32[1024]{0:T(1024)S(1)} %pad_clamp_fusion), kind=kCustom, calls=%fused_computation | custom fusion | bytes 5242944 | tf_op jit(solution)/shard_map/jit(_take)/gather | solution.py:444
  19.6 1.3 collective-permute-start.3
  20.9 4.5 %collective-permute-start.2 = (bf16[3,2,224]{2,1,0:T(2,128)(2,1)S(1)}, bf16[3,2,224]{2,1,0:T(2,128)(2,1)S(1)}, u32[]{:S(2)}, u32[]{:S(2)}) collective-permute-start(bf16[3,2,224]{2,1,0:T(2,128)(2,1)S(1)} %pad_maximum_fusion.6), channel_id=1, source_target_pairs={{0,2},{2,4},{4,6},{6,8},{8,10},{10,12},{12,14},{14,16},{16,18},{18... | collective-permute-start | bytes 8072 | tf_op jit(solution)/shard_map/ppermute | solution.py:368
  25.5 1.3 collective-permute-done.2
  27.1 0.9 convert_bitcast_fusion
  28.0 2.5 %copy.72 = bf16[3,16,14,13,16]{4,3,1,2,0:T(8,128)(2,1)} copy(bf16[3,16,14,13,16]{4,1,2,3,0:T(8,128)(2,1)S(1)} %convert_bitcast_fusion) | data formatting | bytes 559104 | tf_op jit(solution)/shard_map/convert.12
  30.5 2.5 %copy.91 = bf16[3,16,14,13,16]{4,3,2,1,0:T(8,128)(2,1)} copy(bf16[3,16,14,13,16]{4,1,2,3,0:T(8,128)(2,1)S(1)} %convert_bitcast_fusion) | data formatting | bytes 559104 | tf_op jit(solution)/shard_map/concatenate | solution.py:191
  34.6 8.0 %all-to-all-start = ((bf16[16,64,1280]{2,1,0:T(8,128)(2,1)}), bf16[16,64,1280]{2,1,0:T(8,128)(2,1)S(1)}, u32[]{:S(2)}, u32[]{:S(2)}) async-start(bf16[16,64,1280]{2,1,0:T(8,128)(2,1)} %bitcast.114), calls=%async_computation | async-start | bytes 5242880 | tf_op jit(solution)/shard_map/all_to_all | solution.py:450
  43.5 3.8 %reshape.118 = bf16[3,16,14,208]{3,1,2,0:T(8,128)(2,1)S(1)} reshape(bf16[3,16,14,13,16]{4,3,1,2,0:T(8,128)(2,1)} %copy.72) | data formatting | bytes 559104 | tf_op jit(solution)/shard_map/reshape | solution.py:185
  47.8 3.6 %reshape.116 = bf16[256,224,14]{0,2,1:T(8,128)(2,1)} reshape(bf16[256,3136]{0,1:T(8,128)(2,1)} %param.36) | data formatting | bytes 3211264 | tf_op jit(solution)/shard_map/reshape | solution.py:193
  51.4 4.2 %copy.62 = bf16[256,224,14]{1,0,2:T(8,128)(2,1)} copy(bf16[256,224,14]{0,2,1:T(8,128)(2,1)} %reshape.116) | data formatting | bytes 3211264 | tf_op jit(solution)/shard_map/reshape | solution.py:193
  56.5 3.8 %reshape.148 = bf16[3,224,208]{2,1,0:T(8,128)(2,1)S(1)} reshape(bf16[3,16,14,13,16]{4,3,2,1,0:T(8,128)(2,1)} %copy.91) | data formatting | bytes 559104 | tf_op jit(solution)/shard_map/concatenate | solution.py:191
  60.3 3.3 %pad.12.first_ref.second_ref.third_ref = bf16[18,256,224]{2,1,0:T(8,128)(2,1)} pad(bf16[14,256,224]{2,1,0:T(8,128)(2,1)} %bitcast.115, bf16[]{:T(256)} %constant.12.clone.1), padding=2_2x0_0x0_0 | pad | bytes 3670018 | tf_op jit(solution)/shard_map/jit(_pad)/pad | solution.py:194
  63.7 13.7 %copy.61 = bf16[1280,3840]{0,1:T(8,128)(2,1)} copy(bf16[1280,3840]{1,0:T(8,128)(2,1)} %param.31) | data formatting | bytes 19660800 | tf_op jit(solution)/shard_map/optimization_barrier | solution.py:447
  77.6 0.9 maximum_maximum_fusion.spread_ref
  78.5 12.4 %decoder_kernels.1.m_ref = bf16[16,256,256]{2,1,0:T(8,128)(2,1)} custom-call(bf16[18,256,224]{2,1,0:T(8,128)(2,1)} %pad.12.first_ref.second_ref.third_ref, bf16[18,256,224]{2,1,0:T(8,128)(2,1)} %pad.12.first_ref.second_ref.third_ref, bf16[18,256,224]{2,1,0:T(8,128)(2,1)} %pad.12.first_ref.second_ref.third_ref, ...), custom_call_target="tpu_custom_call" | custom-call | tf_op jit(solution)/shard_map/decoder_kernels/pallas_call | solution.py:203
  90.9 1.5 concatenate.60
  92.6 0.8 pad_maximum_fusion.2
  93.4 1.1 fusion
  94.5 1.1 fusion.1
  95.5 0.7 pad_maximum_fusion.edge_ref
  97.1 1.0 multiply_add_fusion.den_ref
  98.1 2.0 %add_convert_fusion.e_ref = bf16[3,256,192]{2,1,0:T(8,128)(2,1)} fusion(f32[3,192]{1,0:T(4,128)S(1)} %concatenate.62, f32[256,192]{1,0:T(8,128)} %constant.61, f32[3,192]{1,0:T(4,128)S(1)} %get-tuple-element.77, f32[256,192]{1,0:T(8,128)} %constant.60, f32[3,192]{1,0:T(4,128)S(1)} %concatenate.61, f32[256,192]{1,0:T(8,128)} %constant.59), kind=kLoop, calls=%fused_computation.6 | loop fusion | flops 884736 | bytes 891648 | tf_op jit(solution)/shard_map/convert_element_type | solution.py:313
  100.1 3.1 %all-to-all-done = bf16[16,64,1280]{2,1,0:T(8,128)(2,1)S(1)} async-done(((bf16[16,64,1280]{2,1,0:T(8,128)(2,1)}), bf16[16,64,1280]{2,1,0:T(8,128)(2,1)S(1)}, u32[]{:S(2)}, u32[]{:S(2)}) %all-to-all-start) | async-done | bytes 2621472 | tf_op jit(solution)/shard_map/all_to_all | solution.py:450
  103.3 1.5 copy-done.2
  104.7 16.9 %project.1.q_ref.k_ref.v_ref = bf16[3840,1024]{1,0:T(8,128)(2,1)} custom-call(bf16[1024,1280]{1,0:T(8,128)(2,1)} %bitcast.112, f32[1,1280]{1,0:T(1,128)} %fusion.3.loc_ref, bf16[1,1280]{1,0:T(2,128)(2,1)} %broadcast_in_dim.131.gain_ref, bf16[3840,1280]{1,0:T(8,128)(2,1)} %bitcast.111), custom_call_target="tpu_custom_call" | custom-call | tf_op jit(solution)/shard_map/project/pallas_call | solution.py:69
  121.7 33.2 %attend.1.m_ref = bf16[1280,1024]{1,0:T(8,128)(2,1)} custom-call(bf16[3840,1024]{1,0:T(8,128)(2,1)} %project.1.q_ref.k_ref.v_ref, bf16[3840,1024]{1,0:T(8,128)(2,1)} %project.1.q_ref.k_ref.v_ref, bf16[3840,1024]{1,0:T(8,128)(2,1)} %project.1.q_ref.k_ref.v_ref), custom_call_target="tpu_custom_call" | custom-call | tf_op jit(solution)/shard_map/attend/pallas_call | solution.py:103
  154.9 11.2 %reduce_dates.1 = bf16[256,256]{1,0:T(8,128)(2,1)} custom-call(bf16[1280,1024]{1,0:T(8,128)(2,1)} %attend.1.m_ref, bf16[1280,1280]{1,0:T(8,128)(2,1)} %w_ref.1, bf16[1024,1280]{1,0:T(8,128)(2,1)} %bitcast.113, f32[1,1280]{1,0:T(1,128)} %fusion.3.loc_ref, bf16[1,1280]{1,0:T(2,128)(2,1)} %broadcast_in_dim.132.gain_ref, bf16[5120,256]{1,0:T(8,128)(2,1)} %wr_ref.1, ...), custom_call_target="tpu_custom_call" | custom-call | tf_op jit(solution)/shard_map/reduce_dates/pallas_call | solution.py:142
  166.1 0.9 fusion.11
  167.0 4.3 %collective-permute-start.4 = (bf16[16,2,256]{2,1,0:T(2,128)(2,1)S(1)}, bf16[16,2,256]{2,1,0:T(2,128)(2,1)S(1)}, u32[]{:S(2)}, u32[]{:S(2)}) collective-permute-start(bf16[16,2,256]{2,1,0:T(2,128)(2,1)S(1)} %get-tuple-element.49), channel_id=1, source_target_pairs={{0,1},{2,3},{4,5},{6,7},{8,9},{10,11},{12,13},{14,15},{16,17},{18,... | collective-permute-start | bytes 49160 | tf_op jit(solution)/shard_map/ppermute | solution.py:368
  171.3 1.3 collective-permute-start.5
  173.2 3.7 %collective-permute-done.5 = bf16[16,2,256]{2,1,0:T(2,128)(2,1)S(1)} collective-permute-done((bf16[16,2,256]{2,1,0:T(2,128)(2,1)S(1)}, bf16[16,2,256]{2,1,0:T(2,128)(2,1)S(1)}, u32[]{:S(2)}, u32[]{:S(2)}) %collective-permute-start.5) | collective-permute-done | bytes 16416 | tf_op jit(solution)/shard_map/ppermute | solution.py:368
  177.0 0.7 pad_maximum_fusion.4
  177.7 1.3 collective-permute-start.6
  179.0 1.5 collective-permute-start.7
  180.5 0.9 pad_maximum_fusion.1
  181.5 0.7 constant_dynamic-update-slice_fusion.22
  182.2 2.7 %collective-permute-done.7 = bf16[2,20,256]{2,1,0:T(8,128)(2,1)S(1)} collective-permute-done((bf16[2,20,256]{2,1,0:T(8,128)(2,1)S(1)}, bf16[2,20,256]{2,1,0:T(8,128)(2,1)S(1)}, u32[]{:S(2)}, u32[]{:S(2)}) %collective-permute-start.7) | collective-permute-done | bytes 20512 | tf_op jit(solution)/shard_map/ppermute | solution.py:368
  185.8 0.8 pad_maximum_fusion.3
  186.6 1.5 concatenate.68
  188.1 10.1 %compose.1 = f32[13,192,192]{2,1,0:T(8,128)} custom-call(bf16[320,256]{1,0:T(8,128)(2,1)} %bitcast.126, bf16[320,256]{1,0:T(8,128)(2,1)} %bitcast.124, bf16[320,256]{1,0:T(8,128)(2,1)} %bitcast.125, bf16[320,256]{1,0:T(8,128)(2,1)} %bitcast.123, bf16[16,256,256]{2,1,0:T(8,128)(2,1)} %decoder_kernels.1.m_ref, bf16[2,256,256]{2,1,0:T(8,128)(2,1)} %pad_maximum_fusion.edge_ref, ...), custom_call_target="tpu_custom_call" | custom-call | tf_op jit(solution)/shard_map/compose/pallas_call | solution.py:397
  (131 shorter events, 9.3 us)
Async XLA Ops:
  0.0 17.4 %copy-start = (bf16[1,16,1,1,4,16,1280]{6,5,4,3,2,1,0:T(8,128)(2,1)S(1)}, bf16[1,16,1,1,4,16,1280]{6,5,4,3,2,1,0:T(8,128)(2,1)}, u32[]{:S(2)}) copy-start(bf16[1,16,1,1,4,16,1280]{6,5,4,3,2,1,0:T(8,128)(2,1)} %param.24) | copy-start | bytes 7864324
  1.5 18.1 %collective-permute-start = (bf16[2,224]{1,0:T(2,128)(2,1)S(1)}, bf16[2,224]{1,0:T(2,128)(2,1)S(1)}, u32[]{:S(2)}, u32[]{:S(2)}) collective-permute-start(bf16[2,224]{1,0:T(2,128)(2,1)S(1)} %pad_maximum_fusion.7), channel_id=1, source_target_pairs={{0,1},{2,3},{4,5},{6,7},{8,9},{10,11},{12,13},{14,15},{16,17},{18,... | collective-permute-start | bytes 2696 | tf_op jit(solution)/shard_map/ppermute | solution.py:368
  6.4 13.2 %collective-permute-start.1 = (bf16[2,224]{1,0:T(2,128)(2,1)S(1)}, bf16[2,224]{1,0:T(2,128)(2,1)S(1)}, u32[]{:S(2)}, u32[]{:S(2)}) collective-permute-start(bf16[2,224]{1,0:T(2,128)(2,1)S(1)} %pad_maximum_fusion.7), channel_id=1, source_target_pairs={{1,0},{3,2},{5,4},{7,6},{9,8},{11,10},{13,12},{15,14},{17,16},{19,... | collective-permute-start | bytes 2696 | tf_op jit(solution)/shard_map/ppermute | solution.py:368
  17.4 9.7 %copy-start.4 = (bf16[9,13,16]{2,1,0:T(8,128)(2,1)S(1)}, bf16[9,13,16]{2,1,0:T(8,128)(2,1)}, u32[]{:S(2)}) copy-start(bf16[9,13,16]{2,1,0:T(8,128)(2,1)} %param.37) | copy-start | bytes 11236
  17.4 9.7 %copy-start.7 = (bf16[3,14,16,1,1]{2,0,1,4,3:T(4,128)(2,1)S(1)}, bf16[3,14,16,1,1]{2,0,1,4,3:T(4,128)(2,1)}, u32[]{:S(2)}) copy-start(bf16[3,14,16,1,1]{2,0,1,4,3:T(4,128)(2,1)} %constant.64) | copy-start | bytes 4036
  19.6 5.9 %collective-permute-start.3 = (bf16[3,2,224]{2,1,0:T(2,128)(2,1)S(1)}, bf16[3,2,224]{2,1,0:T(2,128)(2,1)S(1)}, u32[]{:S(2)}, u32[]{:S(2)}) collective-permute-start(bf16[3,2,224]{2,1,0:T(2,128)(2,1)S(1)} %pad_maximum_fusion.6), channel_id=1, source_target_pairs={{2,0},{4,2},{6,4},{8,6},{10,8},{12,10},{14,12},{16,14},{18,16},{20... | collective-permute-start | bytes 8072 | tf_op jit(solution)/shard_map/ppermute | solution.py:368
  20.9 5.9 %collective-permute-start.2 = (bf16[3,2,224]{2,1,0:T(2,128)(2,1)S(1)}, bf16[3,2,224]{2,1,0:T(2,128)(2,1)S(1)}, u32[]{:S(2)}, u32[]{:S(2)}) collective-permute-start(bf16[3,2,224]{2,1,0:T(2,128)(2,1)S(1)} %pad_maximum_fusion.6), channel_id=1, source_target_pairs={{0,2},{2,4},{4,6},{6,8},{8,10},{10,12},{12,14},{14,16},{16,18},{18... | collective-permute-start | bytes 8072 | tf_op jit(solution)/shard_map/ppermute | solution.py:368
  34.6 68.7 %all-to-all-start = ((bf16[16,64,1280]{2,1,0:T(8,128)(2,1)}), bf16[16,64,1280]{2,1,0:T(8,128)(2,1)S(1)}, u32[]{:S(2)}, u32[]{:S(2)}) async-start(bf16[16,64,1280]{2,1,0:T(8,128)(2,1)} %bitcast.114), calls=%async_computation | async-start | bytes 5242880 | tf_op jit(solution)/shard_map/all_to_all | solution.py:450
  42.6 4.7 %copy-start.8 = (pred[14]{0:T(512)(128)(4,1)S(1)}, pred[14]{0:T(512)(128)(4,1)}, u32[]{:S(2)}) copy-start(pred[14]{0:T(512)(128)(4,1)} %constant.57) | copy-start | bytes 46
  42.6 4.7 %copy-start.9 = (pred[14]{0:T(512)(128)(4,1)S(1)}, pred[14]{0:T(512)(128)(4,1)}, u32[]{:S(2)}) copy-start(pred[14]{0:T(512)(128)(4,1)} %constant.58) | copy-start | bytes 46
  78.5 16.0 %copy-start.3 = (bf16[224,256]{1,0:T(8,128)(2,1)S(1)}, bf16[224,256]{1,0:T(8,128)(2,1)}, u32[]{:S(2)}) copy-start(bf16[224,256]{1,0:T(8,128)(2,1)} %squeeze.51) | copy-start | bytes 344068
  78.5 18.0 %copy-start.5 = (f32[16,192]{1,0:T(8,128)S(1)}, f32[16,192]{1,0:T(8,128)}, u32[]{:S(2)}) copy-start(f32[16,192]{1,0:T(8,128)} %constant.62) | copy-start | bytes 36868
  78.5 18.0 %copy-start.6 = (f32[16,192]{1,0:T(8,128)S(1)}, f32[16,192]{1,0:T(8,128)}, u32[]{:S(2)}) copy-start(f32[16,192]{1,0:T(8,128)} %constant.63) | copy-start | bytes 36868
  103.3 1.5 copy-start.2
  154.9 17.7 %copy-start.10 = (bf16[13]{0:T(256)(128)(2,1)S(1)}, bf16[13]{0:T(256)(128)(2,1)}, u32[]{:S(2)}) copy-start(bf16[13]{0:T(256)(128)(2,1)} %param.38) | copy-start | bytes 82
  167.0 6.2 %collective-permute-start.4 = (bf16[16,2,256]{2,1,0:T(2,128)(2,1)S(1)}, bf16[16,2,256]{2,1,0:T(2,128)(2,1)S(1)}, u32[]{:S(2)}, u32[]{:S(2)}) collective-permute-start(bf16[16,2,256]{2,1,0:T(2,128)(2,1)S(1)} %get-tuple-element.49), channel_id=1, source_target_pairs={{0,1},{2,3},{4,5},{6,7},{8,9},{10,11},{12,13},{14,15},{16,17},{18,... | collective-permute-start | bytes 49160 | tf_op jit(solution)/shard_map/ppermute | solution.py:368
  171.3 5.6 %collective-permute-start.5 = (bf16[16,2,256]{2,1,0:T(2,128)(2,1)S(1)}, bf16[16,2,256]{2,1,0:T(2,128)(2,1)S(1)}, u32[]{:S(2)}, u32[]{:S(2)}) collective-permute-start(bf16[16,2,256]{2,1,0:T(2,128)(2,1)S(1)} %get-tuple-element.50), channel_id=1, source_target_pairs={{1,0},{3,2},{5,4},{7,6},{9,8},{11,10},{13,12},{15,14},{17,16},{19,... | collective-permute-start | bytes 49160 | tf_op jit(solution)/shard_map/ppermute | solution.py:368
  177.7 3.8 %collective-permute-start.6 = (bf16[2,20,256]{2,1,0:T(8,128)(2,1)S(1)}, bf16[2,20,256]{2,1,0:T(8,128)(2,1)S(1)}, u32[]{:S(2)}, u32[]{:S(2)}) collective-permute-start(bf16[2,20,256]{2,1,0:T(8,128)(2,1)S(1)} %get-tuple-element.48), channel_id=1, source_target_pairs={{0,2},{2,4},{4,6},{6,8},{8,10},{10,12},{12,14},{14,16},{16,18},{18... | collective-permute-start | bytes 61448 | tf_op jit(solution)/shard_map/ppermute | solution.py:368
  179.0 5.9 %collective-permute-start.7 = (bf16[2,20,256]{2,1,0:T(8,128)(2,1)S(1)}, bf16[2,20,256]{2,1,0:T(8,128)(2,1)S(1)}, u32[]{:S(2)}, u32[]{:S(2)}) collective-permute-start(bf16[2,20,256]{2,1,0:T(8,128)(2,1)S(1)} %get-tuple-element.47), channel_id=1, source_target_pairs={{2,0},{4,2},{6,4},{8,6},{10,8},{12,10},{14,12},{16,14},{18,16},{20... | collective-permute-start | bytes 61448 | tf_op jit(solution)/shard_map/ppermute | solution.py:368
  188.1 10.1 %copy-start.1 = (bf16[1,16,1,1,4,16,1280]{6,5,4,3,2,1,0:T(8,128)(2,1)S(1)}, bf16[1,16,1,1,4,16,1280]{6,5,4,3,2,1,0:T(8,128)(2,1)}, u32[]{:S(2)}) copy-start(bf16[1,16,1,1,4,16,1280]{6,5,4,3,2,1,0:T(8,128)(2,1)} %param.24) | copy-start | bytes 7864324

commit v2 on v1

v2 whole, which is shorter than its diff:
```python
import functools
import math

import jax
import jax.numpy as jnp
import numpy as np
from jax import lax
from jax.experimental import pallas as pl
from jax.experimental.pallas import tpu as pltpu
from jax.sharding import PartitionSpec as P

HEADS = 16
DATES = 4
PATCH = 14
INTERSECTION = 32
FEAT = 16
PATCHES = 16
RIM = 16
TILE_PX = PATCH * PATCHES
STRIDE = TILE_PX - INTERSECTION
SPAN = PATCH + 2
FAR_PATCH, FAR_PIXEL = divmod(STRIDE - 1, PATCH)
NEAR_PATCH, NEAR_PIXEL = divmod(INTERSECTION, PATCH)
LANES = 256
VMEM = 56 * 2**20

EXPONENT_BOUND = 100.0
SUM_ROWS = 16
PAIR = 2
GROUP = 256

norm_eps = 1e-06
bf16 = jnp.bfloat16
f32 = jnp.float32

NN = (((1,), (0,)), ((), ()))
NT = (((1,), (1,)), ((), ()))
TN = (((0,), (0,)), ((), ()))


def mm(left, right, dims=NN):
    return lax.dot_general(left, right, dims, preferred_element_type=f32)


def layer_norm(values, gain_row):
    average = jnp.mean(values, axis=-1, keepdims=True)
    centered = values - average
    spread = jnp.mean(centered * centered, axis=-1, keepdims=True)
    return centered * lax.rsqrt(spread + norm_eps) * gain_row


def gather_kernel(routes, index_ref, a_ref, *refs):
    outs, (held, in_sems, out_sems) = refs[:-3], refs[-3:]
    loads = [pltpu.make_async_copy(a_ref.at[index_ref[n]], held.at[n], in_sems.at[n]) for n in range(len(routes))]
    for load in loads:
        load.start()
    stores = []
    for n, (out, spot) in enumerate(routes):
        loads[n].wait()
        stores.append(pltpu.make_async_copy(held.at[n], outs[out].at[spot], out_sems.at[n]))
        stores[n].start()
    for store in stores:
        store.wait()


def gather_pieces(arrivals, owner_map, early, late, dates):
    slots, strip, width = arrivals.shape
    tiles = slots // dates
    date, tile = lax.axis_index("date"), lax.axis_index("tile")
    together = [0] + late
    routes, order = [], []
    for s in range(tiles):
        for m in range(dates):
            order.append((s, m))
            routes.append((early.index(s) - 1, m) if s in early[1:] else (len(early) - 1 + m, together.index(s)))
    s_of = jnp.array([s for s, _ in order], jnp.int32)
    m_of = jnp.array([m for _, m in order], jnp.int32)
    wanted = (date ^ m_of) * tiles + (tile ^ s_of)
    spots = jnp.arange(slots, dtype=jnp.int32)[None, :]
    index = jnp.sum(jnp.where(owner_map[None, :] == wanted[:, None], spots, 0), axis=1)
    shapes = [jax.ShapeDtypeStruct((dates, strip, width), bf16)] * (len(early) - 1)
    shapes += [jax.ShapeDtypeStruct((len(together), strip, width), bf16)] * dates
    anywhere = pl.BlockSpec(memory_space=pl.ANY)
    outs = pl.pallas_call(
        functools.partial(gather_kernel, routes),
        in_specs=[pl.BlockSpec(memory_space=pltpu.SMEM), anywhere],
        out_specs=[anywhere] * len(shapes),
        out_shape=shapes,
        scratch_shapes=[
            pltpu.VMEM(arrivals.shape, bf16),
            pltpu.SemaphoreType.DMA((slots,)),
            pltpu.SemaphoreType.DMA((slots,)),
        ],
        compiler_params=pltpu.CompilerParams(vmem_limit_bytes=16 * 2**20),
        name="gather_pieces",
    )(index, arrivals)
    return outs[: len(early) - 1], outs[len(early) - 1 :]


def swap(value, axis, mask):
    return lax.ppermute(value, axis, [(i, i ^ mask) for i in range(lax.axis_size(axis))])


def exchange(arrivals, owner_map):
    dates, tiles = lax.axis_size("date"), lax.axis_size("tile")
    late = list(range(tiles - max(1, tiles // 4), tiles))
    early = list(range(tiles - len(late)))
    rings, mixed = gather_pieces(arrivals, owner_map, early, late, dates)
    rings = [swap(ring, "tile", s) for s, ring in zip(early[1:], rings)]
    mixed = [value if m == 0 else swap(value, "date", m) for m, value in enumerate(mixed)]
    last = []
    for i, s in enumerate(late):
        pieces = jnp.stack([value[1 + i] for value in mixed])
        last.append(swap(pieces, "tile", s))
    first = [(value, 0) for value in mixed]
    for ring in rings:
        first += [(ring, 0) if m == 0 else (swap(ring[m : m + 1], "date", m), 0) for m in range(dates)]
    return first, [(value, m) for value in last for m in range(dates)]


def project_kernel(pieces, *refs):
    x_refs, (loc_ref, gain_ref, w_ref, o_ref, norm_ref, x_out, normed_ref) = refs[:pieces], refs[pieces:]
    step = pl.program_id(0)

    @pl.when(step == 0)
    def _():
        first = 0
        for x_ref in x_refs:
            for row in range(0, x_ref.shape[0], 64):
                x = x_ref[row : row + 64, :]
                x_out[first : first + x.shape[0], :] = x
                residual = x.astype(f32) + loc_ref[...]
                normed = layer_norm(residual, gain_ref[...].astype(f32))
                normed_ref[first : first + x.shape[0], :] = normed.astype(bf16)
                first += x.shape[0]

    packed = mm(w_ref[...], normed_ref[...], (((0,), (1,)), ((), ())))
    packed = packed.astype(bf16)
    o_ref[...] = packed
    packed = packed.astype(f32)
    heads = norm_ref.shape[0]
    squares = jnp.sum((packed * packed).reshape(heads, packed.shape[0] // heads, packed.shape[1]), axis=1)
    norm_ref[...] = jnp.broadcast_to(jnp.max(squares, axis=1, keepdims=True), norm_ref.shape)


def project(pieces, location, gain, weight):
    width = weight.shape[0]
    tokens = sum(piece.shape[1] for piece, _ in pieces)
    block = width // 2
    steps = weight.shape[1] // block
    row = pl.BlockSpec((1, width), lambda i: (0, 0))
    return pl.pallas_call(
        functools.partial(project_kernel, len(pieces)),
        grid=(steps,),
        in_specs=[pl.BlockSpec((None,) + piece.shape[1:], lambda i, n=n: (n, 0, 0)) for piece, n in pieces]
        + [row, row, pl.BlockSpec((width, block), lambda i: (0, i))],
        out_specs=[
            pl.BlockSpec((block, tokens), lambda i: (i, 0)),
            pl.BlockSpec((3 * HEADS // steps, 128), lambda i: (i, 0)),
            pl.BlockSpec((tokens, width), lambda i: (0, 0)),
        ],
        out_shape=[
            jax.ShapeDtypeStruct((weight.shape[1], tokens), bf16),
            jax.ShapeDtypeStruct((3 * HEADS, 128), f32),
            jax.ShapeDtypeStruct((tokens, width), bf16),
        ],
        scratch_shapes=[pltpu.VMEM((tokens, width), bf16)],
        compiler_params=pltpu.CompilerParams(vmem_limit_bytes=VMEM),
        cost_estimate=pl.CostEstimate(
            flops=2 * tokens * width * weight.shape[1], bytes_accessed=weight.size * 2, transcendentals=0
        ),
        name="project",
    )(*[piece for piece, _ in pieces], location, gain, weight)


def with_ones(values):
    return jnp.concatenate([values, jnp.ones((SUM_ROWS, values.shape[1]), bf16)], axis=0)


def attend_kernel(parts, *refs):
    q_refs, k_refs, v_refs, norm_refs = (refs[i * parts : (i + 1) * parts] for i in range(4))
    o_ref, flag_ref = refs[4 * parts :]
    head = o_ref.shape[0] // PAIR
    scale = math.log2(math.e) / math.sqrt(head)

    @pl.when(pl.program_id(0) == 0)
    def _():
        norms = norm_refs[0][...]
        for norm_ref in norm_refs[1:]:
            norms = jnp.maximum(norms, norm_ref[...])
        flag_ref[0] = jnp.max(norms[:HEADS] * norms[HEADS : 2 * HEADS])

    small = flag_ref[0] <= (EXPONENT_BOUND / scale) ** 2

    def rows(n):
        return slice(n * head, (n + 1) * head)

    def side_by_side(part_refs, n):
        return jnp.concatenate([ref[rows(n), :] for ref in part_refs], axis=1)

    def scores(n):
        return mm(side_by_side(k_refs, n), side_by_side(q_refs, n), TN)

    def finish(n, lifted):
        sums = mm(with_ones(side_by_side(v_refs, n)), lifted.astype(bf16))
        o_ref[rows(n), :] = (sums[:head] * (1.0 / sums[head : head + 1])).astype(bf16)

    @pl.when(small)
    def _():
        for n in range(PAIR):
            finish(n, jnp.exp2(scores(n) * scale))

    @pl.when(jnp.logical_not(small))
    def _():
        for n in range(PAIR):
            held = scores(n)
            finish(n, jnp.exp2((held - jnp.max(held, axis=0, keepdims=True)) * scale))


def attend(packed, norms):
    head = packed[0].shape[0] // (3 * HEADS)
    tokens = sum(part.shape[1] for part in packed)
    steps = HEADS // PAIR
    specs = []
    for p in range(3):
        for part in packed:
            specs.append(pl.BlockSpec((PAIR * head, part.shape[1]), lambda h, p=p: (h + p * steps, 0)))
    specs += [pl.BlockSpec(norm.shape, lambda h: (0, 0)) for norm in norms]
    return pl.pallas_call(
        functools.partial(attend_kernel, len(packed)),
        grid=(steps,),
        in_specs=specs,
        out_specs=pl.BlockSpec((PAIR * head, tokens), lambda h: (h, 0)),
        out_shape=jax.ShapeDtypeStruct((HEADS * head, tokens), bf16),
        scratch_shapes=[pltpu.SMEM((1,), f32)],
        compiler_params=pltpu.CompilerParams(vmem_limit_bytes=VMEM),
        name="attend",
    )(*(list(packed) * 3), *norms)


def reduce_kernel(
    place_ref, m_ref, w_ref, x0_ref, x1_ref, loc_ref, gain_ref, wr_ref, bias_ref, profile_ref,
    o_ref, last_ref, first_ref, encoded_ref, reduced_ref
):
    step = pl.program_id(0)
    steps = pl.num_programs(0)
    tiles, dates, strip, width = encoded_ref.shape
    held = jnp.where(step < steps - 1, x0_ref[...].astype(f32), x1_ref[...].astype(f32))
    updated = held + loc_ref[...] + mm(m_ref[...], w_ref[...], TN)
    encoded = layer_norm(updated, gain_ref[...].astype(f32)).astype(bf16)
    part = tiles // steps
    encoded_ref[pl.ds(step * part, part)] = encoded.reshape(part, dates, strip, width)

    @pl.when(step == steps - 1)
    def _():
        total = bias_ref[...].astype(f32)
        for m in range(dates):
            total = total + mm(encoded_ref[:, m].reshape(tiles * strip, width), wr_ref[place_ref[0] ^ m])
        total = 0.5 * total * (1.0 + lax.erf(total * math.sqrt(0.5)))
        for s in range(tiles):
            spot = pl.multiple_of((place_ref[1] ^ s) * strip, strip)
            for half in range(reduced_ref.shape[0]):
                lanes = slice(128 * half, 128 * (half + 1))
                reduced_ref[half, pl.ds(spot, strip), :] = total[s * strip : (s + 1) * strip, lanes]
        for half in range(reduced_ref.shape[0]):
            o_ref[:, 128 * half : 128 * (half + 1)] = reduced_ref[half].astype(bf16)

        def column(b):
            halves = [reduced_ref[half, pl.ds(b, PATCHES, stride=PATCHES), :] for half in range(reduced_ref.shape[0])]
            return jnp.concatenate(halves, axis=1)

        tail = jnp.zeros((PATCHES - 2, o_ref.shape[1]), f32)
        tail = jnp.concatenate([profile_ref[...].astype(f32), tail], axis=0)
        last = place_ref[2] == 1
        sent = [jnp.where(last, column(PATCHES - 2 + i), column(i)) for i in range(2)]
        last_ref[...] = jnp.concatenate(sent + [tail], axis=0).astype(bf16)
        first_ref[...] = jnp.concatenate([column(0), column(1), tail], axis=0).astype(bf16)


def reduce_dates(place, mixed, out_weight, x0, x1, location, gain, reduce_weight, reduce_bias, profile, tiles, dates):
    width, tokens = mixed.shape
    strip = tokens // (tiles * dates)
    dec = reduce_weight.shape[1]
    steps = tokens // GROUP
    row = pl.BlockSpec((1, width), lambda t: (0, 0))
    sent = jax.ShapeDtypeStruct((3 * PATCHES, dec), bf16)
    sent_spec = pl.BlockSpec((3 * PATCHES, dec), lambda t: (0, 0))
    patches = tiles * strip
    return pl.pallas_call(
        reduce_kernel,
        grid=(steps,),
        in_specs=[
            pl.BlockSpec(memory_space=pltpu.SMEM),
            pl.BlockSpec((width, GROUP), lambda t: (0, t)),
            pl.BlockSpec((width, width), lambda t: (0, 0)),
            pl.BlockSpec((GROUP, width), lambda t: (jnp.minimum(t, steps - 2), 0)),
            pl.BlockSpec((GROUP, width), lambda t: (0, 0)),
            row,
            row,
            pl.BlockSpec((dates, width, dec), lambda t: (0, 0, 0)),
            pl.BlockSpec((1, dec), lambda t: (0, 0)),
            pl.BlockSpec((2, dec), lambda t: (0, 0)),
        ],
        out_specs=[pl.BlockSpec((patches, dec), lambda t: (0, 0)), sent_spec, sent_spec],
        out_shape=[jax.ShapeDtypeStruct((patches, dec), bf16), sent, sent],
        scratch_shapes=[pltpu.VMEM((tiles, dates, strip, width), bf16), pltpu.VMEM((dec // 128, patches, 128), f32)],
        compiler_params=pltpu.CompilerParams(vmem_limit_bytes=VMEM),
        name="reduce_dates",
    )(place, mixed, out_weight, x0, x1, location, gain, reduce_weight.reshape(dates, width, dec), reduce_bias, profile)


FIRST_OWN = RIM // PATCH
LAST_OWN = PATCHES - 1 - FIRST_OWN
UPPER = [a for a in range(PATCHES) if PATCH * a + PATCH >= TILE_PX - RIM]
LOWER = [a for a in range(PATCHES) if PATCH * a - 1 < RIM]
ENTRIES = (
    [(0, a) for a in UPPER]
    + [(0, None)]
    + [(1, a) for a in range(FIRST_OWN, LAST_OWN + 1)]
    + [(2, a) for a in LOWER]
    + [(2, None)]
)
SIDE = 16


def placement():
    main = np.zeros((3, SPAN, PATCHES, STRIDE), np.float32)
    side = np.zeros((3, SIDE, STRIDE), np.float32)
    for j in range(SPAN):
        for slot in range(PATCHES):
            if slot == 0:
                which, x = 0, PATCH * (PATCHES - 1) + j - 1
            elif slot == PATCHES - 1:
                which, x = 2, j - 1
            else:
                which, x = 1, PATCH * slot + j - 1
            column = x + (which - 1) * STRIDE - RIM
            if 0 <= x < TILE_PX and 0 <= column < STRIDE:
                main[which, j, slot, column] = 1.0
    rows = []
    for j in range(SPAN):
        x = PATCH * (PATCHES - 2) + j - 1
        if TILE_PX - RIM <= x < TILE_PX:
            side[0, len(rows), x - (TILE_PX - RIM)] = 1.0
            rows.append((0, j))
    for j in range(SPAN):
        x = PATCH + j - 1
        if 0 <= x < RIM:
            side[2, len(rows), STRIDE - RIM + x] = 1.0
            rows.append((2, j))
    side[0, len(rows), RIM - 1] = 1.0
    side[2, len(rows) + 1, STRIDE - RIM] = 1.0
    return main.reshape(3, SPAN * PATCHES, STRIDE), side, rows


PLACE_MAIN, PLACE_SIDE, SIDE_ROWS = placement()


def windows():
    table = np.zeros((3, LANES, STRIDE), np.float32)
    for x in range(STRIDE):
        table[1, x + RIM, x] = 1.0
    for x in range(RIM):
        table[0, TILE_PX - RIM + x, x] = 1.0
        table[2, x, STRIDE - RIM + x] = 1.0
    return table


def row_lanes(classes):
    table = np.zeros((LANES, len(ENTRIES), LANES), np.float32)
    for n, (tile_row, a) in enumerate(ENTRIES):
        for k in range(classes):
            if a is None:
                halo = classes * SPAN + k + (classes if tile_row == 0 else 0)
                table[TILE_PX - 1 if tile_row == 0 else 0, n, halo] = 1.0
                continue
            for i in range(SPAN):
                y = PATCH * a - 1 + i
                if 0 <= y < TILE_PX:
                    table[y, n, k * SPAN + i] = 1.0
    return table.reshape(LANES, -1)


def tap_tables(classes):
    rows = np.zeros((LANES, classes), np.float32)
    columns = np.zeros((FEAT, FEAT * PATCH), np.float32)
    meet = np.zeros((3, LANES, FEAT, PATCH), np.float32)
    for f in range(FEAT):
        columns[f, f * PATCH : (f + 1) * PATCH] = 1.0
    for k in range(classes):
        rows[k * SPAN : (k + 1) * SPAN, k] = 1.0
        rows[classes * SPAN + k, k] = 1.0
        rows[classes * (SPAN + 1) + k, k] = 1.0
        for dy in range(3):
            for i in range(PATCH):
                meet[dy, k * SPAN + i + 2 - dy, :, i] = 1.0
        meet[0, classes * SPAN + k, :, FAR_PIXEL] = 1.0
        meet[2, classes * (SPAN + 1) + k, :, NEAR_PIXEL] = 1.0
    return rows, columns, meet.reshape(3, LANES, FEAT * PATCH)


def kernels_kernel(up_ref, taps_ref, rows_ref, columns_ref, meet_ref, o_ref, edge_ref, turned_ref, column_ref):
    for half in range(turned_ref.shape[0]):
        lanes = slice(128 * half, 128 * (half + 1))
        turned_ref[half] = up_ref[lanes, :].astype(f32).T
        for j in range(PATCH):
            column_ref[j, :, lanes] = turned_ref[half, pl.ds(j, FEAT * PATCH, stride=PATCH), :].astype(bf16)
    spread = []
    for dx in range(3):
        total = None
        for dy in range(3):
            taps = mm(mm(rows_ref[...], taps_ref[3 * dy + dx]).astype(bf16), columns_ref[...])
            part = taps * meet_ref[dy].astype(f32)
            total = part if total is None else total + part
        spread.append(total.astype(bf16))
    for big in range(SPAN):
        total = None
        for dx in range(3):
            j = big - 2 + dx
            if 0 <= j < PATCH:
                part = mm(spread[dx], column_ref[j])
                total = part if total is None else total + part
        o_ref[big] = total.astype(bf16)
    edge_ref[0] = mm(spread[2], column_ref[NEAR_PIXEL]).astype(bf16)
    edge_ref[1] = mm(spread[0], column_ref[FAR_PIXEL]).astype(bf16)


def decoder_kernels(upsample_weight, class_weight):
    channels = upsample_weight.shape[0]
    tables = [jnp.asarray(table, bf16) for table in tap_tables(class_weight.shape[1])]
    return pl.pallas_call(
        kernels_kernel,
        out_shape=[
            jax.ShapeDtypeStruct((SPAN, LANES, channels), bf16),
            jax.ShapeDtypeStruct((2, LANES, channels), bf16),
        ],
        scratch_shapes=[
            pltpu.VMEM((channels // 128, upsample_weight.shape[1], 128), f32),
            pltpu.VMEM((PATCH, FEAT * PATCH, channels), bf16),
        ],
        compiler_params=pltpu.CompilerParams(vmem_limit_bytes=VMEM),
        name="decoder_kernels",
    )(upsample_weight, class_weight, *tables)


def compose_kernel(
    classes, own_ref, before_ref, after_ref, above_ref, below_ref, profile_ref, m_ref, edge_ref,
    lanes_ref, window_ref, place_ref, side_ref, bias_ref,
    o_ref, a_ref, b_ref, z_ref, z2_ref, acc_ref
):
    count = len(ENTRIES)
    edge = len(UPPER)
    own, before, after, above, below = (
        ref[...].astype(f32) for ref in (own_ref, before_ref, after_ref, above_ref, below_ref)
    )
    slot = lax.broadcasted_iota(jnp.int32, (PATCHES, LANES), 0)

    def line(tile_row, a):
        if tile_row == 1 or a is None:
            a = a if a is not None else (NEAR_PATCH if tile_row == 0 else FAR_PATCH)
            sides = [before[a : a + 1], before[PATCHES + a : PATCHES + a + 1]]
            sides += [after[a : a + 1], after[PATCHES + a : PATCHES + a + 1]]
            return own[PATCHES * a : PATCHES * (a + 1)], sides
        source = above if tile_row == 0 else below
        n = (UPPER if tile_row == 0 else LOWER).index(a)
        first = PATCHES * edge + 4 * n
        return source[PATCHES * n : PATCHES * (n + 1)], [source[first + i : first + i + 1] for i in range(4)]

    def slots(rows, base):
        for i, row in rows.items():
            base = jnp.where(slot == i, row, base)
        return base

    def second(before_row, after_row, near, far):
        rows = {i: before_row if which == 0 else after_row for i, (which, _) in enumerate(SIDE_ROWS)}
        rows[len(SIDE_ROWS)] = near
        rows[len(SIDE_ROWS) + 1] = far
        return slots(rows, jnp.zeros((SIDE, LANES), f32))

    profile = profile_ref[...].astype(f32)
    tail = slice(2 * PATCHES, 2 * PATCHES + 2)
    ends = slice((PATCHES + 4) * edge, (PATCHES + 4) * edge + 6)
    profiles = jnp.concatenate([above[ends], before[tail], profile, after[tail], below[ends]], axis=0)
    row_profiles = [profiles[2 * i : 2 * i + 1] for i in range(9)]
    col_profiles = [profiles[2 * i + 1 : 2 * i + 2] for i in range(9)]
    blank = jnp.zeros((PATCHES - 9, LANES), f32)
    row_table = jnp.concatenate(row_profiles + [blank], axis=0).astype(bf16)
    col_table = jnp.concatenate(col_profiles + [blank], axis=0).astype(bf16)
    weights = mm(row_table, lanes_ref[...])
    rows = [mm(row_table, window_ref[i]) for i in range(3)]
    cols = [mm(col_table, window_ref[i]) for i in range(3)]
    block_rows = jnp.concatenate([rows[i // 3][i : i + 1] for i in range(9)] + [blank[:, :STRIDE]], axis=0)
    block_cols = jnp.concatenate([cols[i % 3][i : i + 1] for i in range(9)] + [blank[:, :STRIDE]], axis=0)
    den = mm(block_rows.astype(bf16), block_cols.astype(bf16), TN)
    spots, side_spots = [], []
    for tile_row in range(3):
        spots.append(sum(place_ref[i].astype(f32) * block_cols[3 * tile_row + i][None] for i in range(3)).astype(bf16))
        side_spots.append(
            sum(side_ref[i].astype(f32) * block_cols[3 * tile_row + i][None] for i in range(3)).astype(bf16)
        )

    def entry_weights(n, tile_row):
        return [weights[3 * tile_row + i : 3 * tile_row + i + 1, LANES * n : LANES * (n + 1)] for i in range(3)]

    main_weights, side_weights = [], []
    for n, (tile_row, a) in enumerate(ENTRIES):
        patches, (l_far, l_near, r_near, r_far) = line(tile_row, a)
        a_ref[n] = slots({0: l_near, PATCHES - 1: r_near}, patches).astype(bf16)
        b_ref[n] = second(
            l_far, r_far, patches[NEAR_PATCH : NEAR_PATCH + 1], patches[FAR_PATCH : FAR_PATCH + 1]
        ).astype(bf16)
        left, middle, right = entry_weights(n, tile_row)
        main_weights.append(slots({0: left, PATCHES - 1: right}, jnp.broadcast_to(middle, (PATCHES, LANES))))
        side_weights.append(second(left, right, left, right))
    main_weights = jnp.stack(main_weights)
    for j in range(SPAN):
        z = mm(a_ref[...].reshape(count * PATCHES, LANES), m_ref[j], NT).reshape(count, PATCHES, LANES)
        z_ref[:, j] = (z * main_weights).astype(bf16)
    side_slot = lax.broadcasted_iota(jnp.int32, (count, SIDE, LANES), 1)
    patches = b_ref[...].astype(f32)
    total = None
    for i in range(len(SIDE_ROWS) + 2):
        kernel = m_ref[SIDE_ROWS[i][1]] if i < len(SIDE_ROWS) else edge_ref[i - len(SIDE_ROWS)]
        part = jnp.where(side_slot == i, patches, 0.0).astype(bf16).reshape(count * SIDE, LANES)
        part = mm(part, kernel, NT)
        total = part if total is None else total + part
    z2_ref[...] = (total.reshape(count, SIDE, LANES) * jnp.stack(side_weights)).astype(bf16)

    acc_ref[...] = jnp.zeros_like(acc_ref)
    for n, (tile_row, a) in enumerate(ENTRIES):
        part = mm(z_ref[n].reshape(SPAN * PATCHES, LANES), spots[tile_row], TN)
        part += mm(z2_ref[n], side_spots[tile_row], TN)
        if a is None:
            first = classes * SPAN + (classes if tile_row == 0 else 0)
            y = 2 * RIM - 1 if tile_row == 0 else STRIDE
            for k in range(classes):
                acc_ref[k, y : y + 1, :] += part[first + k : first + k + 1]
            continue
        y = PATCH * a - 1 + (tile_row - 1) * STRIDE
        low, high = 0, SPAN
        if tile_row == 0:
            high = min(SPAN, TILE_PX - (PATCH * a - 1))
        if tile_row == 2:
            low = max(0, 1 - PATCH * a)
        for k in range(classes):
            acc_ref[k, y + low : y + high, :] += part[k * SPAN + low : k * SPAN + high]
    inverse = 1.0 / jnp.maximum(den, 1.0)
    for k in range(classes):
        o_ref[k] = (acc_ref[k, RIM : RIM + STRIDE, :] + bias_ref[k] * den) * inverse


def forward(size):
    return [(i, i + 1) for i in range(size - 1)]


def backward(size):
    return [(i + 1, i) for i in range(size - 1)]


def exchange_rims(reduced, last, first, profile):
    cols = lax.axis_size("col")
    if cols == 2:
        other = swap(last, "col", 1)
        at_end = lax.axis_index("col") == 1
        before, after = jnp.where(at_end, other, 0), jnp.where(at_end, 0, other)
    else:
        before = lax.ppermute(last, "col", forward(cols))
        after = lax.ppermute(first, "col", backward(cols))

    def lines(rows):
        parts = [reduced[PATCHES * a : PATCHES * (a + 1)] for a in rows]
        for a in rows:
            for side in (before, after):
                parts += [side[a : a + 1], side[PATCHES + a : PATCHES + a + 1]]
        parts += [before[2 * PATCHES : 2 * PATCHES + 2], profile, after[2 * PATCHES : 2 * PATCHES + 2]]
        used = (PATCHES + 4) * len(rows) + 6
        parts.append(jnp.zeros((-used % 16, reduced.shape[1]), bf16))
        return jnp.concatenate(parts, axis=0)

    rows = lax.axis_size("date") * lax.axis_size("tile")
    above = lax.ppermute(lines(UPPER), ("date", "tile"), forward(rows))
    below = lax.ppermute(lines(LOWER), ("date", "tile"), backward(rows))
    return before, after, above, below


def compose(reduced, rims, profile, kernels, edges, class_bias, classes):
    channels = reduced.shape[1]
    count = len(ENTRIES)
    whole = pl.BlockSpec(memory_space=pltpu.VMEM)
    tables = [jnp.asarray(t, bf16) for t in (row_lanes(classes), windows(), PLACE_MAIN, PLACE_SIDE)]
    return pl.pallas_call(
        functools.partial(compose_kernel, classes),
        in_specs=[whole] * 12 + [pl.BlockSpec(memory_space=pltpu.SMEM)],
        out_specs=whole,
        out_shape=jax.ShapeDtypeStruct((classes, STRIDE, STRIDE), f32),
        scratch_shapes=[
            pltpu.VMEM((count, PATCHES, channels), bf16),
            pltpu.VMEM((count, SIDE, channels), bf16),
            pltpu.VMEM((count, SPAN, PATCHES, LANES), bf16),
            pltpu.VMEM((count, SIDE, LANES), bf16),
            pltpu.VMEM((classes, TILE_PX, STRIDE), f32),
        ],
        compiler_params=pltpu.CompilerParams(vmem_limit_bytes=VMEM),
        name="compose",
    )(reduced, *rims, profile, kernels, edges, *tables, class_bias.astype(f32))


def local(
    arrivals,
    owner_map,
    block_ids,
    tile_valid,
    blend_weights,
    location_table,
    norm_gain,
    qkv_weight,
    out_weight,
    final_gain,
    reduce_weight,
    reduce_bias,
    upsample_weight,
    class_weight,
    class_bias,
):
    width = arrivals.shape[-1]
    slots = arrivals.shape[1]
    classes = class_weight.shape[1]
    dates, tiles = lax.axis_size("date"), lax.axis_size("tile")
    first, last = exchange(arrivals.reshape(slots, -1, width), owner_map[0])

    codes = block_ids.reshape(1, 1)
    one_hot = (codes == jnp.arange(location_table.shape[0], dtype=jnp.int32)[None, :]).astype(bf16)
    location = jnp.dot(one_hot, location_table, preferred_element_type=f32)
    profile = blend_weights.reshape(2, TILE_PX).astype(bf16)
    profile = jnp.concatenate([profile[:1] * tile_valid.reshape(1).astype(bf16), profile[1:]], axis=0)
    profile = jnp.pad(profile, ((0, 0), (0, LANES - TILE_PX)))
    kernels, edges = decoder_kernels(upsample_weight, class_weight)

    arrays = [array for array, _ in first]
    arrays, location, profile, kernels, edges = lax.optimization_barrier((arrays, location, profile, kernels, edges))
    first = [(array, n) for array, (_, n) in zip(arrays, first)]
    packed0, norms0, x0 = project(first, location, norm_gain[None], qkv_weight)
    packed1, norms1, x1 = project(last, location, norm_gain[None], qkv_weight)
    mixed = attend([packed0, packed1], [norms0, norms1])
    go_last = jnp.where((lax.axis_index("col") == 0) | (lax.axis_size("col") != 2), 1, 0)
    place = jnp.stack([lax.axis_index("date"), lax.axis_index("tile"), go_last]).astype(jnp.int32)
    reduced, to_after, to_before = reduce_dates(
        place, mixed, out_weight, x0, x1, location, final_gain[None], reduce_weight, reduce_bias[None], profile, tiles, dates
    )
    rims = exchange_rims(reduced, to_after, to_before, profile)
    return compose(reduced, rims, profile, kernels, edges, class_bias, classes)[None]


def solution(mesh):
    placed = (
        P(None, None, "col", "date", "tile", None, None),
        P(),
        P(None, ("date", "tile"), "col"),
        P(None, ("date", "tile"), "col"),
        P(None, ("date", "tile"), "col", None, None),
    ) + (P(),) * 10
    return jax.shard_map(
        local,
        mesh=mesh,
        in_specs=placed,
        out_specs=P(None, None, ("date", "tile"), "col"),
        check_vma=False,
    )
```

time: 202 us -> 153 us (0.76); the launches traced: 198 us -> 153 us
  local copies, waits for them, and re-layouts: 54.8 us -> 14.1 us
  waiting for transfers between devices: 10.8 us -> 24.1 us
  other arithmetic: 13.8 us -> 3.27 us
  matrix products: 4.52 us -> 0.71 us
  starting transfers between devices: 28.4 us -> 24.7 us
    ppermute x8 -> x15, waiting for transfers between devices: 7.72 us -> 24.1 us  [the longest x13 20.3 us: swap(): lax.ppermute(value, axis, [(i, i ^ mask) for i in range(lax.axis_size(axi...]
    optimization_barrier x1 -> x0, local copies, waits for them, and re-layouts: 13.7 us -> none  [local(): lax.optimization_barrier((ordered, profiles, qkv_weight, upsample_weight,...]
    reshape x4 -> x0, local copies, waits for them, and re-layouts: 11.8 us -> none  [the longest x2 7.8 us: decoder_kernels(): upsample_weight.reshape(channels, FEAT * PATCH, PATCH).transpose(2, 0, 1)]
    concatenate x8 -> x2, local copies, waits for them, and re-layouts: 9.59 us -> 0.12 us  [lines(): return jnp.concatenate(parts, axis=0)]
    all_to_all x1 -> x0, starting transfers between devices: 7.99 us -> none  [local(): lax.all_to_all(ordered, ('date', 'tile'), split_axis=0, concat_axis=0, ti...]
    unnamed x52 -> x43, local copies, waits for them, and re-layouts: 3.18 us -> 7.53 us
    ppermute x8 -> x15, starting transfers between devices: 20.4 us -> 24.7 us  [the longest x13 15.7 us: swap(): lax.ppermute(value, axis, [(i, i ^ mask) for i in range(lax.axis_size(axi...]
    concatenate x7 -> x1, other arithmetic: 4.33 us -> 0.53 us  [local(): jnp.concatenate([profile[:1] * tile_valid.reshape(1).astype(bf16), profil...]
  transfers between devices with their start and end apart: 9 -> 15, of which waited for: 4 -> 7; matrix products, arithmetic and copies ran while one was open for 29% -> 8% of each run, Pallas kernels for 6% -> 13%
where the time goes in v2:
time: 153 us
  Pallas kernels  84.2 us (55%)
  starting transfers between devices  24.7 us (16%)
  waiting for transfers between devices  24.1 us (16%)
  local copies, waits for them, and re-layouts  14.1 us (9%)
  other arithmetic  3.27 us (2%)
  between operations  1.57 us (1%)
    pallas_call x1, Pallas kernels, attend(): pl.pallas_call(functools.partial(attend_kernel, len(packed)), grid=(steps...  28 us
    pallas_call x2, Pallas kernels, project(): pl.pallas_call(functools.partial(project_kernel, len(pieces)), grid=(step...  22.9 us
    ppermute x13, waiting for transfers between devices, swap(): lax.ppermute(value, axis, [(i, i ^ mask) for i in range(lax.axis_size(axi...  20.3 us
    ppermute x13, starting transfers between devices, swap(): lax.ppermute(value, axis, [(i, i ^ mask) for i in range(lax.axis_size(axi...  15.7 us
    pallas_call x1, Pallas kernels, reduce_dates(): pl.pallas_call(reduce_kernel, grid=(steps,), in_specs=[pl.BlockSpec(memor...  10.8 us
    pallas_call x1, Pallas kernels, compose(): pl.pallas_call(functools.partial(compose_kernel, classes), in_specs=[whol...  8.53 us
    pallas_call x1, Pallas kernels, gather_pieces(): pl.pallas_call(functools.partial(gather_kernel, routes), in_specs=[pl.Blo...  8.25 us
    ppermute x1, starting transfers between devices, exchange_rims(): above = lax.ppermute(lines(UPPER), ('date', 'tile'), forward(rows))  7.65 us
  transfers between devices with their start and end apart: 15, of which 7 were waited for; matrix products, arithmetic and copies ran while one was open for 8% of the time, Pallas kernels for 13%

profile of v2, /device:TPU:0, one launch (start us, length us, event | category | flops | bytes accessed | tf_op | source)
XLA Modules:
  0.0 152.6 jit_solution(6966578885334312203)
XLA Ops:
  0.0 0.7 xor_add_fusion
  0.7 0.8 select_reduce_fusion.index_ref
  1.5 1.7 %copy-done.1 = bf16[1,16,1,1,4,16,1280]{6,5,4,3,2,1,0:T(8,128)(2,1)S(1)} copy-done((bf16[1,16,1,1,4,16,1280]{6,5,4,3,2,1,0:T(8,128)(2,1)S(1)}, bf16[1,16,1,1,4,16,1280]{6,5,4,3,2,1,0:T(8,128)(2,1)}, u32[]{:S(2)}) %copy-start.1) | copy-done | bytes 2621464
  3.3 8.2 %gather_pieces.1 = (bf16[4,64,1280]{2,1,0:T(8,128)(2,1)S(1)}, bf16[4,64,1280]{2,1,0:T(8,128)(2,1)S(1)}, bf16[2,64,1280]{2,1,0:T(8,128)(2,1)S(1)}, bf16[2,64,1280...) custom-call(s32[16]{0:T(128)S(1)} %select_reduce_fusion.index_ref, ...), custom_call_target="tpu_custom_call" | custom-call | tf_op jit(solution)/shard_map/gather_pieces/pallas_call | solution.py:84
  11.6 0.5 collective-permute-start
  12.1 2.6 %collective-permute-start.1 = (bf16[2,64,1280]{2,1,0:T(8,128)(2,1)S(1)}, bf16[2,64,1280]{2,1,0:T(8,128)(2,1)}, u32[]{:S(2)}, u32[]{:S(2)}) collective-permute-start(bf16[2,64,1280]{2,1,0:T(8,128)(2,1)S(1)} %get-tuple-element.39), channel_id=1, source_target_pairs={{0,16},{8,24},{16,0},{24,8},{1,17},{9,25},{17,1},{25,9},{2,18},{10... | collective-permute-start | bytes 983048 | tf_op jit(solution)/shard_map/ppermute | solution.py:101
  14.7 1.8 %collective-permute-start.3 = (bf16[4,64,1280]{2,1,0:T(8,128)(2,1)S(1)}, bf16[4,64,1280]{2,1,0:T(8,128)(2,1)S(1)}, u32[]{:S(2)}, u32[]{:S(2)}) collective-permute-start(bf16[4,64,1280]{2,1,0:T(8,128)(2,1)S(1)} %get-tuple-element.41), channel_id=1, source_target_pairs={{0,2},{2,0},{4,6},{6,4},{1,3},{3,1},{5,7},{7,5},{8,10},{10,8},{12,... | collective-permute-start | bytes 1966088 | tf_op jit(solution)/shard_map/ppermute | solution.py:101
  16.5 2.6 %collective-permute-start.7 = (bf16[4,64,1280]{2,1,0:T(8,128)(2,1)S(1)}, bf16[4,64,1280]{2,1,0:T(8,128)(2,1)}, u32[]{:S(2)}, u32[]{:S(2)}) collective-permute-start(bf16[4,64,1280]{2,1,0:T(8,128)(2,1)S(1)} %get-tuple-element.42), channel_id=1, source_target_pairs={{0,4},{2,6},{4,0},{6,2},{1,5},{3,7},{5,1},{7,3},{8,12},{10,14},{12... | collective-permute-start | bytes 1966088 | tf_op jit(solution)/shard_map/ppermute | solution.py:101
  20.4 3.6 %copy.26.up_ref = bf16[256,3136]{1,0:T(8,128)(2,1)} copy(bf16[256,3136]{0,1:T(8,128)(2,1)} %param.36) | data formatting | bytes 3211264 | tf_op args[12]
  24.1 0.6 broadcast_in_dim.37.refs_13_.refs_5_
  24.7 0.6 broadcast_in_dim.38.gain_ref
  25.3 0.5 broadcast_in_dim.39.bias_ref
  25.8 5.6 %decoder_kernels.1 = (bf16[16,256,256]{2,1,0:T(8,128)(2,1)}, bf16[2,256,256]{2,1,0:T(8,128)(2,1)}) custom-call(bf16[256,3136]{1,0:T(8,128)(2,1)} %copy.26.up_ref, bf16[9,13,16]{2,1,0:T(8,128)(2,1)} %taps_ref.1, bf16[256,13]{1,0:T(8,128)(2,1)} %constant.40.clone.rows_ref, bf16[16,224]{1,0:T(8,128)(2,1)} %constant.41.clone.columns_ref, ...), custom_call_target="tpu_custom_call" | custom-call | tf_op jit(solution)/shard_map/decoder_kernels/pallas_call | solution.py:431
  31.4 0.5 fusion.5.profile_ref
  32.0 0.6 pad_add_fusion.place_ref
  32.6 0.7 fusion.2.refs_12_.refs_4_.loc_ref
  33.3 0.9 slice.149
  34.2 0.9 slice.148
  35.2 0.9 slice.147
  36.1 9.6 %collective-permute-done.3.refs_4_ = bf16[4,64,1280]{2,1,0:T(8,128)(2,1)S(1)} collective-permute-done((bf16[4,64,1280]{2,1,0:T(8,128)(2,1)S(1)}, bf16[4,64,1280]{2,1,0:T(8,128)(2,1)S(1)}, u32[]{:S(2)}, u32[]{:S(2)}) %collective-permute-start.3) | collective-permute-done | bytes 655392 | tf_op jit(solution)/shard_map/ppermute | solution.py:101
  45.7 0.1 collective-permute-start.4
  45.8 1.7 %collective-permute-start.5 = (bf16[1,64,1280]{2,1,0:T(8,128)(2,1)S(1)}, bf16[1,64,1280]{2,1,0:T(8,128)(2,1)S(1)}, u32[]{:S(2)}, u32[]{:S(2)}) collective-permute-start(bf16[1,64,1280]{2,1,0:T(8,128)(2,1)S(1)} %get-tuple-element.73), channel_id=1, source_target_pairs={{0,16},{8,24},{16,0},{24,8},{1,17},{9,25},{17,1},{25,9},{2,18},{10... | collective-permute-start | bytes 491528 | tf_op jit(solution)/shard_map/ppermute | solution.py:101
  47.5 0.1 collective-permute-start.6
  47.7 0.6 collective-permute-done.7.refs_8_
  48.3 1.1 fusion.9
  49.4 0.1 collective-permute-start.8
  49.5 1.6 %collective-permute-start.9 = (bf16[1,64,1280]{2,1,0:T(8,128)(2,1)S(1)}, bf16[1,64,1280]{2,1,0:T(8,128)(2,1)S(1)}, u32[]{:S(2)}, u32[]{:S(2)}) collective-permute-start(bf16[1,64,1280]{2,1,0:T(8,128)(2,1)S(1)} %get-tuple-element.70), channel_id=1, source_target_pairs={{0,16},{8,24},{16,0},{24,8},{1,17},{9,25},{17,1},{25,9},{2,18},{10... | collective-permute-start | bytes 491528 | tf_op jit(solution)/shard_map/ppermute | solution.py:101
  51.1 0.3 collective-permute-start.10
  51.4 0.1 pad_maximum_fusion
  51.5 1.4 collective-permute-done.5.refs_6_
  52.9 2.6 %collective-permute-start.11 = (bf16[4,64,1280]{2,1,0:T(8,128)(2,1)S(1)}, bf16[4,64,1280]{2,1,0:T(8,128)(2,1)S(1)}, u32[]{:S(2)}, u32[]{:S(2)}) collective-permute-start(bf16[4,64,1280]{2,1,0:T(8,128)(2,1)S(1)} %pad_maximum_fusion), channel_id=1, source_target_pairs={{0,6},{2,4},{4,2},{6,0},{1,7},{3,5},{5,3},{7,1},{8,14},{10,12},{12... | collective-permute-start | bytes 1966088 | tf_op jit(solution)/shard_map/ppermute | solution.py:101
  55.6 4.3 %collective-permute-done.9.refs_10_ = bf16[1,64,1280]{2,1,0:T(8,128)(2,1)S(1)} collective-permute-done((bf16[1,64,1280]{2,1,0:T(8,128)(2,1)S(1)}, bf16[1,64,1280]{2,1,0:T(8,128)(2,1)S(1)}, u32[]{:S(2)}, u32[]{:S(2)}) %collective-permute-start.9) | collective-permute-done | bytes 163872 | tf_op jit(solution)/shard_map/ppermute | solution.py:101
  59.9 2.6 %collective-permute-done.10.refs_11_ = bf16[1,64,1280]{2,1,0:T(8,128)(2,1)S(1)} collective-permute-done((bf16[1,64,1280]{2,1,0:T(8,128)(2,1)S(1)}, bf16[1,64,1280]{2,1,0:T(8,128)(2,1)S(1)}, u32[]{:S(2)}, u32[]{:S(2)}) %collective-permute-start.10) | collective-permute-done | bytes 163872 | tf_op jit(solution)/shard_map/ppermute | solution.py:101
  62.5 0.6 copy-done.18
  63.2 14.1 %project.2 = (bf16[3840,768]{1,0:T(8,128)(2,1)}, f32[48,128]{1,0:T(8,128)}, bf16[768,1280]{1,0:T(8,128)(2,1)}) custom-call(bf16[2,64,1280]{2,1,0:T(8,128)(2,1)} %copy-done.2, bf16[2,64,1280]{2,1,0:T(8,128)(2,1)} %collective-permute-done.refs_1_, bf16[2,64,1280]{2,1,0:T(8,128)(2,1)} %collective-permute-done.1.refs_2_, ...), custom_call_target="tpu_custom_call" | custom-call | flops 7549747200 | bytes 9830400 | tf_op jit(solution)/shard_map/project/pallas_call | solution.py:152
  77.3 0.8 copy-done.3
  78.1 8.9 %project.3 = (bf16[3840,256]{1,0:T(8,128)(2,1)}, f32[48,128]{1,0:T(8,128)}, bf16[256,1280]{1,0:T(8,128)(2,1)}) custom-call(bf16[4,64,1280]{2,1,0:T(8,128)(2,1)} %copy-done.3, bf16[4,64,1280]{2,1,0:T(8,128)(2,1)} %copy-done.3, bf16[4,64,1280]{2,1,0:T(8,128)(2,1)} %copy-done.3, bf16[4,64,1280]{2,1,0:T(8,128)(2,1)} %copy-done.3, ...), custom_call_target="tpu_custom_call" | custom-call | flops 2516582400 | bytes 9830400 | tf_op jit(solution)/shard_map/project/pallas_call | solution.py:152
  87.0 28.0 %attend.1.m_ref = bf16[1280,1024]{1,0:T(8,128)(2,1)} custom-call(bf16[3840,768]{1,0:T(8,128)(2,1)} %get-tuple-element.58.refs_0_.refs_2_.refs_4_, bf16[3840,256]{1,0:T(8,128)(2,1)} %get-tuple-element.59.refs_1_.refs_3_.refs_5_, bf16[3840,768]{1,0:T(8,128)(2,1)} %get-tuple-element.58.refs_0_.refs_2_.refs_4_, ...), custom_call_target="tpu_custom_call" | custom-call | tf_op jit(solution)/shard_map/attend/pallas_call | solution.py:229
  115.0 10.8 %reduce_dates.1 = (bf16[256,256]{1,0:T(8,128)(2,1)}, bf16[48,256]{1,0:T(8,128)(2,1)}, bf16[48,256]{1,0:T(8,128)(2,1)}) custom-call(s32[3]{0:T(128)} %pad_add_fusion.place_ref, bf16[1280,1024]{1,0:T(8,128)(2,1)} %attend.1.m_ref, bf16[1280,1280]{1,0:T(8,128)(2,1)} %w_ref.1, bf16[768,1280]{1,0:T(8,128)(2,1)} %get-tuple-element.62.x0_ref, ...), custom_call_target="tpu_custom_call" | custom-call | tf_op jit(solution)/shard_map/reduce_dates/pallas_call | solution.py:289
  125.9 1.7 %collective-permute-start.12 = (bf16[48,256]{1,0:T(8,128)(2,1)}, bf16[48,256]{1,0:T(8,128)(2,1)S(1)}, u32[]{:S(2)}, u32[]{:S(2)}) collective-permute-start(bf16[48,256]{1,0:T(8,128)(2,1)} %get-tuple-element.66), channel_id=1, source_target_pairs={{0,1},{1,0},{2,3},{3,2},{4,5},{5,4},{6,7},{7,6},{8,9},{9,8},{10,11... | collective-permute-start | bytes 73736 | tf_op jit(solution)/shard_map/ppermute | solution.py:101
  127.5 0.7 fusion.11
  128.3 1.6 %collective-permute-done.12 = bf16[48,256]{1,0:T(8,128)(2,1)S(1)} collective-permute-done((bf16[48,256]{1,0:T(8,128)(2,1)}, bf16[48,256]{1,0:T(8,128)(2,1)S(1)}, u32[]{:S(2)}, u32[]{:S(2)}) %collective-permute-start.12) | collective-permute-done | bytes 24608 | tf_op jit(solution)/shard_map/ppermute | solution.py:101
  130.1 7.7 %collective-permute-start.13 = (bf16[48,256]{1,0:T(8,128)(2,1)S(1)}, bf16[48,256]{1,0:T(8,128)(2,1)S(1)}, u32[]{:S(2)}, u32[]{:S(2)}) collective-permute-start(bf16[48,256]{1,0:T(8,128)(2,1)S(1)} %concatenate.12), channel_id=1, source_target_pairs={{0,2},{2,4},{4,6},{6,8},{8,10},{10,12},{12,14},{14,16},{16,18},{18... | collective-permute-start | bytes 73736 | tf_op jit(solution)/shard_map/ppermute | solution.py:581
  137.8 1.3 collective-permute-start.14
  139.1 0.5 convert_element_type.20.bias_ref
  139.6 3.9 %collective-permute-done.14.below_ref = bf16[48,256]{1,0:T(8,128)(2,1)S(1)} collective-permute-done((bf16[48,256]{1,0:T(8,128)(2,1)S(1)}, bf16[48,256]{1,0:T(8,128)(2,1)S(1)}, u32[]{:S(2)}, u32[]{:S(2)}) %collective-permute-start.14) | collective-permute-done | bytes 24608 | tf_op jit(solution)/shard_map/ppermute | solution.py:582
  143.5 0.6 copy-done.9
  144.1 8.5 %compose.1 = f32[13,192,192]{2,1,0:T(8,128)} custom-call(bf16[256,256]{1,0:T(8,128)(2,1)} %get-tuple-element.65.own_ref, bf16[48,256]{1,0:T(8,128)(2,1)} %copy-done.6, bf16[48,256]{1,0:T(8,128)(2,1)} %copy-done.5, bf16[48,256]{1,0:T(8,128)(2,1)} %copy-done.8, bf16[48,256]{1,0:T(8,128)(2,1)} %copy-done.9, bf16[2,256]{1,0:T(2,128)(2,1)} %fusion.5.profile_ref, ...), custom_call_target="tpu_custom_call" | custom-call | tf_op jit(solution)/shard_map/compose/pallas_call | solution.py:591
  (58 shorter events, 0.4 us)
Async XLA Ops:
  0.0 32.6 %copy-start = (bf16[16,1280]{1,0:T(8,128)(2,1)S(1)}, bf16[16,1280]{1,0:T(8,128)(2,1)}, u32[]{:S(2)}) copy-start(bf16[16,1280]{1,0:T(8,128)(2,1)} %param.29) | copy-start | bytes 122884
  0.0 19.8 %copy-start.12 = (s32[1,1,1,2,224]{4,3,2,1,0:T(2,128)S(1)}, s32[1,1,1,2,224]{4,3,2,1,0:T(2,128)}, u32[]{:S(2)}) copy-start(s32[1,1,1,2,224]{4,3,2,1,0:T(2,128)} %param.28) | copy-start | bytes 5380
  1.5 1.7 %copy-start.1 = (bf16[1,16,1,1,4,16,1280]{6,5,4,3,2,1,0:T(8,128)(2,1)S(1)}, bf16[1,16,1,1,4,16,1280]{6,5,4,3,2,1,0:T(8,128)(2,1)}, u32[]{:S(2)}) copy-start(bf16[1,16,1,1,4,16,1280]{6,5,4,3,2,1,0:T(8,128)(2,1)} %param.24) | copy-start | bytes 7864324
  3.3 20.8 %copy-start.10 = (bf16[1280]{0:T(1024)(128)(2,1)S(1)}, bf16[1280]{0:T(1024)(128)(2,1)}, u32[]{:S(2)}) copy-start(bf16[1280]{0:T(1024)(128)(2,1)} %param.30) | copy-start | bytes 7684
  3.3 21.4 %copy-start.11 = (bf16[1280]{0:T(1024)(128)(2,1)S(1)}, bf16[1280]{0:T(1024)(128)(2,1)}, u32[]{:S(2)}) copy-start(bf16[1280]{0:T(1024)(128)(2,1)} %param.33) | copy-start | bytes 7684
  3.3 22.0 %copy-start.19 = (bf16[256]{0:T(256)(128)(2,1)S(1)}, bf16[256]{0:T(256)(128)(2,1)}, u32[]{:S(2)}) copy-start(bf16[256]{0:T(256)(128)(2,1)} %param.35) | copy-start | bytes 1540
  11.5 19.9 %copy-start.2 = (bf16[2,64,1280]{2,1,0:T(8,128)(2,1)}, bf16[2,64,1280]{2,1,0:T(8,128)(2,1)S(1)}, u32[]{:S(2)}) copy-start(bf16[2,64,1280]{2,1,0:T(8,128)(2,1)S(1)} %get-tuple-element.45.refs_0_) | copy-start | bytes 983044
  11.6 23.6 %collective-permute-start = (bf16[2,64,1280]{2,1,0:T(8,128)(2,1)S(1)}, bf16[2,64,1280]{2,1,0:T(8,128)(2,1)}, u32[]{:S(2)}, u32[]{:S(2)}) collective-permute-start(bf16[2,64,1280]{2,1,0:T(8,128)(2,1)S(1)} %get-tuple-element.38), channel_id=1, source_target_pairs={{0,8},{8,0},{16,24},{24,16},{1,9},{9,1},{17,25},{25,17},{2,10},{10... | collective-permute-start | bytes 983048 | tf_op jit(solution)/shard_map/ppermute | solution.py:101
  12.1 22.1 %collective-permute-start.1 = (bf16[2,64,1280]{2,1,0:T(8,128)(2,1)S(1)}, bf16[2,64,1280]{2,1,0:T(8,128)(2,1)}, u32[]{:S(2)}, u32[]{:S(2)}) collective-permute-start(bf16[2,64,1280]{2,1,0:T(8,128)(2,1)S(1)} %get-tuple-element.39), channel_id=1, source_target_pairs={{0,16},{8,24},{16,0},{24,8},{1,17},{9,25},{17,1},{25,9},{2,18},{10... | collective-permute-start | bytes 983048 | tf_op jit(solution)/shard_map/ppermute | solution.py:101
  14.6 18.6 %collective-permute-start.2 = (bf16[2,64,1280]{2,1,0:T(8,128)(2,1)S(1)}, bf16[2,64,1280]{2,1,0:T(8,128)(2,1)}, u32[]{:S(2)}, u32[]{:S(2)}) collective-permute-start(bf16[2,64,1280]{2,1,0:T(8,128)(2,1)S(1)} %get-tuple-element.40), channel_id=1, source_target_pairs={{0,24},{8,16},{16,8},{24,0},{1,25},{9,17},{17,9},{25,1},{2,26},{10... | collective-permute-start | bytes 983048 | tf_op jit(solution)/shard_map/ppermute | solution.py:101
  14.7 31.0 %collective-permute-start.3 = (bf16[4,64,1280]{2,1,0:T(8,128)(2,1)S(1)}, bf16[4,64,1280]{2,1,0:T(8,128)(2,1)S(1)}, u32[]{:S(2)}, u32[]{:S(2)}) collective-permute-start(bf16[4,64,1280]{2,1,0:T(8,128)(2,1)S(1)} %get-tuple-element.41), channel_id=1, source_target_pairs={{0,2},{2,0},{4,6},{6,4},{1,3},{3,1},{5,7},{7,5},{8,10},{10,8},{12,... | collective-permute-start | bytes 1966088 | tf_op jit(solution)/shard_map/ppermute | solution.py:101
  16.5 31.8 %collective-permute-start.7 = (bf16[4,64,1280]{2,1,0:T(8,128)(2,1)S(1)}, bf16[4,64,1280]{2,1,0:T(8,128)(2,1)}, u32[]{:S(2)}, u32[]{:S(2)}) collective-permute-start(bf16[4,64,1280]{2,1,0:T(8,128)(2,1)S(1)} %get-tuple-element.42), channel_id=1, source_target_pairs={{0,4},{2,6},{4,0},{6,2},{1,5},{3,7},{5,1},{7,3},{8,12},{10,14},{12... | collective-permute-start | bytes 1966088 | tf_op jit(solution)/shard_map/ppermute | solution.py:101
  45.7 16.8 %copy-start.4 = (bf16[4,64,1280]{2,1,0:T(8,128)(2,1)}, bf16[4,64,1280]{2,1,0:T(8,128)(2,1)S(1)}, u32[]{:S(2)}) copy-start(bf16[4,64,1280]{2,1,0:T(8,128)(2,1)S(1)} %collective-permute-done.3.refs_4_) | copy-start | bytes 1966084
  45.7 5.3 %collective-permute-start.4 = (bf16[1,64,1280]{2,1,0:T(8,128)(2,1)S(1)}, bf16[1,64,1280]{2,1,0:T(8,128)(2,1)S(1)}, u32[]{:S(2)}, u32[]{:S(2)}) collective-permute-start(bf16[1,64,1280]{2,1,0:T(8,128)(2,1)S(1)} %get-tuple-element.74), channel_id=1, source_target_pairs={{0,8},{8,0},{16,24},{24,16},{1,9},{9,1},{17,25},{25,17},{2,10},{10... | collective-permute-start | bytes 491528 | tf_op jit(solution)/shard_map/ppermute | solution.py:101
  45.8 7.1 %collective-permute-start.5 = (bf16[1,64,1280]{2,1,0:T(8,128)(2,1)S(1)}, bf16[1,64,1280]{2,1,0:T(8,128)(2,1)S(1)}, u32[]{:S(2)}, u32[]{:S(2)}) collective-permute-start(bf16[1,64,1280]{2,1,0:T(8,128)(2,1)S(1)} %get-tuple-element.73), channel_id=1, source_target_pairs={{0,16},{8,24},{16,0},{24,8},{1,17},{9,25},{17,1},{25,9},{2,18},{10... | collective-permute-start | bytes 491528 | tf_op jit(solution)/shard_map/ppermute | solution.py:101
  47.5 8.0 %collective-permute-start.6 = (bf16[1,64,1280]{2,1,0:T(8,128)(2,1)S(1)}, bf16[1,64,1280]{2,1,0:T(8,128)(2,1)S(1)}, u32[]{:S(2)}, u32[]{:S(2)}) collective-permute-start(bf16[1,64,1280]{2,1,0:T(8,128)(2,1)S(1)} %get-tuple-element.72), channel_id=1, source_target_pairs={{0,24},{8,16},{16,8},{24,0},{1,25},{9,17},{17,9},{25,1},{2,26},{10... | collective-permute-start | bytes 491528 | tf_op jit(solution)/shard_map/ppermute | solution.py:101
  49.4 6.1 %collective-permute-start.8 = (bf16[1,64,1280]{2,1,0:T(8,128)(2,1)S(1)}, bf16[1,64,1280]{2,1,0:T(8,128)(2,1)S(1)}, u32[]{:S(2)}, u32[]{:S(2)}) collective-permute-start(bf16[1,64,1280]{2,1,0:T(8,128)(2,1)S(1)} %get-tuple-element.71), channel_id=1, source_target_pairs={{0,8},{8,0},{16,24},{24,16},{1,9},{9,1},{17,25},{25,17},{2,10},{10... | collective-permute-start | bytes 491528 | tf_op jit(solution)/shard_map/ppermute | solution.py:101
  49.5 10.4 %collective-permute-start.9 = (bf16[1,64,1280]{2,1,0:T(8,128)(2,1)S(1)}, bf16[1,64,1280]{2,1,0:T(8,128)(2,1)S(1)}, u32[]{:S(2)}, u32[]{:S(2)}) collective-permute-start(bf16[1,64,1280]{2,1,0:T(8,128)(2,1)S(1)} %get-tuple-element.70), channel_id=1, source_target_pairs={{0,16},{8,24},{16,0},{24,8},{1,17},{9,25},{17,1},{25,9},{2,18},{10... | collective-permute-start | bytes 491528 | tf_op jit(solution)/shard_map/ppermute | solution.py:101
  51.1 11.4 %copy-start.13 = (bf16[1,64,1280]{2,1,0:T(8,128)(2,1)}, bf16[1,64,1280]{2,1,0:T(8,128)(2,1)S(1)}, u32[]{:S(2)}) copy-start(bf16[1,64,1280]{2,1,0:T(8,128)(2,1)S(1)} %collective-permute-done.4.refs_5_) | copy-start | bytes 491524
  51.1 11.4 %collective-permute-start.10 = (bf16[1,64,1280]{2,1,0:T(8,128)(2,1)S(1)}, bf16[1,64,1280]{2,1,0:T(8,128)(2,1)S(1)}, u32[]{:S(2)}, u32[]{:S(2)}) collective-permute-start(bf16[1,64,1280]{2,1,0:T(8,128)(2,1)S(1)} %get-tuple-element.69), channel_id=1, source_target_pairs={{0,24},{8,16},{16,8},{24,0},{1,25},{9,17},{17,9},{25,1},{2,26},{10... | collective-permute-start | bytes 491528 | tf_op jit(solution)/shard_map/ppermute | solution.py:101
  52.9 9.6 %copy-start.14 = (bf16[1,64,1280]{2,1,0:T(8,128)(2,1)}, bf16[1,64,1280]{2,1,0:T(8,128)(2,1)S(1)}, u32[]{:S(2)}) copy-start(bf16[1,64,1280]{2,1,0:T(8,128)(2,1)S(1)} %collective-permute-done.5.refs_6_) | copy-start | bytes 491524
  52.9 24.4 %collective-permute-start.11 = (bf16[4,64,1280]{2,1,0:T(8,128)(2,1)S(1)}, bf16[4,64,1280]{2,1,0:T(8,128)(2,1)S(1)}, u32[]{:S(2)}, u32[]{:S(2)}) collective-permute-start(bf16[4,64,1280]{2,1,0:T(8,128)(2,1)S(1)} %pad_maximum_fusion), channel_id=1, source_target_pairs={{0,6},{2,4},{4,2},{6,0},{1,7},{3,5},{5,3},{7,1},{8,14},{10,12},{12... | collective-permute-start | bytes 1966088 | tf_op jit(solution)/shard_map/ppermute | solution.py:101
  55.6 7.0 %copy-start.15 = (bf16[1,64,1280]{2,1,0:T(8,128)(2,1)}, bf16[1,64,1280]{2,1,0:T(8,128)(2,1)S(1)}, u32[]{:S(2)}) copy-start(bf16[1,64,1280]{2,1,0:T(8,128)(2,1)S(1)} %collective-permute-done.6.refs_7_) | copy-start | bytes 491524
  55.6 7.0 %copy-start.16 = (bf16[1,64,1280]{2,1,0:T(8,128)(2,1)}, bf16[1,64,1280]{2,1,0:T(8,128)(2,1)S(1)}, u32[]{:S(2)}) copy-start(bf16[1,64,1280]{2,1,0:T(8,128)(2,1)S(1)} %collective-permute-done.8.refs_9_) | copy-start | bytes 491524
  59.9 2.6 %copy-start.17 = (bf16[1,64,1280]{2,1,0:T(8,128)(2,1)}, bf16[1,64,1280]{2,1,0:T(8,128)(2,1)S(1)}, u32[]{:S(2)}) copy-start(bf16[1,64,1280]{2,1,0:T(8,128)(2,1)S(1)} %collective-permute-done.9.refs_10_) | copy-start | bytes 491524
  62.5 0.7 copy-start.18
  77.3 0.9 copy-start.3
  115.0 15.0 %copy-start.7 = (bf16[2,256]{1,0:T(2,128)(2,1)S(1)}, bf16[2,256]{1,0:T(2,128)(2,1)}, u32[]{:S(2)}) copy-start(bf16[2,256]{1,0:T(2,128)(2,1)} %fusion.5.profile_ref) | copy-start | bytes 3076
  115.0 24.0 %copy-start.20 = (bf16[13]{0:T(256)(128)(2,1)S(1)}, bf16[13]{0:T(256)(128)(2,1)}, u32[]{:S(2)}) copy-start(bf16[13]{0:T(256)(128)(2,1)} %param.38) | copy-start | bytes 82
  125.9 4.0 %collective-permute-start.12 = (bf16[48,256]{1,0:T(8,128)(2,1)}, bf16[48,256]{1,0:T(8,128)(2,1)S(1)}, u32[]{:S(2)}, u32[]{:S(2)}) collective-permute-start(bf16[48,256]{1,0:T(8,128)(2,1)} %get-tuple-element.66), channel_id=1, source_target_pairs={{0,1},{1,0},{2,3},{3,2},{4,5},{5,4},{6,7},{7,6},{8,9},{9,8},{10,11... | collective-permute-start | bytes 73736 | tf_op jit(solution)/shard_map/ppermute | solution.py:101
  129.9 13.6 %copy-start.5 = (bf16[48,256]{1,0:T(8,128)(2,1)}, bf16[48,256]{1,0:T(8,128)(2,1)S(1)}, u32[]{:S(2)}) copy-start(bf16[48,256]{1,0:T(8,128)(2,1)S(1)} %get-tuple-element.93.after_ref) | copy-start | bytes 73732
  129.9 13.6 %copy-start.6 = (bf16[48,256]{1,0:T(8,128)(2,1)}, bf16[48,256]{1,0:T(8,128)(2,1)S(1)}, u32[]{:S(2)}) copy-start(bf16[48,256]{1,0:T(8,128)(2,1)S(1)} %get-tuple-element.94.before_ref) | copy-start | bytes 73732
  130.1 9.5 %collective-permute-start.13 = (bf16[48,256]{1,0:T(8,128)(2,1)S(1)}, bf16[48,256]{1,0:T(8,128)(2,1)S(1)}, u32[]{:S(2)}, u32[]{:S(2)}) collective-permute-start(bf16[48,256]{1,0:T(8,128)(2,1)S(1)} %concatenate.12), channel_id=1, source_target_pairs={{0,2},{2,4},{4,6},{6,8},{8,10},{10,12},{12,14},{14,16},{16,18},{18... | collective-permute-start | bytes 73736 | tf_op jit(solution)/shard_map/ppermute | solution.py:581
  137.8 5.7 %collective-permute-start.14 = (bf16[48,256]{1,0:T(8,128)(2,1)S(1)}, bf16[48,256]{1,0:T(8,128)(2,1)S(1)}, u32[]{:S(2)}, u32[]{:S(2)}) collective-permute-start(bf16[48,256]{1,0:T(8,128)(2,1)S(1)} %concatenate.13), channel_id=1, source_target_pairs={{2,0},{4,2},{6,4},{8,6},{10,8},{12,10},{14,12},{16,14},{18,16},{20... | collective-permute-start | bytes 73736 | tf_op jit(solution)/shard_map/ppermute | solution.py:582
  139.6 3.9 %copy-start.8 = (bf16[48,256]{1,0:T(8,128)(2,1)}, bf16[48,256]{1,0:T(8,128)(2,1)S(1)}, u32[]{:S(2)}) copy-start(bf16[48,256]{1,0:T(8,128)(2,1)S(1)} %collective-permute-done.13.above_ref) | copy-start | bytes 73732
  143.5 0.6 copy-start.9

commit v3 on v2

--- a/solution.py
+++ b/solution.py
@@ -50,263 +50,260 @@
 
 
 def gather_kernel(routes, index_ref, a_ref, *refs):
-    outs, (held, in_sems, out_sems) = refs[:-3], refs[-3:]
-    loads = [pltpu.make_async_copy(a_ref.at[index_ref[n]], held.at[n], in_sems.at[n]) for n in range(len(routes))]
-    for load in loads:
-        load.start()
-    stores = []
+    outs, sems = refs[:-1], refs[-1]
+    copies = []
     for n, (out, spot) in enumerate(routes):
-        loads[n].wait()
-        stores.append(pltpu.make_async_copy(held.at[n], outs[out].at[spot], out_sems.at[n]))
-        stores[n].start()
-    for store in stores:
-        store.wait()
-
-
-def gather_pieces(arrivals, owner_map, early, late, dates):
+        copies.append(pltpu.make_async_copy(a_ref.at[index_ref[n]], outs[out].at[spot], sems.at[n]))
+    for copy in copies:
+        copy.start()
+    for copy in copies:
+        copy.wait()
+
+
+def gather_pieces(arrivals, owner_map, rings, together, dates):
     slots, strip, width = arrivals.shape
     tiles = slots // dates
     date, tile = lax.axis_index("date"), lax.axis_index("tile")
-    together = [0] + late
     routes, order = [], []
-    for s in range(tiles):
+    for s in rings + together:
         for m in range(dates):
             order.append((s, m))
-            routes.append((early.index(s) - 1, m) if s in early[1:] else (len(early) - 1 + m, together.index(s)))
+            routes.append((rings.index(s), m) if s in rings else (len(rings) + m, together.index(s)))
     s_of = jnp.array([s for s, _ in order], jnp.int32)
     m_of = jnp.array([m for _, m in order], jnp.int32)
     wanted = (date ^ m_of) * tiles + (tile ^ s_of)
     spots = jnp.arange(slots, dtype=jnp.int32)[None, :]
     index = jnp.sum(jnp.where(owner_map[None, :] == wanted[:, None], spots, 0), axis=1)
-    shapes = [jax.ShapeDtypeStruct((dates, strip, width), bf16)] * (len(early) - 1)
+    shapes = [jax.ShapeDtypeStruct((dates, strip, width), bf16)] * len(rings)
     shapes += [jax.ShapeDtypeStruct((len(together), strip, width), bf16)] * dates
     anywhere = pl.BlockSpec(memory_space=pl.ANY)
     outs = pl.pallas_call(
         functools.partial(gather_kernel, routes),
-        in_specs=[pl.BlockSpec(memory_space=pltpu.SMEM), anywhere],
+        in_specs=[pl.BlockSpec(memory_space=pltpu.SMEM), pl.BlockSpec(memory_space=pltpu.VMEM)],
         out_specs=[anywhere] * len(shapes),
         out_shape=shapes,
-        scratch_shapes=[
-            pltpu.VMEM(arrivals.shape, bf16),
-            pltpu.SemaphoreType.DMA((slots,)),
-            pltpu.SemaphoreType.DMA((slots,)),
-        ],
-        compiler_params=pltpu.CompilerParams(vmem_limit_bytes=16 * 2**20),
+        scratch_shapes=[pltpu.SemaphoreType.DMA((len(routes),))],
+        compiler_params=pltpu.CompilerParams(vmem_limit_bytes=4 * 2**20),
+        cost_estimate=pl.CostEstimate(flops=0, bytes_accessed=0, transcendentals=0),
         name="gather_pieces",
     )(index, arrivals)
-    return outs[: len(early) - 1], outs[len(early) - 1 :]
+    return outs[: len(rings)], outs[len(rings) :]
 
 
 def swap(value, axis, mask):
     return lax.ppermute(value, axis, [(i, i ^ mask) for i in range(lax.axis_size(axis))])
 
 
-def exchange(arrivals, owner_map):
+def exchange(arrivals, owner_map, prepare, use):
     dates, tiles = lax.axis_size("date"), lax.axis_size("tile")
-    late = list(range(tiles - max(1, tiles // 4), tiles))
-    early = list(range(tiles - len(late)))
-    rings, mixed = gather_pieces(arrivals, owner_map, early, late, dates)
-    rings = [swap(ring, "tile", s) for s, ring in zip(early[1:], rings)]
+    half, late = tiles // 2, tiles - max(1, tiles // 4)
+    rings, mixed = gather_pieces(arrivals, owner_map, list(range(1, late)), list(range(late, tiles)), dates)
+    rings = [swap(ring, "tile", s) for s, ring in enumerate(rings, 1)]
     mixed = [value if m == 0 else swap(value, "date", m) for m, value in enumerate(mixed)]
-    last = []
-    for i, s in enumerate(late):
-        pieces = jnp.stack([value[1 + i] for value in mixed])
-        last.append(swap(pieces, "tile", s))
-    first = [(value, 0) for value in mixed]
-    for ring in rings:
-        first += [(ring, 0) if m == 0 else (swap(ring[m : m + 1], "date", m), 0) for m in range(dates)]
-    return first, [(value, m) for value in last for m in range(dates)]
-
-
-def project_kernel(pieces, *refs):
-    x_refs, (loc_ref, gain_ref, w_ref, o_ref, norm_ref, x_out, normed_ref) = refs[:pieces], refs[pieces:]
-    step = pl.program_id(0)
-
-    @pl.when(step == 0)
-    def _():
-        first = 0
-        for x_ref in x_refs:
-            for row in range(0, x_ref.shape[0], 64):
-                x = x_ref[row : row + 64, :]
-                x_out[first : first + x.shape[0], :] = x
-                residual = x.astype(f32) + loc_ref[...]
-                normed = layer_norm(residual, gain_ref[...].astype(f32))
-                normed_ref[first : first + x.shape[0], :] = normed.astype(bf16)
-                first += x.shape[0]
-
-    packed = mm(w_ref[...], normed_ref[...], (((0,), (1,)), ((), ())))
-    packed = packed.astype(bf16)
-    o_ref[...] = packed
-    packed = packed.astype(f32)
-    heads = norm_ref.shape[0]
-    squares = jnp.sum((packed * packed).reshape(heads, packed.shape[0] // heads, packed.shape[1]), axis=1)
-    norm_ref[...] = jnp.broadcast_to(jnp.max(squares, axis=1, keepdims=True), norm_ref.shape)
+    stacked = [jnp.stack([value[i] for value in mixed]) for i in range(tiles - late)]
+    arrivals, stacked = lax.optimization_barrier((arrivals, stacked))
+    last = [(swap(pieces, "tile", late + i), None) for i, pieces in enumerate(stacked)]
+    _, own = gather_pieces(arrivals, owner_map, [], [0], dates)
+    own = [value if m == 0 else swap(value, "date", m) for m, value in enumerate(own)]
+    prepared = prepare(stacked)
+    close, far = rings[: half - 1], rings[half - 1 :]
+    close, prepared = lax.optimization_barrier((close, prepared))
+
+    def cross_dates(ring):
+        return [(ring if m == 0 else swap(ring[m : m + 1], "date", m), 0) for m in range(dates)]
+
+    near = [(value, 0) for value in own]
+    for ring in close:
+        near += cross_dates(ring)
+    arrays, far = lax.optimization_barrier(([array for array, _ in near], far))
+    near = [(array, n) for array, (_, n) in zip(arrays, near)]
+    for ring in far:
+        last += cross_dates(ring)
+    return use(near, prepared), last, prepared
+
+
+def with_ones(values):
+    return jnp.concatenate([values, jnp.ones((SUM_ROWS, values.shape[1]), bf16)], axis=0)
+
+
+def normalize(x, loc_ref, gain_ref):
+    return layer_norm(x.astype(f32) + loc_ref[...], gain_ref[...].astype(f32)).astype(bf16)
+
+
+def project_block(weight_ref, normed, packed_ref, norm_ref):
+    width = weight_ref.shape[0]
+    block = width // 2
+    heads = HEADS // 2
+    for first in range(0, weight_ref.shape[1], block):
+        packed = mm(weight_ref[:, first : first + block], normed, (((0,), (1,)), ((), ()))).astype(bf16)
+        packed_ref[first : first + block, :] = packed
+        if first < 2 * width:
+            packed = packed.astype(f32)
+            squares = jnp.sum((packed * packed).reshape(heads, block // heads, packed.shape[1]), axis=1)
+            largest = jnp.max(squares, axis=1, keepdims=True)
+            row = first // block * heads
+            norm_ref[row : row + heads, :] = jnp.broadcast_to(largest, (heads, norm_ref.shape[1]))
+
+
+def project_kernel(places, *refs):
+    count = len(places)
+    piece_refs, (loc_ref, gain_ref, weight_ref, packed_ref, norm_ref, x_ref, normed_ref) = refs[:count], refs[count:]
+    first = 0
+    for piece_ref, place in zip(piece_refs, places):
+        x = piece_ref[place]
+        x_ref[first : first + x.shape[0], :] = x
+        normed_ref[first : first + x.shape[0], :] = normalize(x, loc_ref, gain_ref)
+        first += x.shape[0]
+    project_block(weight_ref, normed_ref[...], packed_ref, norm_ref)
 
 
 def project(pieces, location, gain, weight):
     width = weight.shape[0]
     tokens = sum(piece.shape[1] for piece, _ in pieces)
-    block = width // 2
-    steps = weight.shape[1] // block
-    row = pl.BlockSpec((1, width), lambda i: (0, 0))
+    whole = pl.BlockSpec(memory_space=pltpu.VMEM)
+    specs = [pl.BlockSpec((1,) + piece.shape[1:], lambda i: (0, 0, 0)) for piece, _ in pieces]
     return pl.pallas_call(
-        functools.partial(project_kernel, len(pieces)),
-        grid=(steps,),
-        in_specs=[pl.BlockSpec((None,) + piece.shape[1:], lambda i, n=n: (n, 0, 0)) for piece, n in pieces]
-        + [row, row, pl.BlockSpec((width, block), lambda i: (0, i))],
-        out_specs=[
-            pl.BlockSpec((block, tokens), lambda i: (i, 0)),
-            pl.BlockSpec((3 * HEADS // steps, 128), lambda i: (i, 0)),
-            pl.BlockSpec((tokens, width), lambda i: (0, 0)),
-        ],
+        functools.partial(project_kernel, [n for _, n in pieces]),
+        grid=(1,),
+        in_specs=specs + [whole] * 3,
+        out_specs=[whole] * 3,
         out_shape=[
             jax.ShapeDtypeStruct((weight.shape[1], tokens), bf16),
-            jax.ShapeDtypeStruct((3 * HEADS, 128), f32),
+            jax.ShapeDtypeStruct((2 * HEADS, 128), f32),
             jax.ShapeDtypeStruct((tokens, width), bf16),
         ],
         scratch_shapes=[pltpu.VMEM((tokens, width), bf16)],
-        compiler_params=pltpu.CompilerParams(vmem_limit_bytes=VMEM),
-        cost_estimate=pl.CostEstimate(
-            flops=2 * tokens * width * weight.shape[1], bytes_accessed=weight.size * 2, transcendentals=0
-        ),
+        compiler_params=pltpu.CompilerParams(vmem_limit_bytes=16 * 2**20),
+        cost_estimate=pl.CostEstimate(flops=0, bytes_accessed=0, transcendentals=0),
         name="project",
     )(*[piece for piece, _ in pieces], location, gain, weight)
 
 
-def with_ones(values):
-    return jnp.concatenate([values, jnp.ones((SUM_ROWS, values.shape[1]), bf16)], axis=0)
-
-
-def attend_kernel(parts, *refs):
-    q_refs, k_refs, v_refs, norm_refs = (refs[i * parts : (i + 1) * parts] for i in range(4))
-    o_ref, flag_ref = refs[4 * parts :]
-    head = o_ref.shape[0] // PAIR
+def encode_kernel(places, order, place_ref, packed_ref, norm_ref, x_ref, *refs):
+    count = len(places)
+    piece_refs, refs = refs[:count], refs[count:]
+    (
+        loc_ref, gain_ref, weight_ref, out_ref, final_ref, wr_ref, bias_ref, profile_ref,
+        o_ref, last_ref, first_ref, tail_ref, normed_ref, rest_ref, rest_norm_ref, mixed_ref, encoded_ref, reduced_ref
+    ) = refs
+    first = 0
+    for piece_ref, n in zip(piece_refs, places):
+        x = piece_ref[...].reshape(-1, piece_ref.shape[-1]) if n is None else piece_ref[0]
+        tail_ref[first : first + x.shape[0], :] = x
+        normed_ref[first : first + x.shape[0], :] = normalize(x, loc_ref, gain_ref)
+        first += x.shape[0]
+    width = weight_ref.shape[0]
+    head = width // HEADS
     scale = math.log2(math.e) / math.sqrt(head)
-
-    @pl.when(pl.program_id(0) == 0)
-    def _():
-        norms = norm_refs[0][...]
-        for norm_ref in norm_refs[1:]:
-            norms = jnp.maximum(norms, norm_ref[...])
-        flag_ref[0] = jnp.max(norms[:HEADS] * norms[HEADS : 2 * HEADS])
-
-    small = flag_ref[0] <= (EXPONENT_BOUND / scale) ** 2
-
-    def rows(n):
-        return slice(n * head, (n + 1) * head)
-
-    def side_by_side(part_refs, n):
-        return jnp.concatenate([ref[rows(n), :] for ref in part_refs], axis=1)
+    project_block(weight_ref, normed_ref[...], rest_ref, rest_norm_ref)
+    packed_refs = (packed_ref, rest_ref)
+    norms = jnp.maximum(norm_ref[...], rest_norm_ref[...])
+    small = jnp.max(norms[:HEADS] * norms[HEADS:]) <= (EXPONENT_BOUND / scale) ** 2
+
+    def side_by_side(which, n):
+        rows = pl.ds(pl.multiple_of(which * width + n * head, 16), head)
+        return jnp.concatenate([ref[rows, :] for ref in packed_refs], axis=1)
 
     def scores(n):
-        return mm(side_by_side(k_refs, n), side_by_side(q_refs, n), TN)
+        return mm(side_by_side(1, n), side_by_side(0, n), TN)
 
     def finish(n, lifted):
-        sums = mm(with_ones(side_by_side(v_refs, n)), lifted.astype(bf16))
-        o_ref[rows(n), :] = (sums[:head] * (1.0 / sums[head : head + 1])).astype(bf16)
+        sums = mm(with_ones(side_by_side(2, n)), lifted.astype(bf16))
+        rows = pl.ds(pl.multiple_of(n * head, 16), head)
+        mixed_ref[rows, :] = (sums[:head] * (1.0 / sums[head : head + 1])).astype(bf16)
 
     @pl.when(small)
     def _():
-        for n in range(PAIR):
-            finish(n, jnp.exp2(scores(n) * scale))
+        def heads(pair, carry):
+            for n in range(PAIR):
+                finish(pair * PAIR + n, jnp.exp2(scores(pair * PAIR + n) * scale))
+            return carry
+
+        lax.fori_loop(0, HEADS // PAIR, heads, 0)
 
     @pl.when(jnp.logical_not(small))
     def _():
-        for n in range(PAIR):
+        def heads(n, carry):
             held = scores(n)
             finish(n, jnp.exp2((held - jnp.max(held, axis=0, keepdims=True)) * scale))
-
-
-def attend(packed, norms):
-    head = packed[0].shape[0] // (3 * HEADS)
-    tokens = sum(part.shape[1] for part in packed)
-    steps = HEADS // PAIR
-    specs = []
-    for p in range(3):
-        for part in packed:
-            specs.append(pl.BlockSpec((PAIR * head, part.shape[1]), lambda h, p=p: (h + p * steps, 0)))
-    specs += [pl.BlockSpec(norm.shape, lambda h: (0, 0)) for norm in norms]
-    return pl.pallas_call(
-        functools.partial(attend_kernel, len(packed)),
-        grid=(steps,),
-        in_specs=specs,
-        out_specs=pl.BlockSpec((PAIR * head, tokens), lambda h: (h, 0)),
-        out_shape=jax.ShapeDtypeStruct((HEADS * head, tokens), bf16),
-        scratch_shapes=[pltpu.SMEM((1,), f32)],
-        compiler_params=pltpu.CompilerParams(vmem_limit_bytes=VMEM),
-        name="attend",
-    )(*(list(packed) * 3), *norms)
-
-
-def reduce_kernel(
-    place_ref, m_ref, w_ref, x0_ref, x1_ref, loc_ref, gain_ref, wr_ref, bias_ref, profile_ref,
-    o_ref, last_ref, first_ref, encoded_ref, reduced_ref
+            return carry
+
+        lax.fori_loop(0, HEADS, heads, 0)
+
+    tiles, dates, strip, _ = encoded_ref.shape
+    first = 0
+    step = tiles * dates * strip // 4
+    for held_ref in (x_ref, tail_ref):
+        for row in range(0, held_ref.shape[0], step):
+            held = held_ref[row : row + step, :].astype(f32) + loc_ref[...]
+            updated = held + mm(mixed_ref[:, first : first + step], out_ref[...], TN)
+            encoded = layer_norm(updated, final_ref[...].astype(f32)).astype(bf16)
+            part = step // (dates * strip)
+            group = first // (dates * strip)
+            encoded_ref[group : group + part] = encoded.reshape(part, dates, strip, width)
+            first += step
+    total = bias_ref[...].astype(f32)
+    for m in range(dates):
+        total = total + mm(encoded_ref[:, m].reshape(tiles * strip, width), wr_ref[place_ref[0] ^ m])
+    total = 0.5 * total * (1.0 + lax.erf(total * math.sqrt(0.5)))
+    halves = range(reduced_ref.shape[0])
+    for n, s in enumerate(order):
+        spot = pl.multiple_of((place_ref[1] ^ s) * strip, strip)
+        for half in halves:
+            lanes = slice(128 * half, 128 * (half + 1))
+            reduced_ref[half, pl.ds(spot, strip), :] = total[n * strip : (n + 1) * strip, lanes]
+    for half in halves:
+        o_ref[:, 128 * half : 128 * (half + 1)] = reduced_ref[half].astype(bf16)
+
+    def column(b):
+        return jnp.concatenate([reduced_ref[half, pl.ds(b, PATCHES, stride=PATCHES), :] for half in halves], axis=1)
+
+    tail = jnp.zeros((PATCHES - 2, o_ref.shape[1]), f32)
+    tail = jnp.concatenate([profile_ref[...].astype(f32), tail], axis=0)
+    is_last = place_ref[2] == 1
+    sent = [jnp.where(is_last, column(PATCHES - 2 + i), column(i)) for i in range(2)]
+    last_ref[...] = jnp.concatenate(sent + [tail], axis=0).astype(bf16)
+    first_ref[...] = jnp.concatenate([column(0), column(1), tail], axis=0).astype(bf16)
+
+
+def encode(
+    place, packed, norms, x, last, location, gain, weight, out_weight, final_gain, reduce_weight, reduce_bias, profile,
+    tiles, dates
 ):
-    step = pl.program_id(0)
-    steps = pl.num_programs(0)
-    tiles, dates, strip, width = encoded_ref.shape
-    held = jnp.where(step < steps - 1, x0_ref[...].astype(f32), x1_ref[...].astype(f32))
-    updated = held + loc_ref[...] + mm(m_ref[...], w_ref[...], TN)
-    encoded = layer_norm(updated, gain_ref[...].astype(f32)).astype(bf16)
-    part = tiles // steps
-    encoded_ref[pl.ds(step * part, part)] = encoded.reshape(part, dates, strip, width)
-
-    @pl.when(step == steps - 1)
-    def _():
-        total = bias_ref[...].astype(f32)
-        for m in range(dates):
-            total = total + mm(encoded_ref[:, m].reshape(tiles * strip, width), wr_ref[place_ref[0] ^ m])
-        total = 0.5 * total * (1.0 + lax.erf(total * math.sqrt(0.5)))
-        for s in range(tiles):
-            spot = pl.multiple_of((place_ref[1] ^ s) * strip, strip)
-            for half in range(reduced_ref.shape[0]):
-                lanes = slice(128 * half, 128 * (half + 1))
-                reduced_ref[half, pl.ds(spot, strip), :] = total[s * strip : (s + 1) * strip, lanes]
-        for half in range(reduced_ref.shape[0]):
-            o_ref[:, 128 * half : 128 * (half + 1)] = reduced_ref[half].astype(bf16)
-
-        def column(b):
-            halves = [reduced_ref[half, pl.ds(b, PATCHES, stride=PATCHES), :] for half in range(reduced_ref.shape[0])]
-            return jnp.concatenate(halves, axis=1)
-
-        tail = jnp.zeros((PATCHES - 2, o_ref.shape[1]), f32)
-        tail = jnp.concatenate([profile_ref[...].astype(f32), tail], axis=0)
-        last = place_ref[2] == 1
-        sent = [jnp.where(last, column(PATCHES - 2 + i), column(i)) for i in range(2)]
-        last_ref[...] = jnp.concatenate(sent + [tail], axis=0).astype(bf16)
-        first_ref[...] = jnp.concatenate([column(0), column(1), tail], axis=0).astype(bf16)
-
-
-def reduce_dates(place, mixed, out_weight, x0, x1, location, gain, reduce_weight, reduce_bias, profile, tiles, dates):
-    width, tokens = mixed.shape
+    width = weight.shape[0]
+    tokens = 2 * x.shape[0]
+    rest = tokens - x.shape[0]
     strip = tokens // (tiles * dates)
     dec = reduce_weight.shape[1]
-    steps = tokens // GROUP
-    row = pl.BlockSpec((1, width), lambda t: (0, 0))
+    patches = tiles * strip
+    quarter = tiles // 4
+    order = list(range(2 * quarter)) + list(range(3 * quarter, tiles)) + list(range(2 * quarter, 3 * quarter))
     sent = jax.ShapeDtypeStruct((3 * PATCHES, dec), bf16)
-    sent_spec = pl.BlockSpec((3 * PATCHES, dec), lambda t: (0, 0))
-    patches = tiles * strip
+    whole = pl.BlockSpec(memory_space=pltpu.VMEM)
+    pieces = [
+        pl.BlockSpec(piece.shape if n is None else (1,) + piece.shape[1:], lambda i: (0, 0, 0)) for piece, n in last
+    ]
     return pl.pallas_call(
-        reduce_kernel,
-        grid=(steps,),
-        in_specs=[
-            pl.BlockSpec(memory_space=pltpu.SMEM),
-            pl.BlockSpec((width, GROUP), lambda t: (0, t)),
-            pl.BlockSpec((width, width), lambda t: (0, 0)),
-            pl.BlockSpec((GROUP, width), lambda t: (jnp.minimum(t, steps - 2), 0)),
-            pl.BlockSpec((GROUP, width), lambda t: (0, 0)),
-            row,
-            row,
-            pl.BlockSpec((dates, width, dec), lambda t: (0, 0, 0)),
-            pl.BlockSpec((1, dec), lambda t: (0, 0)),
-            pl.BlockSpec((2, dec), lambda t: (0, 0)),
+        functools.partial(encode_kernel, [n for _, n in last], order),
+        grid=(1,),
+        in_specs=[pl.BlockSpec(memory_space=pltpu.SMEM)] + [whole] * 3 + pieces + [whole] * 8,
+        out_specs=[whole] * 3,
+        out_shape=[jax.ShapeDtypeStruct((patches, dec), bf16), sent, sent],
+        scratch_shapes=[
+            pltpu.VMEM((rest, width), bf16),
+            pltpu.VMEM((rest, width), bf16),
+            pltpu.VMEM((3 * width, rest), bf16),
+            pltpu.VMEM((2 * HEADS, 128), f32),
+            pltpu.VMEM((width, tokens), bf16),
+            pltpu.VMEM((tiles, dates, strip, width), bf16),
+            pltpu.VMEM((dec // 128, patches, 128), f32),
         ],
-        out_specs=[pl.BlockSpec((patches, dec), lambda t: (0, 0)), sent_spec, sent_spec],
-        out_shape=[jax.ShapeDtypeStruct((patches, dec), bf16), sent, sent],
-        scratch_shapes=[pltpu.VMEM((tiles, dates, strip, width), bf16), pltpu.VMEM((dec // 128, patches, 128), f32)],
-        compiler_params=pltpu.CompilerParams(vmem_limit_bytes=VMEM),
-        name="reduce_dates",
-    )(place, mixed, out_weight, x0, x1, location, gain, reduce_weight.reshape(dates, width, dec), reduce_bias, profile)
+        compiler_params=pltpu.CompilerParams(vmem_limit_bytes=36 * 2**20),
+        name="encode",
+    )(
+        place, packed, norms, x, *[piece for piece, _ in last], location, gain, weight, out_weight, final_gain,
+        reduce_weight.reshape(dates, width, dec), reduce_bias, profile,
+    )
 
 
 FIRST_OWN = RIM // PATCH
@@ -439,6 +436,7 @@
             pltpu.VMEM((PATCH, FEAT * PATCH, channels), bf16),
         ],
         compiler_params=pltpu.CompilerParams(vmem_limit_bytes=VMEM),
+        cost_estimate=pl.CostEstimate(flops=0, bytes_accessed=0, transcendentals=0),
         name="decoder_kernels",
     )(upsample_weight, class_weight, *tables)
 
@@ -626,26 +624,27 @@
     slots = arrivals.shape[1]
     classes = class_weight.shape[1]
     dates, tiles = lax.axis_size("date"), lax.axis_size("tile")
-    first, last = exchange(arrivals.reshape(slots, -1, width), owner_map[0])
-
     codes = block_ids.reshape(1, 1)
     one_hot = (codes == jnp.arange(location_table.shape[0], dtype=jnp.int32)[None, :]).astype(bf16)
-    location = jnp.dot(one_hot, location_table, preferred_element_type=f32)
-    profile = blend_weights.reshape(2, TILE_PX).astype(bf16)
-    profile = jnp.concatenate([profile[:1] * tile_valid.reshape(1).astype(bf16), profile[1:]], axis=0)
-    profile = jnp.pad(profile, ((0, 0), (0, LANES - TILE_PX)))
-    kernels, edges = decoder_kernels(upsample_weight, class_weight)
-
-    arrays = [array for array, _ in first]
-    arrays, location, profile, kernels, edges = lax.optimization_barrier((arrays, location, profile, kernels, edges))
-    first = [(array, n) for array, (_, n) in zip(arrays, first)]
-    packed0, norms0, x0 = project(first, location, norm_gain[None], qkv_weight)
-    packed1, norms1, x1 = project(last, location, norm_gain[None], qkv_weight)
-    mixed = attend([packed0, packed1], [norms0, norms1])
+
+    def prepare(stacked):
+        table, blend, up, _ = lax.optimization_barrier((location_table, blend_weights, upsample_weight, stacked))
+        location = jnp.dot(one_hot, table, preferred_element_type=f32)
+        profile = blend.reshape(2, TILE_PX).astype(bf16)
+        profile = jnp.concatenate([profile[:1] * tile_valid.reshape(1).astype(bf16), profile[1:]], axis=0)
+        profile = jnp.pad(profile, ((0, 0), (0, LANES - TILE_PX)))
+        return (location, profile) + tuple(decoder_kernels(up, class_weight))
+
+    def use(pieces, prepared):
+        return project(pieces, prepared[0], norm_gain[None], qkv_weight)
+
+    (packed, norms, x), last, prepared = exchange(arrivals.reshape(slots, -1, width), owner_map[0], prepare, use)
+    location, profile, kernels, edges = prepared
     go_last = jnp.where((lax.axis_index("col") == 0) | (lax.axis_size("col") != 2), 1, 0)
     place = jnp.stack([lax.axis_index("date"), lax.axis_index("tile"), go_last]).astype(jnp.int32)
-    reduced, to_after, to_before = reduce_dates(
-        place, mixed, out_weight, x0, x1, location, final_gain[None], reduce_weight, reduce_bias[None], profile, tiles, dates
+    reduced, to_after, to_before = encode(
+        place, packed, norms, x, last, location, norm_gain[None], qkv_weight, out_weight, final_gain[None],
+        reduce_weight, reduce_bias[None], profile, tiles, dates
     )
     rims = exchange_rims(reduced, to_after, to_before, profile)
     return compose(reduced, rims, profile, kernels, edges, class_bias, classes)[None]

time: 153 us -> 138 us (0.902)
  Pallas kernels: 84.2 us -> 68.4 us
  starting transfers between devices: 24.7 us -> 30.5 us
  local copies, waits for them, and re-layouts: 14.1 us -> 11.8 us
  waiting for transfers between devices: 24.1 us -> 21.9 us
    pallas_call x4 -> x2, Pallas kernels: 61.8 us -> 50.3 us  [the longest x1 44.2 us: encode(): pl.pallas_call(functools.partial(encode_kernel, [n for _, n in last], ord...]
    pallas_call x1 -> x2, Pallas kernels: 8.25 us -> 3.88 us  [gather_pieces(): pl.pallas_call(functools.partial(gather_kernel, routes), in_specs=[pl.Blo...]
    optimization_barrier x0 -> x1, local copies, waits for them, and re-layouts: none -> 3.65 us  [prepare(): lax.optimization_barrier((location_table, blend_weights, upsample_weight,...]
    ppermute x1, starting transfers between devices: 7.65 us -> 11.1 us  [exchange_rims(): above = lax.ppermute(lines(UPPER), ('date', 'tile'), forward(rows))]
    slice x6 -> x2, local copies, waits for them, and re-layouts: 3.93 us -> 0.86 us  [cross_dates(): ring[m:m + 1]]
    ppermute x13 -> x16, starting transfers between devices: 15.7 us -> 17.9 us  [swap(): lax.ppermute(value, axis, [(i, i ^ mask) for i in range(lax.axis_size(axi...]
    ppermute x13 -> x16, waiting for transfers between devices: 20.3 us -> 18.2 us  [swap(): lax.ppermute(value, axis, [(i, i ^ mask) for i in range(lax.axis_size(axi...]
    unnamed x43 -> x40, local copies, waits for them, and re-layouts: 7.53 us -> 7.11 us
  transfers between devices with their start and end apart: 15 -> 18, of which waited for: 7 -> 6; matrix products, arithmetic and copies ran while one was open for 8% -> 5% of each run, Pallas kernels for 13% -> 10%
where the time goes in v3:
time: 138 us
  Pallas kernels  68.4 us (50%)
  starting transfers between devices  30.5 us (22%)
  waiting for transfers between devices  21.9 us (16%)
  local copies, waits for them, and re-layouts  11.8 us (9%)
  other arithmetic  3.27 us (2%)
  between operations  1.61 us (1%)
    pallas_call x1, Pallas kernels, encode(): pl.pallas_call(functools.partial(encode_kernel, [n for _, n in last], ord...  44.2 us
    ppermute x16, waiting for transfers between devices, swap(): lax.ppermute(value, axis, [(i, i ^ mask) for i in range(lax.axis_size(axi...  18.2 us
    ppermute x16, starting transfers between devices, swap(): lax.ppermute(value, axis, [(i, i ^ mask) for i in range(lax.axis_size(axi...  17.9 us
    ppermute x1, starting transfers between devices, exchange_rims(): above = lax.ppermute(lines(UPPER), ('date', 'tile'), forward(rows))  11.1 us
    pallas_call x1, Pallas kernels, compose(): pl.pallas_call(functools.partial(compose_kernel, classes), in_specs=[whol...  8.52 us
    unnamed x40, local copies, waits for them, and re-layouts  7.11 us
    pallas_call x1, Pallas kernels, project(): pl.pallas_call(functools.partial(project_kernel, [n for _, n in pieces]),...  6.1 us
    pallas_call x1, Pallas kernels, decoder_kernels(): pl.pallas_call(kernels_kernel, out_shape=[jax.ShapeDtypeStruct((SPAN, LAN...  5.67 us
  transfers between devices with their start and end apart: 18, of which 6 were waited for; matrix products, arithmetic and copies ran while one was open for 5% of the time, Pallas kernels for 10%

profile of v3, /device:TPU:0, one launch (start us, length us, event | category | flops | bytes accessed | tf_op | source)
XLA Modules:
  0.0 137.6 jit_solution(10290939076457613655)
XLA Ops:
  0.0 0.7 xor_add_fusion
  0.7 0.8 select_reduce_fusion.index_ref
  1.5 1.7 %copy-done.2 = bf16[1,16,1,1,4,16,1280]{6,5,4,3,2,1,0:T(8,128)(2,1)S(1)} copy-done((bf16[1,16,1,1,4,16,1280]{6,5,4,3,2,1,0:T(8,128)(2,1)S(1)}, bf16[1,16,1,1,4,16,1280]{6,5,4,3,2,1,0:T(8,128)(2,1)}, u32[]{:S(2)}) %copy-start.2) | copy-done | bytes 2621464
  3.3 2.5 %gather_pieces.2 = (bf16[4,64,1280]{2,1,0:T(8,128)(2,1)S(1)}, bf16[4,64,1280]{2,1,0:T(8,128)(2,1)}, bf16[1,64,1280]{2,1,0:T(8,128)(2,1)S(1)}, bf16[1,64,1280]{2,...) custom-call(s32[12]{0:T(128)S(1)} %select_reduce_fusion.index_ref, ...), custom_call_target="tpu_custom_call" | custom-call | tf_op jit(solution)/shard_map/gather_pieces/pallas_call | solution.py:80
  5.7 0.0 copy-start.16
  5.8 2.4 %collective-permute-start.2 = (bf16[1,64,1280]{2,1,0:T(8,128)(2,1)S(1)}, bf16[1,64,1280]{2,1,0:T(8,128)(2,1)S(1)}, u32[]{:S(2)}, u32[]{:S(2)}) collective-permute-start(bf16[1,64,1280]{2,1,0:T(8,128)(2,1)S(1)} %get-tuple-element.44), channel_id=1, source_target_pairs={{0,24},{8,16},{16,8},{24,0},{1,25},{9,17},{17,9},{25,1},{2,26},{10... | collective-permute-start | bytes 491528 | tf_op jit(solution)/shard_map/ppermute | solution.py:94
  8.2 0.6 collective-permute-start.1
  8.8 0.0 collective-permute-start
  8.9 1.8 %collective-permute-start.6 = (bf16[4,64,1280]{2,1,0:T(8,128)(2,1)S(1)}, bf16[4,64,1280]{2,1,0:T(8,128)(2,1)S(1)}, u32[]{:S(2)}, u32[]{:S(2)}) collective-permute-start(bf16[4,64,1280]{2,1,0:T(8,128)(2,1)S(1)} %get-tuple-element.50), channel_id=1, source_target_pairs={{0,2},{2,0},{4,6},{6,4},{1,3},{3,1},{5,7},{7,5},{8,10},{10,8},{12,... | collective-permute-start | bytes 1966088 | tf_op jit(solution)/shard_map/ppermute | solution.py:94
  10.7 2.6 %collective-permute-start.10 = (bf16[4,64,1280]{2,1,0:T(8,128)(2,1)}, bf16[4,64,1280]{2,1,0:T(8,128)(2,1)S(1)}, u32[]{:S(2)}, u32[]{:S(2)}) collective-permute-start(bf16[4,64,1280]{2,1,0:T(8,128)(2,1)} %get-tuple-element.58), channel_id=1, source_target_pairs={{0,4},{2,6},{4,0},{6,2},{1,5},{3,7},{5,1},{7,3},{8,12},{10,14},{12... | collective-permute-start | bytes 1966088 | tf_op jit(solution)/shard_map/ppermute | solution.py:94
  14.6 0.2 select_reduce_fusion.1.index_ref
  14.8 0.0 collective-permute-done.2
  14.8 1.7 %collective-permute-done.1 = bf16[1,64,1280]{2,1,0:T(8,128)(2,1)S(1)} collective-permute-done((bf16[1,64,1280]{2,1,0:T(8,128)(2,1)S(1)}, bf16[1,64,1280]{2,1,0:T(8,128)(2,1)S(1)}, u32[]{:S(2)}, u32[]{:S(2)}) %collective-permute-start.1) | collective-permute-done | bytes 163872 | tf_op jit(solution)/shard_map/ppermute | solution.py:94
  16.5 0.0 collective-permute-done
  16.5 0.9 pad_maximum_fusion
  17.4 1.4 %gather_pieces.3 = (bf16[1,64,1280]{2,1,0:T(8,128)(2,1)S(1)}, bf16[1,64,1280]{2,1,0:T(8,128)(2,1)S(1)}, bf16[1,64,1280]{2,1,0:T(8,128)(2,1)S(1)}, bf16[1,64,1280]{2,1,0:T(8,128)(2,1)S(1)}) custom-call(s32[4]{0:T(128)S(1)} %select_reduce_fusion.1.index_ref, bf16[16,64,1280]{2,1,0:T(8,128)(2,1)S(1)} %bitcast.19), custom_call_target="tpu_custom_call" | custom-call | tf_op jit(solution)/shard_map/gather_pieces/pallas_call | solution.py:80
  18.8 0.1 collective-permute-start.3
  18.9 2.4 %collective-permute-start.4 = (bf16[1,64,1280]{2,1,0:T(8,128)(2,1)S(1)}, bf16[1,64,1280]{2,1,0:T(8,128)(2,1)S(1)}, u32[]{:S(2)}, u32[]{:S(2)}) collective-permute-start(bf16[1,64,1280]{2,1,0:T(8,128)(2,1)S(1)} %get-tuple-element.48), channel_id=1, source_target_pairs={{0,16},{8,24},{16,0},{24,8},{1,17},{9,25},{17,1},{25,9},{2,18},{10... | collective-permute-start | bytes 491528 | tf_op jit(solution)/shard_map/ppermute | solution.py:94
  21.3 0.1 collective-permute-start.5
  21.4 0.1 fusion.2.refs_8_.refs_5_
  21.5 3.6 %copy.28.up_ref = bf16[256,3136]{1,0:T(8,128)(2,1)} copy(bf16[256,3136]{0,1:T(8,128)(2,1)} %param.38) | data formatting | bytes 3211264 | tf_op jit(solution)/shard_map/optimization_barrier | solution.py:631
  25.2 5.7 %decoder_kernels.1 = (bf16[16,256,256]{2,1,0:T(8,128)(2,1)}, bf16[2,256,256]{2,1,0:T(8,128)(2,1)}) custom-call(bf16[256,3136]{1,0:T(8,128)(2,1)} %copy.28.up_ref, bf16[9,13,16]{2,1,0:T(8,128)(2,1)} %taps_ref.1, bf16[256,13]{1,0:T(8,128)(2,1)} %constant.46.clone.rows_ref, bf16[16,224]{1,0:T(8,128)(2,1)} %constant.47.clone.columns_ref, ...), custom_call_target="tpu_custom_call" | custom-call | tf_op jit(solution)/shard_map/decoder_kernels/pallas_call | solution.py:428
  30.9 8.9 %collective-permute-done.6.refs_4_ = bf16[4,64,1280]{2,1,0:T(8,128)(2,1)S(1)} collective-permute-done((bf16[4,64,1280]{2,1,0:T(8,128)(2,1)S(1)}, bf16[4,64,1280]{2,1,0:T(8,128)(2,1)S(1)}, u32[]{:S(2)}, u32[]{:S(2)}) %collective-permute-start.6) | collective-permute-done | bytes 655392 | tf_op jit(solution)/shard_map/ppermute | solution.py:94
  39.7 0.1 collective-permute-start.7
  39.8 1.5 %collective-permute-start.8 = (bf16[1,64,1280]{2,1,0:T(8,128)(2,1)S(1)}, bf16[1,64,1280]{2,1,0:T(8,128)(2,1)S(1)}, u32[]{:S(2)}, u32[]{:S(2)}) collective-permute-start(bf16[1,64,1280]{2,1,0:T(8,128)(2,1)S(1)} %get-tuple-element.81), channel_id=1, source_target_pairs={{0,16},{8,24},{16,0},{24,8},{1,17},{9,25},{17,1},{25,9},{2,18},{10... | collective-permute-start | bytes 491528 | tf_op jit(solution)/shard_map/ppermute | solution.py:94
  41.3 0.4 collective-permute-start.9
  41.7 2.5 %collective-permute-start.11 = (bf16[4,64,1280]{2,1,0:T(8,128)(2,1)}, bf16[4,64,1280]{2,1,0:T(8,128)(2,1)S(1)}, u32[]{:S(2)}, u32[]{:S(2)}) collective-permute-start(bf16[4,64,1280]{2,1,0:T(8,128)(2,1)} %pad_maximum_fusion), channel_id=1, source_target_pairs={{0,6},{2,4},{4,2},{6,0},{1,7},{3,5},{5,3},{7,1},{8,14},{10,12},{12... | collective-permute-start | bytes 1966088 | tf_op jit(solution)/shard_map/ppermute | solution.py:94
  44.2 2.7 %collective-permute-done.8.refs_6_ = bf16[1,64,1280]{2,1,0:T(8,128)(2,1)S(1)} collective-permute-done((bf16[1,64,1280]{2,1,0:T(8,128)(2,1)S(1)}, bf16[1,64,1280]{2,1,0:T(8,128)(2,1)S(1)}, u32[]{:S(2)}, u32[]{:S(2)}) %collective-permute-start.8) | collective-permute-done | bytes 163872 | tf_op jit(solution)/shard_map/ppermute | solution.py:94
  46.9 2.6 %collective-permute-done.9.refs_7_ = bf16[1,64,1280]{2,1,0:T(8,128)(2,1)S(1)} collective-permute-done((bf16[1,64,1280]{2,1,0:T(8,128)(2,1)S(1)}, bf16[1,64,1280]{2,1,0:T(8,128)(2,1)S(1)}, u32[]{:S(2)}, u32[]{:S(2)}) %collective-permute-start.9) | collective-permute-done | bytes 163872 | tf_op jit(solution)/shard_map/ppermute | solution.py:94
  49.5 0.8 fusion.9
  50.3 0.6 collective-permute-start.12
  50.9 1.4 %collective-permute-start.13 = (bf16[1,64,1280]{2,1,0:T(8,128)(2,1)}, bf16[1,64,1280]{2,1,0:T(8,128)(2,1)S(1)}, u32[]{:S(2)}, u32[]{:S(2)}) collective-permute-start(bf16[1,64,1280]{2,1,0:T(8,128)(2,1)} %get-tuple-element.78), channel_id=1, source_target_pairs={{0,16},{8,24},{16,0},{24,8},{1,17},{9,25},{17,1},{25,9},{2,18},{10... | collective-permute-start | bytes 491528 | tf_op jit(solution)/shard_map/ppermute | solution.py:94
  52.4 0.1 pad_add_fusion.place_ref
  52.4 3.8 %copy-done.1 = bf16[1280,3840]{1,0:T(8,128)(2,1)S(1)} copy-done((bf16[1280,3840]{1,0:T(8,128)(2,1)S(1)}, bf16[1280,3840]{1,0:T(8,128)(2,1)}, u32[]{:S(2)}) %copy-start.1) | copy-done | bytes 9830424
  56.2 0.9 copy-done.8
  57.2 6.1 %project.1 = (bf16[3840,512]{1,0:T(8,128)(2,1)S(1)}, f32[32,128]{1,0:T(8,128)S(1)}, bf16[512,1280]{1,0:T(8,128)(2,1)S(1)}) custom-call(bf16[1,64,1280]{2,1,0:T(8,128)(2,1)S(1)} %get-tuple-element.59.refs_0_, bf16[1,64,1280]{2,1,0:T(8,128)(2,1)S(1)} %collective-permute-done.3.refs_1_, bf16[1,64,1280]{2,1,0:T(8,128)(2,1)S(1)} %collective-permute-done.4.refs_2_, ...), custom_call_target="tpu_custom_call" | custom-call | tf_op jit(solution)/shard_map/project/pallas_call | solution.py:165
  63.3 0.0 copy-start.19
  63.3 44.2 %encode.1 = (bf16[256,256]{1,0:T(8,128)(2,1)S(1)}, bf16[48,256]{1,0:T(8,128)(2,1)S(1)}, bf16[48,256]{1,0:T(8,128)(2,1)}) custom-call(s32[3]{0:T(128)S(1)} %pad_add_fusion.place_ref, bf16[3840,512]{1,0:T(8,128)(2,1)S(1)} %get-tuple-element.68.packed_ref, f32[32,128]{1,0:T(8,128)S(1)} %get-tuple-element.69.norm_ref, ...), custom_call_target="tpu_custom_call" | custom-call | tf_op jit(solution)/shard_map/encode/pallas_call | solution.py:286
  107.6 1.5 %collective-permute-start.15 = (bf16[48,256]{1,0:T(8,128)(2,1)S(1)}, bf16[48,256]{1,0:T(8,128)(2,1)S(1)}, u32[]{:S(2)}, u32[]{:S(2)}) collective-permute-start(bf16[48,256]{1,0:T(8,128)(2,1)S(1)} %get-tuple-element.74), channel_id=1, source_target_pairs={{0,1},{1,0},{2,3},{3,2},{4,5},{5,4},{6,7},{7,6},{8,9},{9,8},{10,11... | collective-permute-start | bytes 73736 | tf_op jit(solution)/shard_map/ppermute | solution.py:94
  109.1 2.3 %collective-permute-done.15 = bf16[48,256]{1,0:T(8,128)(2,1)S(1)} collective-permute-done((bf16[48,256]{1,0:T(8,128)(2,1)S(1)}, bf16[48,256]{1,0:T(8,128)(2,1)S(1)}, u32[]{:S(2)}, u32[]{:S(2)}) %collective-permute-start.15) | collective-permute-done | bytes 24608 | tf_op jit(solution)/shard_map/ppermute | solution.py:94
  111.5 0.1 concatenate.12
  111.6 11.1 %collective-permute-start.16 = (bf16[48,256]{1,0:T(8,128)(2,1)S(1)}, bf16[48,256]{1,0:T(8,128)(2,1)S(1)}, u32[]{:S(2)}, u32[]{:S(2)}) collective-permute-start(bf16[48,256]{1,0:T(8,128)(2,1)S(1)} %concatenate.12), channel_id=1, source_target_pairs={{0,2},{2,4},{4,6},{6,8},{8,10},{10,12},{12,14},{14,16},{16,18},{18... | collective-permute-start | bytes 73736 | tf_op jit(solution)/shard_map/ppermute | solution.py:579
  122.6 0.1 concatenate.13
  122.7 1.5 %collective-permute-start.17 = (bf16[48,256]{1,0:T(8,128)(2,1)S(1)}, bf16[48,256]{1,0:T(8,128)(2,1)S(1)}, u32[]{:S(2)}, u32[]{:S(2)}) collective-permute-start(bf16[48,256]{1,0:T(8,128)(2,1)S(1)} %concatenate.13), channel_id=1, source_target_pairs={{2,0},{4,2},{6,4},{8,6},{10,8},{12,10},{14,12},{16,14},{18,16},{20... | collective-permute-start | bytes 73736 | tf_op jit(solution)/shard_map/ppermute | solution.py:580
  124.2 0.5 convert_element_type.20.bias_ref
  124.8 3.7 %collective-permute-done.17.below_ref = bf16[48,256]{1,0:T(8,128)(2,1)S(1)} collective-permute-done((bf16[48,256]{1,0:T(8,128)(2,1)S(1)}, bf16[48,256]{1,0:T(8,128)(2,1)S(1)}, u32[]{:S(2)}, u32[]{:S(2)}) %collective-permute-start.17) | collective-permute-done | bytes 24608 | tf_op jit(solution)/shard_map/ppermute | solution.py:580
  128.4 0.6 copy-done.13
  129.0 8.5 %compose.1 = f32[13,192,192]{2,1,0:T(8,128)} custom-call(bf16[256,256]{1,0:T(8,128)(2,1)} %copy-done.6, bf16[48,256]{1,0:T(8,128)(2,1)} %copy-done.11, bf16[48,256]{1,0:T(8,128)(2,1)} %copy-done.10, bf16[48,256]{1,0:T(8,128)(2,1)} %copy-done.12, bf16[48,256]{1,0:T(8,128)(2,1)} %copy-done.13, bf16[2,256]{1,0:T(2,128)(2,1)} %copy-done.9, ...), custom_call_target="tpu_custom_call" | custom-call | tf_op jit(solution)/shard_map/compose/pallas_call | solution.py:589
  (59 shorter events, 0.2 us)
Async XLA Ops:
  0.0 21.4 %copy-start = (bf16[16,1280]{1,0:T(8,128)(2,1)S(1)}, bf16[16,1280]{1,0:T(8,128)(2,1)}, u32[]{:S(2)}) copy-start(bf16[16,1280]{1,0:T(8,128)(2,1)} %param.31) | copy-start | bytes 122884
  0.0 14.6 %copy-start.17 = (s32[1,16]{1,0:T(1,128)S(1)}, s32[1,16]{1,0:T(1,128)}, u32[]{:S(2)}) copy-start(s32[1,16]{1,0:T(1,128)} %param.27) | copy-start | bytes 196
  1.5 1.7 %copy-start.2 = (bf16[1,16,1,1,4,16,1280]{6,5,4,3,2,1,0:T(8,128)(2,1)S(1)}, bf16[1,16,1,1,4,16,1280]{6,5,4,3,2,1,0:T(8,128)(2,1)}, u32[]{:S(2)}) copy-start(bf16[1,16,1,1,4,16,1280]{6,5,4,3,2,1,0:T(8,128)(2,1)} %param.26) | copy-start | bytes 7864324
  3.3 14.1 %copy-start.3 = (bf16[1,16,1,1,4,16,1280]{6,5,4,3,2,1,0:T(8,128)(2,1)S(1)}, bf16[1,16,1,1,4,16,1280]{6,5,4,3,2,1,0:T(8,128)(2,1)}, u32[]{:S(2)}) copy-start(bf16[1,16,1,1,4,16,1280]{6,5,4,3,2,1,0:T(8,128)(2,1)} %param.26) | copy-start | bytes 7864324
  5.7 15.6 %copy-start.16 = (s32[1,1,1,2,224]{4,3,2,1,0:T(2,128)S(1)}, s32[1,1,1,2,224]{4,3,2,1,0:T(2,128)}, u32[]{:S(2)}) copy-start(s32[1,1,1,2,224]{4,3,2,1,0:T(2,128)} %param.30) | copy-start | bytes 5380
  5.8 9.0 %collective-permute-start.2 = (bf16[1,64,1280]{2,1,0:T(8,128)(2,1)S(1)}, bf16[1,64,1280]{2,1,0:T(8,128)(2,1)S(1)}, u32[]{:S(2)}, u32[]{:S(2)}) collective-permute-start(bf16[1,64,1280]{2,1,0:T(8,128)(2,1)S(1)} %get-tuple-element.44), channel_id=1, source_target_pairs={{0,24},{8,16},{16,8},{24,0},{1,25},{9,17},{17,9},{25,1},{2,26},{10... | collective-permute-start | bytes 491528 | tf_op jit(solution)/shard_map/ppermute | solution.py:94
  8.2 8.3 %collective-permute-start.1 = (bf16[1,64,1280]{2,1,0:T(8,128)(2,1)S(1)}, bf16[1,64,1280]{2,1,0:T(8,128)(2,1)S(1)}, u32[]{:S(2)}, u32[]{:S(2)}) collective-permute-start(bf16[1,64,1280]{2,1,0:T(8,128)(2,1)S(1)} %get-tuple-element.43), channel_id=1, source_target_pairs={{0,16},{8,24},{16,0},{24,8},{1,17},{9,25},{17,1},{25,9},{2,18},{10... | collective-permute-start | bytes 491528 | tf_op jit(solution)/shard_map/ppermute | solution.py:94
  8.8 7.6 %collective-permute-start = (bf16[1,64,1280]{2,1,0:T(8,128)(2,1)S(1)}, bf16[1,64,1280]{2,1,0:T(8,128)(2,1)S(1)}, u32[]{:S(2)}, u32[]{:S(2)}) collective-permute-start(bf16[1,64,1280]{2,1,0:T(8,128)(2,1)S(1)} %get-tuple-element.42), channel_id=1, source_target_pairs={{0,8},{8,0},{16,24},{24,16},{1,9},{9,1},{17,25},{25,17},{2,10},{10... | collective-permute-start | bytes 491528 | tf_op jit(solution)/shard_map/ppermute | solution.py:94
  8.9 30.8 %collective-permute-start.6 = (bf16[4,64,1280]{2,1,0:T(8,128)(2,1)S(1)}, bf16[4,64,1280]{2,1,0:T(8,128)(2,1)S(1)}, u32[]{:S(2)}, u32[]{:S(2)}) collective-permute-start(bf16[4,64,1280]{2,1,0:T(8,128)(2,1)S(1)} %get-tuple-element.50), channel_id=1, source_target_pairs={{0,2},{2,0},{4,6},{6,4},{1,3},{3,1},{5,7},{7,5},{8,10},{10,8},{12,... | collective-permute-start | bytes 1966088 | tf_op jit(solution)/shard_map/ppermute | solution.py:94
  10.7 33.5 %collective-permute-start.10 = (bf16[4,64,1280]{2,1,0:T(8,128)(2,1)}, bf16[4,64,1280]{2,1,0:T(8,128)(2,1)S(1)}, u32[]{:S(2)}, u32[]{:S(2)}) collective-permute-start(bf16[4,64,1280]{2,1,0:T(8,128)(2,1)} %get-tuple-element.58), channel_id=1, source_target_pairs={{0,4},{2,6},{4,0},{6,2},{1,5},{3,7},{5,1},{7,3},{8,12},{10,14},{12... | collective-permute-start | bytes 1966088 | tf_op jit(solution)/shard_map/ppermute | solution.py:94
  18.8 21.0 %collective-permute-start.3 = (bf16[1,64,1280]{2,1,0:T(8,128)(2,1)S(1)}, bf16[1,64,1280]{2,1,0:T(8,128)(2,1)S(1)}, u32[]{:S(2)}, u32[]{:S(2)}) collective-permute-start(bf16[1,64,1280]{2,1,0:T(8,128)(2,1)S(1)} %get-tuple-element.47), channel_id=1, source_target_pairs={{0,8},{8,0},{16,24},{24,16},{1,9},{9,1},{17,25},{25,17},{2,10},{10... | collective-permute-start | bytes 491528 | tf_op jit(solution)/shard_map/ppermute | solution.py:94
  18.9 22.4 %collective-permute-start.4 = (bf16[1,64,1280]{2,1,0:T(8,128)(2,1)S(1)}, bf16[1,64,1280]{2,1,0:T(8,128)(2,1)S(1)}, u32[]{:S(2)}, u32[]{:S(2)}) collective-permute-start(bf16[1,64,1280]{2,1,0:T(8,128)(2,1)S(1)} %get-tuple-element.48), channel_id=1, source_target_pairs={{0,16},{8,24},{16,0},{24,8},{1,17},{9,25},{17,1},{25,9},{2,18},{10... | collective-permute-start | bytes 491528 | tf_op jit(solution)/shard_map/ppermute | solution.py:94
  21.3 20.4 %collective-permute-start.5 = (bf16[1,64,1280]{2,1,0:T(8,128)(2,1)S(1)}, bf16[1,64,1280]{2,1,0:T(8,128)(2,1)S(1)}, u32[]{:S(2)}, u32[]{:S(2)}) collective-permute-start(bf16[1,64,1280]{2,1,0:T(8,128)(2,1)S(1)} %get-tuple-element.49), channel_id=1, source_target_pairs={{0,24},{8,16},{16,8},{24,0},{1,25},{9,17},{17,9},{25,1},{2,26},{10... | collective-permute-start | bytes 491528 | tf_op jit(solution)/shard_map/ppermute | solution.py:94
  21.5 101.1 %copy-start.9 = (bf16[2,256]{1,0:T(2,128)(2,1)}, bf16[2,256]{1,0:T(2,128)(2,1)S(1)}, u32[]{:S(2)}) copy-start(bf16[2,256]{1,0:T(2,128)(2,1)S(1)} %fusion.5.refs_12_.profile_ref) | copy-start | bytes 3076
  25.2 27.1 %copy-start.14 = (bf16[1280]{0:T(1024)(128)(2,1)S(1)}, bf16[1280]{0:T(1024)(128)(2,1)}, u32[]{:S(2)}) copy-start(bf16[1280]{0:T(1024)(128)(2,1)} %param.32) | copy-start | bytes 7684
  25.2 27.2 %copy-start.15 = (bf16[1280]{0:T(1024)(128)(2,1)S(1)}, bf16[1280]{0:T(1024)(128)(2,1)}, u32[]{:S(2)}) copy-start(bf16[1280]{0:T(1024)(128)(2,1)} %param.35) | copy-start | bytes 7684
  25.2 27.2 %copy-start.18 = (bf16[256]{0:T(256)(128)(2,1)S(1)}, bf16[256]{0:T(256)(128)(2,1)}, u32[]{:S(2)}) copy-start(bf16[256]{0:T(256)(128)(2,1)} %param.37) | copy-start | bytes 1540
  39.7 4.4 %collective-permute-start.7 = (bf16[1,64,1280]{2,1,0:T(8,128)(2,1)S(1)}, bf16[1,64,1280]{2,1,0:T(8,128)(2,1)S(1)}, u32[]{:S(2)}, u32[]{:S(2)}) collective-permute-start(bf16[1,64,1280]{2,1,0:T(8,128)(2,1)S(1)} %get-tuple-element.82), channel_id=1, source_target_pairs={{0,8},{8,0},{16,24},{24,16},{1,9},{9,1},{17,25},{25,17},{2,10},{10... | collective-permute-start | bytes 491528 | tf_op jit(solution)/shard_map/ppermute | solution.py:94
  39.8 7.1 %collective-permute-start.8 = (bf16[1,64,1280]{2,1,0:T(8,128)(2,1)S(1)}, bf16[1,64,1280]{2,1,0:T(8,128)(2,1)S(1)}, u32[]{:S(2)}, u32[]{:S(2)}) collective-permute-start(bf16[1,64,1280]{2,1,0:T(8,128)(2,1)S(1)} %get-tuple-element.81), channel_id=1, source_target_pairs={{0,16},{8,24},{16,0},{24,8},{1,17},{9,25},{17,1},{25,9},{2,18},{10... | collective-permute-start | bytes 491528 | tf_op jit(solution)/shard_map/ppermute | solution.py:94
  41.3 8.2 %collective-permute-start.9 = (bf16[1,64,1280]{2,1,0:T(8,128)(2,1)S(1)}, bf16[1,64,1280]{2,1,0:T(8,128)(2,1)S(1)}, u32[]{:S(2)}, u32[]{:S(2)}) collective-permute-start(bf16[1,64,1280]{2,1,0:T(8,128)(2,1)S(1)} %get-tuple-element.80), channel_id=1, source_target_pairs={{0,24},{8,16},{16,8},{24,0},{1,25},{9,17},{17,9},{25,1},{2,26},{10... | collective-permute-start | bytes 491528 | tf_op jit(solution)/shard_map/ppermute | solution.py:94
  41.7 21.6 %collective-permute-start.11 = (bf16[4,64,1280]{2,1,0:T(8,128)(2,1)}, bf16[4,64,1280]{2,1,0:T(8,128)(2,1)S(1)}, u32[]{:S(2)}, u32[]{:S(2)}) collective-permute-start(bf16[4,64,1280]{2,1,0:T(8,128)(2,1)} %pad_maximum_fusion), channel_id=1, source_target_pairs={{0,6},{2,4},{4,2},{6,0},{1,7},{3,5},{5,3},{7,1},{8,14},{10,12},{12... | collective-permute-start | bytes 1966088 | tf_op jit(solution)/shard_map/ppermute | solution.py:94
  49.5 0.8 copy-start.7
  50.3 13.0 %collective-permute-start.12 = (bf16[1,64,1280]{2,1,0:T(8,128)(2,1)}, bf16[1,64,1280]{2,1,0:T(8,128)(2,1)S(1)}, u32[]{:S(2)}, u32[]{:S(2)}) collective-permute-start(bf16[1,64,1280]{2,1,0:T(8,128)(2,1)} %get-tuple-element.79), channel_id=1, source_target_pairs={{0,8},{8,0},{16,24},{24,16},{1,9},{9,1},{17,25},{25,17},{2,10},{10... | collective-permute-start | bytes 491528 | tf_op jit(solution)/shard_map/ppermute | solution.py:94
  50.9 12.4 %collective-permute-start.13 = (bf16[1,64,1280]{2,1,0:T(8,128)(2,1)}, bf16[1,64,1280]{2,1,0:T(8,128)(2,1)S(1)}, u32[]{:S(2)}, u32[]{:S(2)}) collective-permute-start(bf16[1,64,1280]{2,1,0:T(8,128)(2,1)} %get-tuple-element.78), channel_id=1, source_target_pairs={{0,16},{8,24},{16,0},{24,8},{1,17},{9,25},{17,1},{25,9},{2,18},{10... | collective-permute-start | bytes 491528 | tf_op jit(solution)/shard_map/ppermute | solution.py:94
  52.3 11.0 %collective-permute-start.14 = (bf16[1,64,1280]{2,1,0:T(8,128)(2,1)}, bf16[1,64,1280]{2,1,0:T(8,128)(2,1)S(1)}, u32[]{:S(2)}, u32[]{:S(2)}) collective-permute-start(bf16[1,64,1280]{2,1,0:T(8,128)(2,1)} %get-tuple-element.77), channel_id=1, source_target_pairs={{0,24},{8,16},{16,8},{24,0},{1,25},{9,17},{17,9},{25,1},{2,26},{10... | collective-permute-start | bytes 491528 | tf_op jit(solution)/shard_map/ppermute | solution.py:94
  52.4 3.8 %copy-start.1 = (bf16[1280,3840]{1,0:T(8,128)(2,1)S(1)}, bf16[1280,3840]{1,0:T(8,128)(2,1)}, u32[]{:S(2)}) copy-start(bf16[1280,3840]{1,0:T(8,128)(2,1)} %refs_7_.1) | copy-start | bytes 29491204
  56.2 0.9 copy-start.8
  57.2 6.2 %copy-start.4 = (bf16[1280,1280]{1,0:T(8,128)(2,1)S(1)}, bf16[1280,1280]{1,0:T(8,128)(2,1)}, u32[]{:S(2)}) copy-start(bf16[1280,1280]{1,0:T(8,128)(2,1)} %refs_8_.1) | copy-start | bytes 9830404
  57.2 6.2 %copy-start.5 = (bf16[5120,256]{1,0:T(8,128)(2,1)S(1)}, bf16[5120,256]{1,0:T(8,128)(2,1)}, u32[]{:S(2)}) copy-start(bf16[5120,256]{1,0:T(8,128)(2,1)} %param.36) | copy-start | bytes 7864324
  63.3 60.9 %copy-start.19 = (bf16[13]{0:T(256)(128)(2,1)S(1)}, bf16[13]{0:T(256)(128)(2,1)}, u32[]{:S(2)}) copy-start(bf16[13]{0:T(256)(128)(2,1)} %param.40) | copy-start | bytes 82
  107.6 20.9 %copy-start.6 = (bf16[256,256]{1,0:T(8,128)(2,1)}, bf16[256,256]{1,0:T(8,128)(2,1)S(1)}, u32[]{:S(2)}) copy-start(bf16[256,256]{1,0:T(8,128)(2,1)S(1)} %get-tuple-element.73.own_ref) | copy-start | bytes 393220
  107.6 3.9 %collective-permute-start.15 = (bf16[48,256]{1,0:T(8,128)(2,1)S(1)}, bf16[48,256]{1,0:T(8,128)(2,1)S(1)}, u32[]{:S(2)}, u32[]{:S(2)}) collective-permute-start(bf16[48,256]{1,0:T(8,128)(2,1)S(1)} %get-tuple-element.74), channel_id=1, source_target_pairs={{0,1},{1,0},{2,3},{3,2},{4,5},{5,4},{6,7},{7,6},{8,9},{9,8},{10,11... | collective-permute-start | bytes 73736 | tf_op jit(solution)/shard_map/ppermute | solution.py:94
  111.4 17.0 %copy-start.10 = (bf16[48,256]{1,0:T(8,128)(2,1)}, bf16[48,256]{1,0:T(8,128)(2,1)S(1)}, u32[]{:S(2)}) copy-start(bf16[48,256]{1,0:T(8,128)(2,1)S(1)} %get-tuple-element.101.after_ref) | copy-start | bytes 73732
  111.4 17.0 %copy-start.11 = (bf16[48,256]{1,0:T(8,128)(2,1)}, bf16[48,256]{1,0:T(8,128)(2,1)S(1)}, u32[]{:S(2)}) copy-start(bf16[48,256]{1,0:T(8,128)(2,1)S(1)} %get-tuple-element.102.before_ref) | copy-start | bytes 73732
  111.6 13.2 %collective-permute-start.16 = (bf16[48,256]{1,0:T(8,128)(2,1)S(1)}, bf16[48,256]{1,0:T(8,128)(2,1)S(1)}, u32[]{:S(2)}, u32[]{:S(2)}) collective-permute-start(bf16[48,256]{1,0:T(8,128)(2,1)S(1)} %concatenate.12), channel_id=1, source_target_pairs={{0,2},{2,4},{4,6},{6,8},{8,10},{10,12},{12,14},{14,16},{16,18},{18... | collective-permute-start | bytes 73736 | tf_op jit(solution)/shard_map/ppermute | solution.py:579
  122.7 5.7 %collective-permute-start.17 = (bf16[48,256]{1,0:T(8,128)(2,1)S(1)}, bf16[48,256]{1,0:T(8,128)(2,1)S(1)}, u32[]{:S(2)}, u32[]{:S(2)}) collective-permute-start(bf16[48,256]{1,0:T(8,128)(2,1)S(1)} %concatenate.13), channel_id=1, source_target_pairs={{2,0},{4,2},{6,4},{8,6},{10,8},{12,10},{14,12},{16,14},{18,16},{20... | collective-permute-start | bytes 73736 | tf_op jit(solution)/shard_map/ppermute | solution.py:580
  124.8 3.7 %copy-start.12 = (bf16[48,256]{1,0:T(8,128)(2,1)}, bf16[48,256]{1,0:T(8,128)(2,1)S(1)}, u32[]{:S(2)}) copy-start(bf16[48,256]{1,0:T(8,128)(2,1)S(1)} %collective-permute-done.16.above_ref) | copy-start | bytes 73732
  128.4 0.6 copy-start.13

commit v4 on v3

--- a/solution.py
+++ b/solution.py
@@ -49,45 +49,29 @@
     return centered * lax.rsqrt(spread + norm_eps) * gain_row
 
 
-def gather_kernel(routes, index_ref, a_ref, *refs):
-    outs, sems = refs[:-1], refs[-1]
-    copies = []
-    for n, (out, spot) in enumerate(routes):
-        copies.append(pltpu.make_async_copy(a_ref.at[index_ref[n]], outs[out].at[spot], sems.at[n]))
-    for copy in copies:
-        copy.start()
-    for copy in copies:
-        copy.wait()
-
-
-def gather_pieces(arrivals, owner_map, rings, together, dates):
+def gather_kernel(dates, tiles, routes, owner_ref, a_ref, *refs):
+    outs, slot_ref = refs[:-1], refs[-1]
+    for slot in range(dates * tiles):
+        slot_ref[owner_ref[slot]] = slot
+    date, tile = lax.axis_index("date"), lax.axis_index("tile")
+    for s, m, out, spot in routes:
+        outs[out][spot] = a_ref[slot_ref[(date ^ m) * tiles + (tile ^ s)]]
+
+
+def gather_pieces(arrivals, owner_map, groups, dates):
     slots, strip, width = arrivals.shape
-    tiles = slots // dates
-    date, tile = lax.axis_index("date"), lax.axis_index("tile")
-    routes, order = [], []
-    for s in rings + together:
-        for m in range(dates):
-            order.append((s, m))
-            routes.append((rings.index(s), m) if s in rings else (len(rings) + m, together.index(s)))
-    s_of = jnp.array([s for s, _ in order], jnp.int32)
-    m_of = jnp.array([m for _, m in order], jnp.int32)
-    wanted = (date ^ m_of) * tiles + (tile ^ s_of)
-    spots = jnp.arange(slots, dtype=jnp.int32)[None, :]
-    index = jnp.sum(jnp.where(owner_map[None, :] == wanted[:, None], spots, 0), axis=1)
-    shapes = [jax.ShapeDtypeStruct((dates, strip, width), bf16)] * len(rings)
-    shapes += [jax.ShapeDtypeStruct((len(together), strip, width), bf16)] * dates
-    anywhere = pl.BlockSpec(memory_space=pl.ANY)
-    outs = pl.pallas_call(
-        functools.partial(gather_kernel, routes),
-        in_specs=[pl.BlockSpec(memory_space=pltpu.SMEM), pl.BlockSpec(memory_space=pltpu.VMEM)],
-        out_specs=[anywhere] * len(shapes),
-        out_shape=shapes,
-        scratch_shapes=[pltpu.SemaphoreType.DMA((len(routes),))],
-        compiler_params=pltpu.CompilerParams(vmem_limit_bytes=4 * 2**20),
+    routes = [(s, m, n, i) for n, group in enumerate(groups) for i, (s, m) in enumerate(group)]
+    whole = pl.BlockSpec(memory_space=pltpu.VMEM)
+    return pl.pallas_call(
+        functools.partial(gather_kernel, dates, slots // dates, routes),
+        in_specs=[pl.BlockSpec(memory_space=pltpu.SMEM), whole],
+        out_specs=[whole] * len(groups),
+        out_shape=[pltpu.VMEM((len(group), strip, width), bf16) for group in groups],
+        scratch_shapes=[pltpu.SMEM((slots,), jnp.int32)],
+        compiler_params=pltpu.CompilerParams(vmem_limit_bytes=12 * 2**20),
         cost_estimate=pl.CostEstimate(flops=0, bytes_accessed=0, transcendentals=0),
         name="gather_pieces",
-    )(index, arrivals)
-    return outs[: len(rings)], outs[len(rings) :]
+    )(owner_map, arrivals)
 
 
 def swap(value, axis, mask):
@@ -97,17 +81,21 @@
 def exchange(arrivals, owner_map, prepare, use):
     dates, tiles = lax.axis_size("date"), lax.axis_size("tile")
     half, late = tiles // 2, tiles - max(1, tiles // 4)
-    rings, mixed = gather_pieces(arrivals, owner_map, list(range(1, late)), list(range(late, tiles)), dates)
-    rings = [swap(ring, "tile", s) for s, ring in enumerate(rings, 1)]
+    groups = [[(s, m) for m in range(dates)] for s in range(1, late)]
+    groups += [[(s, m) for s in range(late, tiles)] for m in range(dates)]
+    groups += [[(0, m)] for m in range(dates)]
+    pieces = gather_pieces(arrivals, owner_map, groups, dates)
+    rings, mixed, own = pieces[: late - 1], pieces[late - 1 : -dates], pieces[-dates:]
+    far = [swap(ring, "tile", s) for s, ring in enumerate(rings[half - 1 :], half)]
     mixed = [value if m == 0 else swap(value, "date", m) for m, value in enumerate(mixed)]
-    stacked = [jnp.stack([value[i] for value in mixed]) for i in range(tiles - late)]
-    arrivals, stacked = lax.optimization_barrier((arrivals, stacked))
-    last = [(swap(pieces, "tile", late + i), None) for i, pieces in enumerate(stacked)]
-    _, own = gather_pieces(arrivals, owner_map, [], [0], dates)
+    last = [jnp.stack([value[i] for value in mixed]) for i in range(tiles - late)]
+    own, last = lax.optimization_barrier((own, last))
+    close = [swap(ring, "tile", s) for s, ring in enumerate(rings[: half - 1], 1)]
     own = [value if m == 0 else swap(value, "date", m) for m, value in enumerate(own)]
-    prepared = prepare(stacked)
-    close, far = rings[: half - 1], rings[half - 1 :]
-    close, prepared = lax.optimization_barrier((close, prepared))
+    prepared = prepare(last)
+    far, last, first = lax.optimization_barrier((far, last, prepared[0]))
+    prepared = (first,) + prepared[1:]
+    last = [(swap(pieces, "tile", s), None) for s, pieces in enumerate(last, late)]
 
     def cross_dates(ring):
         return [(ring if m == 0 else swap(ring[m : m + 1], "date", m), 0) for m in range(dates)]
@@ -115,11 +103,10 @@
     near = [(value, 0) for value in own]
     for ring in close:
         near += cross_dates(ring)
-    arrays, far = lax.optimization_barrier(([array for array, _ in near], far))
-    near = [(array, n) for array, (_, n) in zip(arrays, near)]
+    middle = []
     for ring in far:
-        last += cross_dates(ring)
-    return use(near, prepared), last, prepared
+        middle += cross_dates(ring)
+    return zip(*[use(pieces, prepared) for pieces in (near, middle, last)]), prepared
 
 
 def with_ones(values):
@@ -150,7 +137,7 @@
     piece_refs, (loc_ref, gain_ref, weight_ref, packed_ref, norm_ref, x_ref, normed_ref) = refs[:count], refs[count:]
     first = 0
     for piece_ref, place in zip(piece_refs, places):
-        x = piece_ref[place]
+        x = piece_ref[...].reshape(-1, piece_ref.shape[-1]) if place is None else piece_ref[place]
         x_ref[first : first + x.shape[0], :] = x
         normed_ref[first : first + x.shape[0], :] = normalize(x, loc_ref, gain_ref)
         first += x.shape[0]
@@ -159,9 +146,11 @@
 
 def project(pieces, location, gain, weight):
     width = weight.shape[0]
-    tokens = sum(piece.shape[1] for piece, _ in pieces)
+    tokens = sum(piece.shape[1] * (piece.shape[0] if n is None else 1) for piece, n in pieces)
     whole = pl.BlockSpec(memory_space=pltpu.VMEM)
-    specs = [pl.BlockSpec((1,) + piece.shape[1:], lambda i: (0, 0, 0)) for piece, _ in pieces]
+    specs = [
+        pl.BlockSpec(piece.shape if n is None else (1,) + piece.shape[1:], lambda i: (0, 0, 0)) for piece, n in pieces
+    ]
     return pl.pallas_call(
         functools.partial(project_kernel, [n for _, n in pieces]),
         grid=(1,),
@@ -179,25 +168,18 @@
     )(*[piece for piece, _ in pieces], location, gain, weight)
 
 
-def encode_kernel(places, order, place_ref, packed_ref, norm_ref, x_ref, *refs):
-    count = len(places)
-    piece_refs, refs = refs[:count], refs[count:]
+def encode_kernel(parts, place_ref, *refs):
+    packed_refs, norm_refs, x_refs = (refs[i * parts : (i + 1) * parts] for i in range(3))
     (
-        loc_ref, gain_ref, weight_ref, out_ref, final_ref, wr_ref, bias_ref, profile_ref,
-        o_ref, last_ref, first_ref, tail_ref, normed_ref, rest_ref, rest_norm_ref, mixed_ref, encoded_ref, reduced_ref
-    ) = refs
-    first = 0
-    for piece_ref, n in zip(piece_refs, places):
-        x = piece_ref[...].reshape(-1, piece_ref.shape[-1]) if n is None else piece_ref[0]
-        tail_ref[first : first + x.shape[0], :] = x
-        normed_ref[first : first + x.shape[0], :] = normalize(x, loc_ref, gain_ref)
-        first += x.shape[0]
-    width = weight_ref.shape[0]
+        loc_ref, out_ref, final_ref, wr_ref, bias_ref, profile_ref,
+        o_ref, last_ref, first_ref, mixed_ref, encoded_ref, reduced_ref
+    ) = refs[3 * parts :]
+    width = out_ref.shape[0]
     head = width // HEADS
     scale = math.log2(math.e) / math.sqrt(head)
-    project_block(weight_ref, normed_ref[...], rest_ref, rest_norm_ref)
-    packed_refs = (packed_ref, rest_ref)
-    norms = jnp.maximum(norm_ref[...], rest_norm_ref[...])
+    norms = norm_refs[0][...]
+    for norm_ref in norm_refs[1:]:
+        norms = jnp.maximum(norms, norm_ref[...])
     small = jnp.max(norms[:HEADS] * norms[HEADS:]) <= (EXPONENT_BOUND / scale) ** 2
 
     def side_by_side(which, n):
@@ -233,7 +215,7 @@
     tiles, dates, strip, _ = encoded_ref.shape
     first = 0
     step = tiles * dates * strip // 4
-    for held_ref in (x_ref, tail_ref):
+    for held_ref in x_refs:
         for row in range(0, held_ref.shape[0], step):
             held = held_ref[row : row + step, :].astype(f32) + loc_ref[...]
             updated = held + mm(mixed_ref[:, first : first + step], out_ref[...], TN)
@@ -247,11 +229,11 @@
         total = total + mm(encoded_ref[:, m].reshape(tiles * strip, width), wr_ref[place_ref[0] ^ m])
     total = 0.5 * total * (1.0 + lax.erf(total * math.sqrt(0.5)))
     halves = range(reduced_ref.shape[0])
-    for n, s in enumerate(order):
+    for s in range(tiles):
         spot = pl.multiple_of((place_ref[1] ^ s) * strip, strip)
         for half in halves:
             lanes = slice(128 * half, 128 * (half + 1))
-            reduced_ref[half, pl.ds(spot, strip), :] = total[n * strip : (n + 1) * strip, lanes]
+            reduced_ref[half, pl.ds(spot, strip), :] = total[s * strip : (s + 1) * strip, lanes]
     for half in halves:
         o_ref[:, 128 * half : 128 * (half + 1)] = reduced_ref[half].astype(bf16)
 
@@ -267,41 +249,29 @@
 
 
 def encode(
-    place, packed, norms, x, last, location, gain, weight, out_weight, final_gain, reduce_weight, reduce_bias, profile,
-    tiles, dates
+    place, packed, norms, x, location, out_weight, final_gain, reduce_weight, reduce_bias, profile, tiles, dates
 ):
-    width = weight.shape[0]
-    tokens = 2 * x.shape[0]
-    rest = tokens - x.shape[0]
+    width = out_weight.shape[0]
+    tokens = sum(part.shape[0] for part in x)
     strip = tokens // (tiles * dates)
     dec = reduce_weight.shape[1]
     patches = tiles * strip
-    quarter = tiles // 4
-    order = list(range(2 * quarter)) + list(range(3 * quarter, tiles)) + list(range(2 * quarter, 3 * quarter))
     sent = jax.ShapeDtypeStruct((3 * PATCHES, dec), bf16)
     whole = pl.BlockSpec(memory_space=pltpu.VMEM)
-    pieces = [
-        pl.BlockSpec(piece.shape if n is None else (1,) + piece.shape[1:], lambda i: (0, 0, 0)) for piece, n in last
-    ]
     return pl.pallas_call(
-        functools.partial(encode_kernel, [n for _, n in last], order),
-        grid=(1,),
-        in_specs=[pl.BlockSpec(memory_space=pltpu.SMEM)] + [whole] * 3 + pieces + [whole] * 8,
+        functools.partial(encode_kernel, len(packed)),
+        in_specs=[pl.BlockSpec(memory_space=pltpu.SMEM)] + [whole] * (3 * len(packed) + 6),
         out_specs=[whole] * 3,
         out_shape=[jax.ShapeDtypeStruct((patches, dec), bf16), sent, sent],
         scratch_shapes=[
-            pltpu.VMEM((rest, width), bf16),
-            pltpu.VMEM((rest, width), bf16),
-            pltpu.VMEM((3 * width, rest), bf16),
-            pltpu.VMEM((2 * HEADS, 128), f32),
             pltpu.VMEM((width, tokens), bf16),
             pltpu.VMEM((tiles, dates, strip, width), bf16),
             pltpu.VMEM((dec // 128, patches, 128), f32),
         ],
-        compiler_params=pltpu.CompilerParams(vmem_limit_bytes=36 * 2**20),
+        compiler_params=pltpu.CompilerParams(vmem_limit_bytes=28 * 2**20),
         name="encode",
     )(
-        place, packed, norms, x, *[piece for piece, _ in last], location, gain, weight, out_weight, final_gain,
+        place, *packed, *norms, *x, location, out_weight, final_gain,
         reduce_weight.reshape(dates, width, dec), reduce_bias, profile,
     )
 
@@ -396,7 +366,12 @@
     return rows, columns, meet.reshape(3, LANES, FEAT * PATCH)
 
 
-def kernels_kernel(up_ref, taps_ref, rows_ref, columns_ref, meet_ref, o_ref, edge_ref, turned_ref, column_ref):
+def prepare_kernel(
+    up_ref, taps_ref, rows_ref, columns_ref, meet_ref, weight_ref,
+    o_ref, edge_ref, held_ref, turned_ref, column_ref, sem
+):
+    load = pltpu.make_async_copy(weight_ref, held_ref, sem)
+    load.start()
     for half in range(turned_ref.shape[0]):
         lanes = slice(128 * half, 128 * (half + 1))
         turned_ref[half] = up_ref[lanes, :].astype(f32).T
@@ -420,25 +395,31 @@
         o_ref[big] = total.astype(bf16)
     edge_ref[0] = mm(spread[2], column_ref[NEAR_PIXEL]).astype(bf16)
     edge_ref[1] = mm(spread[0], column_ref[FAR_PIXEL]).astype(bf16)
-
-
-def decoder_kernels(upsample_weight, class_weight):
+    load.wait()
+
+
+def prepare_weights(upsample_weight, class_weight, qkv_weight):
     channels = upsample_weight.shape[0]
     tables = [jnp.asarray(table, bf16) for table in tap_tables(class_weight.shape[1])]
+    whole = pl.BlockSpec(memory_space=pltpu.VMEM)
     return pl.pallas_call(
-        kernels_kernel,
+        prepare_kernel,
+        in_specs=[whole] * 5 + [pl.BlockSpec(memory_space=pltpu.HBM)],
+        out_specs=[whole] * 3,
         out_shape=[
             jax.ShapeDtypeStruct((SPAN, LANES, channels), bf16),
             jax.ShapeDtypeStruct((2, LANES, channels), bf16),
+            pltpu.VMEM(qkv_weight.shape, bf16),
         ],
         scratch_shapes=[
             pltpu.VMEM((channels // 128, upsample_weight.shape[1], 128), f32),
             pltpu.VMEM((PATCH, FEAT * PATCH, channels), bf16),
+            pltpu.SemaphoreType.DMA,
         ],
-        compiler_params=pltpu.CompilerParams(vmem_limit_bytes=VMEM),
+        compiler_params=pltpu.CompilerParams(vmem_limit_bytes=24 * 2**20),
         cost_estimate=pl.CostEstimate(flops=0, bytes_accessed=0, transcendentals=0),
-        name="decoder_kernels",
-    )(upsample_weight, class_weight, *tables)
+        name="prepare_weights",
+    )(upsample_weight, class_weight, *tables, pltpu.with_memory_space_constraint(qkv_weight, pltpu.HBM))
 
 
 def compose_kernel(
@@ -633,18 +614,19 @@
         profile = blend.reshape(2, TILE_PX).astype(bf16)
         profile = jnp.concatenate([profile[:1] * tile_valid.reshape(1).astype(bf16), profile[1:]], axis=0)
         profile = jnp.pad(profile, ((0, 0), (0, LANES - TILE_PX)))
-        return (location, profile) + tuple(decoder_kernels(up, class_weight))
+        kernels, edges, held_weight = prepare_weights(up, class_weight, qkv_weight)
+        return edges, location, profile, kernels, held_weight
 
     def use(pieces, prepared):
-        return project(pieces, prepared[0], norm_gain[None], qkv_weight)
-
-    (packed, norms, x), last, prepared = exchange(arrivals.reshape(slots, -1, width), owner_map[0], prepare, use)
-    location, profile, kernels, edges = prepared
+        return project(pieces, prepared[1], norm_gain[None], prepared[4])
+
+    (packed, norms, x), prepared = exchange(arrivals.reshape(slots, -1, width), owner_map[0], prepare, use)
+    edges, location, profile, kernels, _ = prepared
     go_last = jnp.where((lax.axis_index("col") == 0) | (lax.axis_size("col") != 2), 1, 0)
     place = jnp.stack([lax.axis_index("date"), lax.axis_index("tile"), go_last]).astype(jnp.int32)
     reduced, to_after, to_before = encode(
-        place, packed, norms, x, last, location, norm_gain[None], qkv_weight, out_weight, final_gain[None],
-        reduce_weight, reduce_bias[None], profile, tiles, dates
+        place, packed, norms, x, location, out_weight, final_gain[None], reduce_weight, reduce_bias[None], profile,
+        tiles, dates
     )
     rims = exchange_rims(reduced, to_after, to_before, profile)
     return compose(reduced, rims, profile, kernels, edges, class_bias, classes)[None]

time: 138 us -> 131 us (0.949)
  Pallas kernels: 68.4 us -> 62.8 us
    pallas_call x4 -> x3, Pallas kernels: 53.8 us -> 40.9 us  [the longest x1 34.5 us: encode(): pl.pallas_call(functools.partial(encode_kernel, len(packed)), in_specs=[p...]
    pallas_call x1 -> x3, Pallas kernels: 6.1 us -> 13.4 us  [project(): pl.pallas_call(functools.partial(project_kernel, [n for _, n in pieces]),...]
    ppermute x1, starting transfers between devices: 11.1 us -> 8.34 us  [exchange_rims(): above = lax.ppermute(lines(UPPER), ('date', 'tile'), forward(rows))]
    ppermute x16, starting transfers between devices: 17.9 us -> 20.5 us  [swap(): lax.ppermute(value, axis, [(i, i ^ mask) for i in range(lax.axis_size(axi...]
    unnamed x40 -> x54, local copies, waits for them, and re-layouts: 7.11 us -> 7.38 us
  transfers between devices with their start and end apart: 18 -> 18, of which waited for: 6 -> 8; matrix products, arithmetic and copies ran while one was open for 5% -> 5% of each run, Pallas kernels for 10% -> 11%
where the time goes in v4:
time: 131 us; the launch traced here: 130 us
  Pallas kernels  62.8 us (48%)
  starting transfers between devices  30.3 us (23%)
  waiting for transfers between devices  21.3 us (16%)
  local copies, waits for them, and re-layouts  11.5 us (9%)
  other arithmetic  2.78 us (2%)
  between operations  1.66 us (1%)
    pallas_call x1, Pallas kernels, encode(): pl.pallas_call(functools.partial(encode_kernel, len(packed)), in_specs=[p...  34.5 us
    ppermute x16, starting transfers between devices, swap(): lax.ppermute(value, axis, [(i, i ^ mask) for i in range(lax.axis_size(axi...  20.5 us
    ppermute x16, waiting for transfers between devices, swap(): lax.ppermute(value, axis, [(i, i ^ mask) for i in range(lax.axis_size(axi...  17.6 us
    pallas_call x3, Pallas kernels, project(): pl.pallas_call(functools.partial(project_kernel, [n for _, n in pieces]),...  13.4 us
    pallas_call x1, Pallas kernels, compose(): pl.pallas_call(functools.partial(compose_kernel, classes), in_specs=[whol...  8.53 us
    ppermute x1, starting transfers between devices, exchange_rims(): above = lax.ppermute(lines(UPPER), ('date', 'tile'), forward(rows))  8.34 us
    unnamed x54, local copies, waits for them, and re-layouts  7.38 us
    pallas_call x1, Pallas kernels, prepare_weights(): pl.pallas_call(prepare_kernel, in_specs=[whole] * 5 + [pl.BlockSpec(memor...  4.63 us
  transfers between devices with their start and end apart: 18, of which 8 were waited for; matrix products, arithmetic and copies ran while one was open for 5% of the time, Pallas kernels for 11%

profile of v4, /device:TPU:0, one launch (start us, length us, event | category | flops | bytes accessed | tf_op | source)
XLA Modules:
  0.0 130.5 jit_solution(6806748965309771729)
XLA Ops:
  0.0 1.8 %copy-done.3 = bf16[1,16,1,1,4,16,1280]{6,5,4,3,2,1,0:T(8,128)(2,1)S(1)} copy-done((bf16[1,16,1,1,4,16,1280]{6,5,4,3,2,1,0:T(8,128)(2,1)S(1)}, bf16[1,16,1,1,4,16,1280]{6,5,4,3,2,1,0:T(8,128)(2,1)}, u32[]{:S(2)}) %copy-start.3) | copy-done | bytes 2621464
  1.8 0.7 copy-done.15
  2.4 1.8 %gather_pieces.1 = (bf16[4,64,1280]{2,1,0:T(8,128)(2,1)}, bf16[4,64,1280]{2,1,0:T(8,128)(2,1)}, bf16[1,64,1280]{2,1,0:T(8,128)(2,1)S(1)}, bf16[1,64,1280]{2,1,0:...) custom-call(s32[16]{0:T(128)S(1)} %bitcast.20, ...), custom_call_target="tpu_custom_call" | custom-call | tf_op jit(solution)/shard_map/gather_pieces/pallas_call | solution.py:65
  4.3 0.7 copy-done.16
  4.9 4.0 %collective-permute-start.10 = (bf16[4,64,1280]{2,1,0:T(8,128)(2,1)}, bf16[4,64,1280]{2,1,0:T(8,128)(2,1)S(1)}, u32[]{:S(2)}, u32[]{:S(2)}) collective-permute-start(bf16[4,64,1280]{2,1,0:T(8,128)(2,1)} %get-tuple-element.58), channel_id=1, source_target_pairs={{0,4},{2,6},{4,0},{6,2},{1,5},{3,7},{5,1},{7,3},{8,12},{10,14},{12... | collective-permute-start | bytes 1966088 | tf_op jit(solution)/shard_map/ppermute | solution.py:78
  9.0 0.7 collective-permute-start.2
  9.6 0.9 collective-permute-start.1
  10.5 0.3 collective-permute-start
  10.8 1.6 %collective-permute-start.6 = (bf16[4,64,1280]{2,1,0:T(8,128)(2,1)}, bf16[4,64,1280]{2,1,0:T(8,128)(2,1)S(1)}, u32[]{:S(2)}, u32[]{:S(2)}) collective-permute-start(bf16[4,64,1280]{2,1,0:T(8,128)(2,1)} %get-tuple-element.52), channel_id=1, source_target_pairs={{0,2},{2,0},{4,6},{6,4},{1,3},{3,1},{5,7},{7,5},{8,10},{10,8},{12,... | collective-permute-start | bytes 1966088 | tf_op jit(solution)/shard_map/ppermute | solution.py:78
  13.1 0.6 broadcast_in_dim.23.refs_11_
  13.7 0.6 broadcast_in_dim.24.refs_13_
  14.9 0.6 pad_add_fusion.place_ref
  15.5 3.4 %collective-permute-done.1 = bf16[1,64,1280]{2,1,0:T(8,128)(2,1)S(1)} collective-permute-done((bf16[1,64,1280]{2,1,0:T(8,128)(2,1)S(1)}, bf16[1,64,1280]{2,1,0:T(8,128)(2,1)S(1)}, u32[]{:S(2)}, u32[]{:S(2)}) %collective-permute-start.1) | collective-permute-done | bytes 163872 | tf_op jit(solution)/shard_map/ppermute | solution.py:78
  19.0 0.9 pad_maximum_fusion
  19.9 0.1 collective-permute-start.3
  20.0 1.3 collective-permute-start.4
  21.2 2.7 %copy.23.up_ref = bf16[256,3136]{1,0:T(8,128)(2,1)S(1)} copy(bf16[256,3136]{0,1:T(8,128)(2,1)} %param.34) | data formatting | bytes 3211264 | tf_op jit(solution)/shard_map/optimization_barrier | solution.py:612
  23.9 0.7 convert_element_type.18
  24.6 0.8 copy-done.8
  25.5 0.8 copy-done.9
  26.2 0.7 copy-done.12
  26.9 4.6 %prepare_weights.1 = (bf16[16,256,256]{2,1,0:T(8,128)(2,1)S(1)}, bf16[2,256,256]{2,1,0:T(8,128)(2,1)S(1)}, bf16[1280,3840]{1,0:T(8,128)(2,1)S(1)}) custom-call(bf16[256,3136]{1,0:T(8,128)(2,1)S(1)} %copy.23.up_ref, bf16[9,13,16]{2,1,0:T(8,128)(2,1)S(1)} %copy-done.9, bf16[256,13]{1,0:T(8,128)(2,1)S(1)} %copy-done.8, bf16[16,224]{1,0:T(8,128)(2,1)S(1)} %copy-done.12, ...), custom_call_target="tpu_custom_call" | custom-call | tf_op jit(solution)/shard_map/prepare_weights/pallas_call | solution.py:405
  31.6 1.3 %copy-done.4 = bf16[16,256,256]{2,1,0:T(8,128)(2,1)} copy-done((bf16[16,256,256]{2,1,0:T(8,128)(2,1)}, bf16[16,256,256]{2,1,0:T(8,128)(2,1)S(1)}, u32[]{:S(2)}) %copy-start.4) | copy-done | bytes 2097176
  32.9 0.1 fusion.2.refs_8_.refs_4_.refs_1_.refs_9_
  33.1 5.0 %collective-permute-done.10.refs_0_ = bf16[4,64,1280]{2,1,0:T(8,128)(2,1)S(1)} collective-permute-done((bf16[4,64,1280]{2,1,0:T(8,128)(2,1)}, bf16[4,64,1280]{2,1,0:T(8,128)(2,1)S(1)}, u32[]{:S(2)}, u32[]{:S(2)}) %collective-permute-start.10) | collective-permute-done | bytes 655392 | tf_op jit(solution)/shard_map/ppermute | solution.py:78
  38.2 1.6 %collective-permute-start.12 = (bf16[1,64,1280]{2,1,0:T(8,128)(2,1)S(1)}, bf16[1,64,1280]{2,1,0:T(8,128)(2,1)S(1)}, u32[]{:S(2)}, u32[]{:S(2)}) collective-permute-start(bf16[1,64,1280]{2,1,0:T(8,128)(2,1)S(1)} %get-tuple-element.76), channel_id=1, source_target_pairs={{0,16},{8,24},{16,0},{24,8},{1,17},{9,25},{17,1},{25,9},{2,18},{10... | collective-permute-start | bytes 491528 | tf_op jit(solution)/shard_map/ppermute | solution.py:78
  39.8 0.3 collective-permute-start.13
  40.0 0.7 collective-permute-done.6.refs_4_
  40.7 2.9 %collective-permute-start.14 = (bf16[4,64,1280]{2,1,0:T(8,128)(2,1)S(1)}, bf16[4,64,1280]{2,1,0:T(8,128)(2,1)S(1)}, u32[]{:S(2)}, u32[]{:S(2)}) collective-permute-start(bf16[4,64,1280]{2,1,0:T(8,128)(2,1)S(1)} %copy-done.18), channel_id=1, source_target_pairs={{0,6},{2,4},{4,2},{6,0},{1,7},{3,5},{5,3},{7,1},{8,14},{10,12},{12... | collective-permute-start | bytes 1966088 | tf_op jit(solution)/shard_map/ppermute | solution.py:78
  43.6 1.2 collective-permute-start.5
  44.9 0.4 collective-permute-start.7
  45.3 1.5 %collective-permute-start.8 = (bf16[1,64,1280]{2,1,0:T(8,128)(2,1)S(1)}, bf16[1,64,1280]{2,1,0:T(8,128)(2,1)S(1)}, u32[]{:S(2)}, u32[]{:S(2)}) collective-permute-start(bf16[1,64,1280]{2,1,0:T(8,128)(2,1)S(1)} %get-tuple-element.79), channel_id=1, source_target_pairs={{0,16},{8,24},{16,0},{24,8},{1,17},{9,25},{17,1},{25,9},{2,18},{10... | collective-permute-start | bytes 491528 | tf_op jit(solution)/shard_map/ppermute | solution.py:78
  46.8 1.1 collective-permute-done.13.refs_3_
  47.8 2.2 %collective-permute-start.9 = (bf16[1,64,1280]{2,1,0:T(8,128)(2,1)S(1)}, bf16[1,64,1280]{2,1,0:T(8,128)(2,1)S(1)}, u32[]{:S(2)}, u32[]{:S(2)}) collective-permute-start(bf16[1,64,1280]{2,1,0:T(8,128)(2,1)S(1)} %get-tuple-element.78), channel_id=1, source_target_pairs={{0,24},{8,16},{16,8},{24,0},{1,25},{9,17},{17,9},{25,1},{2,26},{10... | collective-permute-start | bytes 491528 | tf_op jit(solution)/shard_map/ppermute | solution.py:78
  50.0 3.1 %project.4 = (bf16[3840,256]{1,0:T(8,128)(2,1)S(1)}, f32[32,128]{1,0:T(8,128)S(1)}, bf16[256,1280]{1,0:T(8,128)(2,1)S(1)}) custom-call(bf16[4,64,1280]{2,1,0:T(8,128)(2,1)S(1)} %collective-permute-done.10.refs_0_, bf16[1,64,1280]{2,1,0:T(8,128)(2,1)S(1)} %collective-permute-done.11.refs_1_, bf16[1,64,1280]{2,1,0:T(8,128)(2,1)S(1)} %collective-permute-done.12.refs_2_, ...), custom_call_target="tpu_custom_call" | custom-call | tf_op jit(solution)/shard_map/project/pallas_call | solution.py:154
  53.2 2.6 %collective-permute-done.8.refs_6_ = bf16[1,64,1280]{2,1,0:T(8,128)(2,1)S(1)} collective-permute-done((bf16[1,64,1280]{2,1,0:T(8,128)(2,1)S(1)}, bf16[1,64,1280]{2,1,0:T(8,128)(2,1)S(1)}, u32[]{:S(2)}, u32[]{:S(2)}) %collective-permute-start.8) | collective-permute-done | bytes 163872 | tf_op jit(solution)/shard_map/ppermute | solution.py:78
  55.8 2.6 %collective-permute-done.9.refs_7_ = bf16[1,64,1280]{2,1,0:T(8,128)(2,1)S(1)} collective-permute-done((bf16[1,64,1280]{2,1,0:T(8,128)(2,1)S(1)}, bf16[1,64,1280]{2,1,0:T(8,128)(2,1)S(1)}, u32[]{:S(2)}, u32[]{:S(2)}) %collective-permute-start.9) | collective-permute-done | bytes 163872 | tf_op jit(solution)/shard_map/ppermute | solution.py:78
  58.4 7.0 %project.3 = (bf16[3840,512]{1,0:T(8,128)(2,1)S(1)}, f32[32,128]{1,0:T(8,128)S(1)}, bf16[512,1280]{1,0:T(8,128)(2,1)S(1)}) custom-call(bf16[1,64,1280]{2,1,0:T(8,128)(2,1)S(1)} %get-tuple-element.48.refs_0_, bf16[1,64,1280]{2,1,0:T(8,128)(2,1)} %collective-permute-done.3.refs_1_, bf16[1,64,1280]{2,1,0:T(8,128)(2,1)} %collective-permute-done.4.refs_2_, ...), custom_call_target="tpu_custom_call" | custom-call | tf_op jit(solution)/shard_map/project/pallas_call | solution.py:154
  65.4 3.3 %project.5 = (bf16[3840,256]{1,0:T(8,128)(2,1)S(1)}, f32[32,128]{1,0:T(8,128)S(1)}, bf16[256,1280]{1,0:T(8,128)(2,1)S(1)}) custom-call(bf16[4,64,1280]{2,1,0:T(8,128)(2,1)S(1)} %collective-permute-done.14.refs_0_, f32[1,1280]{1,0:T(1,128)S(1)} %fusion.2.refs_8_.refs_4_.refs_1_.refs_9_, bf16[1,1280]{1,0:T(2,128)(2,1)S(1)} %broadcast_in_dim.22.refs_9_.refs_5_.refs_2_, ...), custom_call_target="tpu_custom_call" | custom-call | tf_op jit(solution)/shard_map/project/pallas_call | solution.py:154
  68.8 34.5 %encode.1 = (bf16[256,256]{1,0:T(8,128)(2,1)S(1)}, bf16[48,256]{1,0:T(8,128)(2,1)S(1)}, bf16[48,256]{1,0:T(8,128)(2,1)}) custom-call(s32[3]{0:T(128)S(1)} %copy-done.13, bf16[3840,512]{1,0:T(8,128)(2,1)S(1)} %get-tuple-element.57.refs_0_, bf16[3840,256]{1,0:T(8,128)(2,1)S(1)} %get-tuple-element.61.refs_1_, bf16[3840,256]{1,0:T(8,128)(2,1)S(1)} %get-tuple-element.63.refs_2_, ...), custom_call_target="tpu_custom_call" | custom-call | tf_op jit(solution)/shard_map/encode/pallas_call | solution.py:261
  103.2 1.6 %collective-permute-start.15 = (bf16[48,256]{1,0:T(8,128)(2,1)S(1)}, bf16[48,256]{1,0:T(8,128)(2,1)S(1)}, u32[]{:S(2)}, u32[]{:S(2)}) collective-permute-start(bf16[48,256]{1,0:T(8,128)(2,1)S(1)} %get-tuple-element.72), channel_id=1, source_target_pairs={{0,1},{1,0},{2,3},{3,2},{4,5},{5,4},{6,7},{7,6},{8,9},{9,8},{10,11... | collective-permute-start | bytes 73736 | tf_op jit(solution)/shard_map/ppermute | solution.py:78
  104.8 2.2 %collective-permute-done.15 = bf16[48,256]{1,0:T(8,128)(2,1)S(1)} collective-permute-done((bf16[48,256]{1,0:T(8,128)(2,1)S(1)}, bf16[48,256]{1,0:T(8,128)(2,1)S(1)}, u32[]{:S(2)}, u32[]{:S(2)}) %collective-permute-start.15) | collective-permute-done | bytes 24608 | tf_op jit(solution)/shard_map/ppermute | solution.py:78
  107.2 8.3 %collective-permute-start.16 = (bf16[48,256]{1,0:T(8,128)(2,1)S(1)}, bf16[48,256]{1,0:T(8,128)(2,1)S(1)}, u32[]{:S(2)}, u32[]{:S(2)}) collective-permute-start(bf16[48,256]{1,0:T(8,128)(2,1)S(1)} %concatenate.12), channel_id=1, source_target_pairs={{0,2},{2,4},{4,6},{6,8},{8,10},{10,12},{12,14},{14,16},{16,18},{18... | collective-permute-start | bytes 73736 | tf_op jit(solution)/shard_map/ppermute | solution.py:560
  115.6 1.5 %collective-permute-start.17 = (bf16[48,256]{1,0:T(8,128)(2,1)S(1)}, bf16[48,256]{1,0:T(8,128)(2,1)S(1)}, u32[]{:S(2)}, u32[]{:S(2)}) collective-permute-start(bf16[48,256]{1,0:T(8,128)(2,1)S(1)} %concatenate.13), channel_id=1, source_target_pairs={{2,0},{4,2},{6,4},{8,6},{10,8},{12,10},{14,12},{16,14},{18,16},{20... | collective-permute-start | bytes 73736 | tf_op jit(solution)/shard_map/ppermute | solution.py:561
  117.1 0.5 convert_element_type.20.bias_ref
  117.7 3.6 %collective-permute-done.17.below_ref = bf16[48,256]{1,0:T(8,128)(2,1)S(1)} collective-permute-done((bf16[48,256]{1,0:T(8,128)(2,1)S(1)}, bf16[48,256]{1,0:T(8,128)(2,1)S(1)}, u32[]{:S(2)}, u32[]{:S(2)}) %collective-permute-start.17) | collective-permute-done | bytes 24608 | tf_op jit(solution)/shard_map/ppermute | solution.py:561
  121.4 0.6 copy-done.22
  121.9 8.5 %compose.1 = f32[13,192,192]{2,1,0:T(8,128)} custom-call(bf16[256,256]{1,0:T(8,128)(2,1)} %copy-done.7, bf16[48,256]{1,0:T(8,128)(2,1)} %copy-done.20, bf16[48,256]{1,0:T(8,128)(2,1)} %copy-done.19, bf16[48,256]{1,0:T(8,128)(2,1)} %copy-done.21, bf16[48,256]{1,0:T(8,128)(2,1)} %copy-done.22, bf16[2,256]{1,0:T(2,128)(2,1)} %copy-done.10, ...), custom_call_target="tpu_custom_call" | custom-call | tf_op jit(solution)/shard_map/compose/pallas_call | solution.py:570
  (70 shorter events, 0.4 us)
Async XLA Ops:
  0.0 32.9 %copy-start = (bf16[16,1280]{1,0:T(8,128)(2,1)S(1)}, bf16[16,1280]{1,0:T(8,128)(2,1)}, u32[]{:S(2)}) copy-start(bf16[16,1280]{1,0:T(8,128)(2,1)} %param.27) | copy-start | bytes 122884
  0.0 13.7 %copy-start.25 = (bf16[256]{0:T(256)(128)(2,1)S(1)}, bf16[256]{0:T(256)(128)(2,1)}, u32[]{:S(2)}) copy-start(bf16[256]{0:T(256)(128)(2,1)} %param.33) | copy-start | bytes 1540
  0.0 1.8 %copy-start.3 = (bf16[1,16,1,1,4,16,1280]{6,5,4,3,2,1,0:T(8,128)(2,1)S(1)}, bf16[1,16,1,1,4,16,1280]{6,5,4,3,2,1,0:T(8,128)(2,1)}, u32[]{:S(2)}) copy-start(bf16[1,16,1,1,4,16,1280]{6,5,4,3,2,1,0:T(8,128)(2,1)} %param.22) | copy-start | bytes 7864324
  1.8 0.7 copy-start.15
  2.4 10.6 %copy-start.23 = (bf16[1280]{0:T(1024)(128)(2,1)S(1)}, bf16[1280]{0:T(1024)(128)(2,1)}, u32[]{:S(2)}) copy-start(bf16[1280]{0:T(1024)(128)(2,1)} %param.28) | copy-start | bytes 7684
  2.4 10.6 %copy-start.24 = (bf16[1280]{0:T(1024)(128)(2,1)S(1)}, bf16[1280]{0:T(1024)(128)(2,1)}, u32[]{:S(2)}) copy-start(bf16[1280]{0:T(1024)(128)(2,1)} %param.31) | copy-start | bytes 7684
  4.3 0.7 copy-start.16
  4.9 19.7 %copy-start.5 = (bf16[3,256,224]{2,1,0:T(8,128)(2,1)S(1)}, bf16[3,256,224]{2,1,0:T(8,128)(2,1)}, u32[]{:S(2)}) copy-start(bf16[3,256,224]{2,1,0:T(8,128)(2,1)} %constant.34.clone.meet_ref) | copy-start | bytes 1032196
  4.9 33.1 %collective-permute-start.10 = (bf16[4,64,1280]{2,1,0:T(8,128)(2,1)}, bf16[4,64,1280]{2,1,0:T(8,128)(2,1)S(1)}, u32[]{:S(2)}, u32[]{:S(2)}) collective-permute-start(bf16[4,64,1280]{2,1,0:T(8,128)(2,1)} %get-tuple-element.58), channel_id=1, source_target_pairs={{0,4},{2,6},{4,0},{6,2},{1,5},{3,7},{5,1},{7,3},{8,12},{10,14},{12... | collective-permute-start | bytes 1966088 | tf_op jit(solution)/shard_map/ppermute | solution.py:78
  9.0 6.6 %collective-permute-start.2 = (bf16[1,64,1280]{2,1,0:T(8,128)(2,1)S(1)}, bf16[1,64,1280]{2,1,0:T(8,128)(2,1)S(1)}, u32[]{:S(2)}, u32[]{:S(2)}) collective-permute-start(bf16[1,64,1280]{2,1,0:T(8,128)(2,1)S(1)} %get-tuple-element.47), channel_id=1, source_target_pairs={{0,24},{8,16},{16,8},{24,0},{1,25},{9,17},{17,9},{25,1},{2,26},{10... | collective-permute-start | bytes 491528 | tf_op jit(solution)/shard_map/ppermute | solution.py:78
  9.6 9.4 %collective-permute-start.1 = (bf16[1,64,1280]{2,1,0:T(8,128)(2,1)S(1)}, bf16[1,64,1280]{2,1,0:T(8,128)(2,1)S(1)}, u32[]{:S(2)}, u32[]{:S(2)}) collective-permute-start(bf16[1,64,1280]{2,1,0:T(8,128)(2,1)S(1)} %get-tuple-element.46), channel_id=1, source_target_pairs={{0,16},{8,24},{16,0},{24,8},{1,17},{9,25},{17,1},{25,9},{2,18},{10... | collective-permute-start | bytes 491528 | tf_op jit(solution)/shard_map/ppermute | solution.py:78
  10.5 8.5 %collective-permute-start = (bf16[1,64,1280]{2,1,0:T(8,128)(2,1)S(1)}, bf16[1,64,1280]{2,1,0:T(8,128)(2,1)S(1)}, u32[]{:S(2)}, u32[]{:S(2)}) collective-permute-start(bf16[1,64,1280]{2,1,0:T(8,128)(2,1)S(1)} %get-tuple-element.45), channel_id=1, source_target_pairs={{0,8},{8,0},{16,24},{24,16},{1,9},{9,1},{17,25},{25,17},{2,10},{10... | collective-permute-start | bytes 491528 | tf_op jit(solution)/shard_map/ppermute | solution.py:78
  10.8 29.9 %collective-permute-start.6 = (bf16[4,64,1280]{2,1,0:T(8,128)(2,1)}, bf16[4,64,1280]{2,1,0:T(8,128)(2,1)S(1)}, u32[]{:S(2)}, u32[]{:S(2)}) collective-permute-start(bf16[4,64,1280]{2,1,0:T(8,128)(2,1)} %get-tuple-element.52), channel_id=1, source_target_pairs={{0,2},{2,0},{4,6},{6,4},{1,3},{3,1},{5,7},{7,5},{8,10},{10,8},{12,... | collective-permute-start | bytes 1966088 | tf_op jit(solution)/shard_map/ppermute | solution.py:78
  19.9 19.9 %collective-permute-start.3 = (bf16[1,64,1280]{2,1,0:T(8,128)(2,1)}, bf16[1,64,1280]{2,1,0:T(8,128)(2,1)}, u32[]{:S(2)}, u32[]{:S(2)}) collective-permute-start(bf16[1,64,1280]{2,1,0:T(8,128)(2,1)} %get-tuple-element.49), channel_id=1, source_target_pairs={{0,8},{8,0},{16,24},{24,16},{1,9},{9,1},{17,25},{25,17},{2,10},{10... | collective-permute-start | bytes 491528 | tf_op jit(solution)/shard_map/ppermute | solution.py:78
  20.0 23.7 %collective-permute-start.4 = (bf16[1,64,1280]{2,1,0:T(8,128)(2,1)}, bf16[1,64,1280]{2,1,0:T(8,128)(2,1)}, u32[]{:S(2)}, u32[]{:S(2)}) collective-permute-start(bf16[1,64,1280]{2,1,0:T(8,128)(2,1)} %get-tuple-element.50), channel_id=1, source_target_pairs={{0,16},{8,24},{16,0},{24,8},{1,17},{9,25},{17,1},{25,9},{2,18},{10... | collective-permute-start | bytes 491528 | tf_op jit(solution)/shard_map/ppermute | solution.py:78
  24.6 0.8 copy-start.8
  25.5 0.8 copy-start.9
  26.2 0.7 copy-start.12
  26.9 13.8 %copy-start.18 = (bf16[4,64,1280]{2,1,0:T(8,128)(2,1)S(1)}, bf16[4,64,1280]{2,1,0:T(8,128)(2,1)}, u32[]{:S(2)}) copy-start(bf16[4,64,1280]{2,1,0:T(8,128)(2,1)} %pad_maximum_fusion) | copy-start | bytes 1966084
  26.9 16.7 %copy-start.17 = (bf16[1,64,1280]{2,1,0:T(8,128)(2,1)S(1)}, bf16[1,64,1280]{2,1,0:T(8,128)(2,1)}, u32[]{:S(2)}) copy-start(bf16[1,64,1280]{2,1,0:T(8,128)(2,1)} %copy-done.16) | copy-start | bytes 491524
  31.6 1.4 %copy-start.4 = (bf16[16,256,256]{2,1,0:T(8,128)(2,1)}, bf16[16,256,256]{2,1,0:T(8,128)(2,1)S(1)}, u32[]{:S(2)}) copy-start(bf16[16,256,256]{2,1,0:T(8,128)(2,1)S(1)} %get-tuple-element.73.m_ref) | copy-start | bytes 6291460
  32.9 20.2 %copy-start.6 = (bf16[2,256,256]{2,1,0:T(8,128)(2,1)}, bf16[2,256,256]{2,1,0:T(8,128)(2,1)S(1)}, u32[]{:S(2)}) copy-start(bf16[2,256,256]{2,1,0:T(8,128)(2,1)S(1)} %get-tuple-element.74.edge_ref) | copy-start | bytes 786436
  38.1 6.8 %collective-permute-start.11 = (bf16[1,64,1280]{2,1,0:T(8,128)(2,1)S(1)}, bf16[1,64,1280]{2,1,0:T(8,128)(2,1)S(1)}, u32[]{:S(2)}, u32[]{:S(2)}) collective-permute-start(bf16[1,64,1280]{2,1,0:T(8,128)(2,1)S(1)} %get-tuple-element.77), channel_id=1, source_target_pairs={{0,8},{8,0},{16,24},{24,16},{1,9},{9,1},{17,25},{25,17},{2,10},{10... | collective-permute-start | bytes 491528 | tf_op jit(solution)/shard_map/ppermute | solution.py:78
  38.2 7.2 %collective-permute-start.12 = (bf16[1,64,1280]{2,1,0:T(8,128)(2,1)S(1)}, bf16[1,64,1280]{2,1,0:T(8,128)(2,1)S(1)}, u32[]{:S(2)}, u32[]{:S(2)}) collective-permute-start(bf16[1,64,1280]{2,1,0:T(8,128)(2,1)S(1)} %get-tuple-element.76), channel_id=1, source_target_pairs={{0,16},{8,24},{16,0},{24,8},{1,17},{9,25},{17,1},{25,9},{2,18},{10... | collective-permute-start | bytes 491528 | tf_op jit(solution)/shard_map/ppermute | solution.py:78
  39.8 8.1 %collective-permute-start.13 = (bf16[1,64,1280]{2,1,0:T(8,128)(2,1)S(1)}, bf16[1,64,1280]{2,1,0:T(8,128)(2,1)S(1)}, u32[]{:S(2)}, u32[]{:S(2)}) collective-permute-start(bf16[1,64,1280]{2,1,0:T(8,128)(2,1)S(1)} %get-tuple-element.75), channel_id=1, source_target_pairs={{0,24},{8,16},{16,8},{24,0},{1,25},{9,17},{17,9},{25,1},{2,26},{10... | collective-permute-start | bytes 491528 | tf_op jit(solution)/shard_map/ppermute | solution.py:78
  40.7 24.7 %collective-permute-start.14 = (bf16[4,64,1280]{2,1,0:T(8,128)(2,1)S(1)}, bf16[4,64,1280]{2,1,0:T(8,128)(2,1)S(1)}, u32[]{:S(2)}, u32[]{:S(2)}) collective-permute-start(bf16[4,64,1280]{2,1,0:T(8,128)(2,1)S(1)} %copy-done.18), channel_id=1, source_target_pairs={{0,6},{2,4},{4,2},{6,0},{1,7},{3,5},{5,3},{7,1},{8,14},{10,12},{12... | collective-permute-start | bytes 1966088 | tf_op jit(solution)/shard_map/ppermute | solution.py:78
  43.6 9.5 %collective-permute-start.5 = (bf16[1,64,1280]{2,1,0:T(8,128)(2,1)S(1)}, bf16[1,64,1280]{2,1,0:T(8,128)(2,1)S(1)}, u32[]{:S(2)}, u32[]{:S(2)}) collective-permute-start(bf16[1,64,1280]{2,1,0:T(8,128)(2,1)S(1)} %copy-done.17), channel_id=1, source_target_pairs={{0,24},{8,16},{16,8},{24,0},{1,25},{9,17},{17,9},{25,1},{2,26},{10... | collective-permute-start | bytes 491528 | tf_op jit(solution)/shard_map/ppermute | solution.py:78
  44.9 8.3 %collective-permute-start.7 = (bf16[1,64,1280]{2,1,0:T(8,128)(2,1)S(1)}, bf16[1,64,1280]{2,1,0:T(8,128)(2,1)S(1)}, u32[]{:S(2)}, u32[]{:S(2)}) collective-permute-start(bf16[1,64,1280]{2,1,0:T(8,128)(2,1)S(1)} %get-tuple-element.80), channel_id=1, source_target_pairs={{0,8},{8,0},{16,24},{24,16},{1,9},{9,1},{17,25},{25,17},{2,10},{10... | collective-permute-start | bytes 491528 | tf_op jit(solution)/shard_map/ppermute | solution.py:78
  45.3 10.4 %collective-permute-start.8 = (bf16[1,64,1280]{2,1,0:T(8,128)(2,1)S(1)}, bf16[1,64,1280]{2,1,0:T(8,128)(2,1)S(1)}, u32[]{:S(2)}, u32[]{:S(2)}) collective-permute-start(bf16[1,64,1280]{2,1,0:T(8,128)(2,1)S(1)} %get-tuple-element.79), channel_id=1, source_target_pairs={{0,16},{8,24},{16,0},{24,8},{1,17},{9,25},{17,1},{25,9},{2,18},{10... | collective-permute-start | bytes 491528 | tf_op jit(solution)/shard_map/ppermute | solution.py:78
  47.8 10.5 %collective-permute-start.9 = (bf16[1,64,1280]{2,1,0:T(8,128)(2,1)S(1)}, bf16[1,64,1280]{2,1,0:T(8,128)(2,1)S(1)}, u32[]{:S(2)}, u32[]{:S(2)}) collective-permute-start(bf16[1,64,1280]{2,1,0:T(8,128)(2,1)S(1)} %get-tuple-element.78), channel_id=1, source_target_pairs={{0,24},{8,16},{16,8},{24,0},{1,25},{9,17},{17,9},{25,1},{2,26},{10... | collective-permute-start | bytes 491528 | tf_op jit(solution)/shard_map/ppermute | solution.py:78
  50.0 65.5 %copy-start.10 = (bf16[2,256]{1,0:T(2,128)(2,1)}, bf16[2,256]{1,0:T(2,128)(2,1)S(1)}, u32[]{:S(2)}) copy-start(bf16[2,256]{1,0:T(2,128)(2,1)S(1)} %fusion.5.refs_14_.profile_ref) | copy-start | bytes 3076
  65.3 3.4 %copy-start.1 = (bf16[1280,1280]{1,0:T(8,128)(2,1)S(1)}, bf16[1280,1280]{1,0:T(8,128)(2,1)}, u32[]{:S(2)}) copy-start(bf16[1280,1280]{1,0:T(8,128)(2,1)} %refs_10_.1) | copy-start | bytes 9830404
  65.4 3.4 %copy-start.2 = (bf16[5120,256]{1,0:T(8,128)(2,1)S(1)}, bf16[5120,256]{1,0:T(8,128)(2,1)}, u32[]{:S(2)}) copy-start(bf16[5120,256]{1,0:T(8,128)(2,1)} %param.32) | copy-start | bytes 7864324
  65.4 3.4 %copy-start.11 = (bf16[1,1280]{1,0:T(2,128)(2,1)S(1)}, bf16[1,1280]{1,0:T(2,128)(2,1)}, u32[]{:S(2)}) copy-start(bf16[1,1280]{1,0:T(2,128)(2,1)} %broadcast_in_dim.23.refs_11_) | copy-start | bytes 7684
  65.4 3.4 %copy-start.13 = (s32[3]{0:T(128)S(1)}, s32[3]{0:T(128)}, u32[]{:S(2)}) copy-start(s32[3]{0:T(128)} %pad_add_fusion.place_ref) | copy-start | bytes 40
  65.4 3.4 %copy-start.14 = (bf16[1,256]{1,0:T(2,128)(2,1)S(1)}, bf16[1,256]{1,0:T(2,128)(2,1)}, u32[]{:S(2)}) copy-start(bf16[1,256]{1,0:T(2,128)(2,1)} %broadcast_in_dim.24.refs_13_) | copy-start | bytes 1540
  68.8 48.4 %copy-start.26 = (bf16[13]{0:T(256)(128)(2,1)S(1)}, bf16[13]{0:T(256)(128)(2,1)}, u32[]{:S(2)}) copy-start(bf16[13]{0:T(256)(128)(2,1)} %param.36) | copy-start | bytes 82
  103.2 18.1 %copy-start.7 = (bf16[256,256]{1,0:T(8,128)(2,1)}, bf16[256,256]{1,0:T(8,128)(2,1)S(1)}, u32[]{:S(2)}) copy-start(bf16[256,256]{1,0:T(8,128)(2,1)S(1)} %get-tuple-element.71.own_ref) | copy-start | bytes 393220
  103.2 3.8 %collective-permute-start.15 = (bf16[48,256]{1,0:T(8,128)(2,1)S(1)}, bf16[48,256]{1,0:T(8,128)(2,1)S(1)}, u32[]{:S(2)}, u32[]{:S(2)}) collective-permute-start(bf16[48,256]{1,0:T(8,128)(2,1)S(1)} %get-tuple-element.72), channel_id=1, source_target_pairs={{0,1},{1,0},{2,3},{3,2},{4,5},{5,4},{6,7},{7,6},{8,9},{9,8},{10,11... | collective-permute-start | bytes 73736 | tf_op jit(solution)/shard_map/ppermute | solution.py:78
  107.1 14.3 %copy-start.19 = (bf16[48,256]{1,0:T(8,128)(2,1)}, bf16[48,256]{1,0:T(8,128)(2,1)S(1)}, u32[]{:S(2)}) copy-start(bf16[48,256]{1,0:T(8,128)(2,1)S(1)} %get-tuple-element.99.after_ref) | copy-start | bytes 73732
  107.1 14.3 %copy-start.20 = (bf16[48,256]{1,0:T(8,128)(2,1)}, bf16[48,256]{1,0:T(8,128)(2,1)S(1)}, u32[]{:S(2)}) copy-start(bf16[48,256]{1,0:T(8,128)(2,1)S(1)} %get-tuple-element.100.before_ref) | copy-start | bytes 73732
  107.2 10.5 %collective-permute-start.16 = (bf16[48,256]{1,0:T(8,128)(2,1)S(1)}, bf16[48,256]{1,0:T(8,128)(2,1)S(1)}, u32[]{:S(2)}, u32[]{:S(2)}) collective-permute-start(bf16[48,256]{1,0:T(8,128)(2,1)S(1)} %concatenate.12), channel_id=1, source_target_pairs={{0,2},{2,4},{4,6},{6,8},{8,10},{10,12},{12,14},{14,16},{16,18},{18... | collective-permute-start | bytes 73736 | tf_op jit(solution)/shard_map/ppermute | solution.py:560
  115.6 5.7 %collective-permute-start.17 = (bf16[48,256]{1,0:T(8,128)(2,1)S(1)}, bf16[48,256]{1,0:T(8,128)(2,1)S(1)}, u32[]{:S(2)}, u32[]{:S(2)}) collective-permute-start(bf16[48,256]{1,0:T(8,128)(2,1)S(1)} %concatenate.13), channel_id=1, source_target_pairs={{2,0},{4,2},{6,4},{8,6},{10,8},{12,10},{14,12},{16,14},{18,16},{20... | collective-permute-start | bytes 73736 | tf_op jit(solution)/shard_map/ppermute | solution.py:561
  117.7 3.7 %copy-start.21 = (bf16[48,256]{1,0:T(8,128)(2,1)}, bf16[48,256]{1,0:T(8,128)(2,1)S(1)}, u32[]{:S(2)}) copy-start(bf16[48,256]{1,0:T(8,128)(2,1)S(1)} %collective-permute-done.16.above_ref) | copy-start | bytes 73732
  121.3 0.6 copy-start.22

commit v5 on v4

--- a/solution.py
+++ b/solution.py
@@ -26,7 +26,7 @@
 
 EXPONENT_BOUND = 100.0
 SUM_ROWS = 16
-PAIR = 2
+PAIR = 4
 GROUP = 256
 
 norm_eps = 1e-06
@@ -89,7 +89,8 @@
     far = [swap(ring, "tile", s) for s, ring in enumerate(rings[half - 1 :], half)]
     mixed = [value if m == 0 else swap(value, "date", m) for m, value in enumerate(mixed)]
     last = [jnp.stack([value[i] for value in mixed]) for i in range(tiles - late)]
-    own, last = lax.optimization_barrier((own, last))
+    others, last = lax.optimization_barrier((own[1:], last))
+    own = [own[0]] + list(others)
     close = [swap(ring, "tile", s) for s, ring in enumerate(rings[: half - 1], 1)]
     own = [value if m == 0 else swap(value, "date", m) for m, value in enumerate(own)]
     prepared = prepare(last)
@@ -425,7 +426,7 @@
 def compose_kernel(
     classes, own_ref, before_ref, after_ref, above_ref, below_ref, profile_ref, m_ref, edge_ref,
     lanes_ref, window_ref, place_ref, side_ref, bias_ref,
-    o_ref, a_ref, b_ref, z_ref, z2_ref, acc_ref
+    o_ref, a_ref, b_ref, z_ref, z2_ref, acc_ref, out_ref, sems
 ):
     count = len(ENTRIES)
     edge = len(UPPER)
@@ -506,6 +507,19 @@
     z2_ref[...] = (total.reshape(count, SIDE, LANES) * jnp.stack(side_weights)).astype(bf16)
 
     acc_ref[...] = jnp.zeros_like(acc_ref)
+    inverse = 1.0 / jnp.maximum(den, 1.0)
+    step = STRIDE // sems.shape[0]
+    copies = []
+
+    def finish():
+        first = len(copies) * step
+        rows = slice(first, first + step)
+        for k in range(classes):
+            total = acc_ref[k, RIM + first : RIM + first + step, :] + bias_ref[k] * den[rows]
+            out_ref[k, rows, :] = total * inverse[rows]
+        copies.append(pltpu.make_async_copy(out_ref.at[:, rows, :], o_ref.at[:, rows, :], sems.at[len(copies)]))
+        copies[-1].start()
+
     for n, (tile_row, a) in enumerate(ENTRIES):
         part = mm(z_ref[n].reshape(SPAN * PATCHES, LANES), spots[tile_row], TN)
         part += mm(z2_ref[n], side_spots[tile_row], TN)
@@ -523,9 +537,22 @@
             low = max(0, 1 - PATCH * a)
         for k in range(classes):
             acc_ref[k, y + low : y + high, :] += part[k * SPAN + low : k * SPAN + high]
-    inverse = 1.0 / jnp.maximum(den, 1.0)
-    for k in range(classes):
-        o_ref[k] = (acc_ref[k, RIM : RIM + STRIDE, :] + bias_ref[k] * den) * inverse
+        if tile_row == 1:
+            clear = min(y + PATCH, STRIDE) - RIM
+            while (len(copies) + 1) * step <= clear and len(copies) + 1 < sems.shape[0]:
+                finish()
+    while len(copies) < sems.shape[0]:
+        finish()
+    for copy in copies:
+        copy.wait()
+
+
+def forward(size):
+    return [(i, i + 1) for i in range(size - 1)]
+
+
+def backward(size):
+    return [(i + 1, i) for i in range(size - 1)]
 
 
 def forward(size):
@@ -570,7 +597,7 @@
     return pl.pallas_call(
         functools.partial(compose_kernel, classes),
         in_specs=[whole] * 12 + [pl.BlockSpec(memory_space=pltpu.SMEM)],
-        out_specs=whole,
+        out_specs=pl.BlockSpec(memory_space=pl.ANY),
         out_shape=jax.ShapeDtypeStruct((classes, STRIDE, STRIDE), f32),
         scratch_shapes=[
             pltpu.VMEM((count, PATCHES, channels), bf16),
@@ -578,8 +605,10 @@
             pltpu.VMEM((count, SPAN, PATCHES, LANES), bf16),
             pltpu.VMEM((count, SIDE, LANES), bf16),
             pltpu.VMEM((classes, TILE_PX, STRIDE), f32),
+            pltpu.VMEM((classes, STRIDE, STRIDE), f32),
+            pltpu.SemaphoreType.DMA((4,)),
         ],
-        compiler_params=pltpu.CompilerParams(vmem_limit_bytes=VMEM),
+        compiler_params=pltpu.CompilerParams(vmem_limit_bytes=52 * 2**20),
         name="compose",
     )(reduced, *rims, profile, kernels, edges, *tables, class_bias.astype(f32))
 

time: 131 us -> 130 us (level)
    unnamed x54 -> x50, local copies, waits for them, and re-layouts: 7.38 us -> 6.81 us
  transfers between devices with their start and end apart: 18 -> 18, of which waited for: 8 -> 9; matrix products, arithmetic and copies ran while one was open for 5% -> 5% of each run, Pallas kernels for 11% -> 11%
where the time goes in v5:
time: 130 us; the launch traced here: 129 us
  Pallas kernels  62.1 us (48%)
  starting transfers between devices  30.1 us (23%)
  waiting for transfers between devices  22 us (17%)
  local copies, waits for them, and re-layouts  10.9 us (8%)
  other arithmetic  2.31 us (2%)
  between operations  1.84 us (1%)
    pallas_call x1, Pallas kernels, encode(): pl.pallas_call(functools.partial(encode_kernel, len(packed)), in_specs=[p...  34.7 us
    ppermute x16, starting transfers between devices, swap(): lax.ppermute(value, axis, [(i, i ^ mask) for i in range(lax.axis_size(axi...  20.5 us
    ppermute x16, waiting for transfers between devices, swap(): lax.ppermute(value, axis, [(i, i ^ mask) for i in range(lax.axis_size(axi...  17.6 us
    pallas_call x3, Pallas kernels, project(): pl.pallas_call(functools.partial(project_kernel, [n for _, n in pieces]),...  13.4 us
    ppermute x1, starting transfers between devices, exchange_rims(): above = lax.ppermute(lines(UPPER), ('date', 'tile'), forward(rows))  8.32 us
    pallas_call x1, Pallas kernels, compose(): pl.pallas_call(functools.partial(compose_kernel, classes), in_specs=[whol...  7.6 us
    unnamed x50, local copies, waits for them, and re-layouts  6.81 us
    pallas_call x1, Pallas kernels, prepare_weights(): pl.pallas_call(prepare_kernel, in_specs=[whole] * 5 + [pl.BlockSpec(memor...  4.63 us
  transfers between devices with their start and end apart: 18, of which 9 were waited for; matrix products, arithmetic and copies ran while one was open for 5% of the time, Pallas kernels for 11%

profile of v5, /device:TPU:0, one launch (start us, length us, event | category | flops | bytes accessed | tf_op | source)
XLA Modules:
  0.0 129.3 jit_solution(11744006509772022406)
XLA Ops:
  0.0 1.8 %copy-done.3 = bf16[1,16,1,1,4,16,1280]{6,5,4,3,2,1,0:T(8,128)(2,1)S(1)} copy-done((bf16[1,16,1,1,4,16,1280]{6,5,4,3,2,1,0:T(8,128)(2,1)S(1)}, bf16[1,16,1,1,4,16,1280]{6,5,4,3,2,1,0:T(8,128)(2,1)}, u32[]{:S(2)}) %copy-start.3) | copy-done | bytes 2621464
  1.8 0.7 copy-done.17
  2.4 1.8 %gather_pieces.1 = (bf16[4,64,1280]{2,1,0:T(8,128)(2,1)}, bf16[4,64,1280]{2,1,0:T(8,128)(2,1)}, bf16[1,64,1280]{2,1,0:T(8,128)(2,1)S(1)}, bf16[1,64,1280]{2,1,0:...) custom-call(s32[16]{0:T(128)S(1)} %bitcast.20, ...), custom_call_target="tpu_custom_call" | custom-call | tf_op jit(solution)/shard_map/gather_pieces/pallas_call | solution.py:65
  4.3 0.7 copy-done.18
  4.9 4.0 %collective-permute-start.10 = (bf16[4,64,1280]{2,1,0:T(8,128)(2,1)}, bf16[4,64,1280]{2,1,0:T(8,128)(2,1)S(1)}, u32[]{:S(2)}, u32[]{:S(2)}) collective-permute-start(bf16[4,64,1280]{2,1,0:T(8,128)(2,1)} %get-tuple-element.56), channel_id=1, source_target_pairs={{0,4},{2,6},{4,0},{6,2},{1,5},{3,7},{5,1},{7,3},{8,12},{10,14},{12... | collective-permute-start | bytes 1966088 | tf_op jit(solution)/shard_map/ppermute | solution.py:78
  9.0 0.7 collective-permute-start.2
  9.6 0.9 collective-permute-start.1
  10.5 0.3 collective-permute-start
  10.8 1.6 %collective-permute-start.6 = (bf16[4,64,1280]{2,1,0:T(8,128)(2,1)}, bf16[4,64,1280]{2,1,0:T(8,128)(2,1)S(1)}, u32[]{:S(2)}, u32[]{:S(2)}) collective-permute-start(bf16[4,64,1280]{2,1,0:T(8,128)(2,1)} %get-tuple-element.50), channel_id=1, source_target_pairs={{0,2},{2,0},{4,6},{6,4},{1,3},{3,1},{5,7},{7,5},{8,10},{10,8},{12,... | collective-permute-start | bytes 1966088 | tf_op jit(solution)/shard_map/ppermute | solution.py:78
  13.1 0.6 broadcast_in_dim.23.refs_11_
  13.7 0.6 broadcast_in_dim.24.refs_13_
  14.9 0.7 pad_add_fusion.place_ref
  15.6 3.4 %collective-permute-done.1 = bf16[1,64,1280]{2,1,0:T(8,128)(2,1)S(1)} collective-permute-done((bf16[1,64,1280]{2,1,0:T(8,128)(2,1)S(1)}, bf16[1,64,1280]{2,1,0:T(8,128)(2,1)S(1)}, u32[]{:S(2)}, u32[]{:S(2)}) %collective-permute-start.1) | collective-permute-done | bytes 163872 | tf_op jit(solution)/shard_map/ppermute | solution.py:78
  19.0 0.9 pad_maximum_fusion
  19.9 0.1 collective-permute-start.3
  20.0 1.3 collective-permute-start.4
  21.3 2.7 %copy.23.up_ref = bf16[256,3136]{1,0:T(8,128)(2,1)S(1)} copy(bf16[256,3136]{0,1:T(8,128)(2,1)} %param.34) | data formatting | bytes 3211264 | tf_op jit(solution)/shard_map/optimization_barrier | solution.py:641
  24.0 0.7 convert_element_type.18
  24.7 0.8 copy-done.10
  25.5 0.8 copy-done.11
  26.3 0.7 copy-done.14
  27.0 4.6 %prepare_weights.1 = (bf16[16,256,256]{2,1,0:T(8,128)(2,1)S(1)}, bf16[2,256,256]{2,1,0:T(8,128)(2,1)S(1)}, bf16[1280,3840]{1,0:T(8,128)(2,1)S(1)}) custom-call(bf16[256,3136]{1,0:T(8,128)(2,1)S(1)} %copy.23.up_ref, bf16[9,13,16]{2,1,0:T(8,128)(2,1)S(1)} %copy-done.11, bf16[256,13]{1,0:T(8,128)(2,1)S(1)} %copy-done.10, bf16[16,224]{1,0:T(8,128)(2,1)S(1)} %copy-done.14, ...), custom_call_target="tpu_custom_call" | custom-call | tf_op jit(solution)/shard_map/prepare_weights/pallas_call | solution.py:406
  31.6 1.3 %copy-done.4 = bf16[16,256,256]{2,1,0:T(8,128)(2,1)} copy-done((bf16[16,256,256]{2,1,0:T(8,128)(2,1)}, bf16[16,256,256]{2,1,0:T(8,128)(2,1)S(1)}, u32[]{:S(2)}) %copy-start.4) | copy-done | bytes 2097176
  33.0 0.1 fusion.2.refs_8_.refs_4_.refs_1_.refs_9_
  33.1 5.0 %collective-permute-done.10.refs_0_ = bf16[4,64,1280]{2,1,0:T(8,128)(2,1)S(1)} collective-permute-done((bf16[4,64,1280]{2,1,0:T(8,128)(2,1)}, bf16[4,64,1280]{2,1,0:T(8,128)(2,1)S(1)}, u32[]{:S(2)}, u32[]{:S(2)}) %collective-permute-start.10) | collective-permute-done | bytes 655392 | tf_op jit(solution)/shard_map/ppermute | solution.py:78
  38.1 0.1 collective-permute-start.11
  38.2 1.6 %collective-permute-start.12 = (bf16[1,64,1280]{2,1,0:T(8,128)(2,1)S(1)}, bf16[1,64,1280]{2,1,0:T(8,128)(2,1)S(1)}, u32[]{:S(2)}, u32[]{:S(2)}) collective-permute-start(bf16[1,64,1280]{2,1,0:T(8,128)(2,1)S(1)} %get-tuple-element.74), channel_id=1, source_target_pairs={{0,16},{8,24},{16,0},{24,8},{1,17},{9,25},{17,1},{25,9},{2,18},{10... | collective-permute-start | bytes 491528 | tf_op jit(solution)/shard_map/ppermute | solution.py:78
  39.8 0.3 collective-permute-start.13
  40.0 0.7 collective-permute-done.6.refs_4_
  40.7 2.9 %collective-permute-start.14 = (bf16[4,64,1280]{2,1,0:T(8,128)(2,1)S(1)}, bf16[4,64,1280]{2,1,0:T(8,128)(2,1)S(1)}, u32[]{:S(2)}, u32[]{:S(2)}) collective-permute-start(bf16[4,64,1280]{2,1,0:T(8,128)(2,1)S(1)} %copy-done.20), channel_id=1, source_target_pairs={{0,6},{2,4},{4,2},{6,0},{1,7},{3,5},{5,3},{7,1},{8,14},{10,12},{12... | collective-permute-start | bytes 1966088 | tf_op jit(solution)/shard_map/ppermute | solution.py:78
  43.6 1.2 collective-permute-start.5
  44.9 0.4 collective-permute-start.7
  45.3 1.5 %collective-permute-start.8 = (bf16[1,64,1280]{2,1,0:T(8,128)(2,1)S(1)}, bf16[1,64,1280]{2,1,0:T(8,128)(2,1)S(1)}, u32[]{:S(2)}, u32[]{:S(2)}) collective-permute-start(bf16[1,64,1280]{2,1,0:T(8,128)(2,1)S(1)} %get-tuple-element.77), channel_id=1, source_target_pairs={{0,16},{8,24},{16,0},{24,8},{1,17},{9,25},{17,1},{25,9},{2,18},{10... | collective-permute-start | bytes 491528 | tf_op jit(solution)/shard_map/ppermute | solution.py:78
  46.8 1.1 collective-permute-done.13.refs_3_
  47.8 2.2 %collective-permute-start.9 = (bf16[1,64,1280]{2,1,0:T(8,128)(2,1)S(1)}, bf16[1,64,1280]{2,1,0:T(8,128)(2,1)S(1)}, u32[]{:S(2)}, u32[]{:S(2)}) collective-permute-start(bf16[1,64,1280]{2,1,0:T(8,128)(2,1)S(1)} %get-tuple-element.76), channel_id=1, source_target_pairs={{0,24},{8,16},{16,8},{24,0},{1,25},{9,17},{17,9},{25,1},{2,26},{10... | collective-permute-start | bytes 491528 | tf_op jit(solution)/shard_map/ppermute | solution.py:78
  50.0 3.1 %project.4 = (bf16[3840,256]{1,0:T(8,128)(2,1)S(1)}, f32[32,128]{1,0:T(8,128)S(1)}, bf16[256,1280]{1,0:T(8,128)(2,1)S(1)}) custom-call(bf16[4,64,1280]{2,1,0:T(8,128)(2,1)S(1)} %collective-permute-done.10.refs_0_, bf16[1,64,1280]{2,1,0:T(8,128)(2,1)S(1)} %collective-permute-done.11.refs_1_, bf16[1,64,1280]{2,1,0:T(8,128)(2,1)S(1)} %collective-permute-done.12.refs_2_, ...), custom_call_target="tpu_custom_call" | custom-call | tf_op jit(solution)/shard_map/project/pallas_call | solution.py:155
  53.2 2.6 %collective-permute-done.8.refs_6_ = bf16[1,64,1280]{2,1,0:T(8,128)(2,1)S(1)} collective-permute-done((bf16[1,64,1280]{2,1,0:T(8,128)(2,1)S(1)}, bf16[1,64,1280]{2,1,0:T(8,128)(2,1)S(1)}, u32[]{:S(2)}, u32[]{:S(2)}) %collective-permute-start.8) | collective-permute-done | bytes 163872 | tf_op jit(solution)/shard_map/ppermute | solution.py:78
  55.8 2.6 %collective-permute-done.9.refs_7_ = bf16[1,64,1280]{2,1,0:T(8,128)(2,1)S(1)} collective-permute-done((bf16[1,64,1280]{2,1,0:T(8,128)(2,1)S(1)}, bf16[1,64,1280]{2,1,0:T(8,128)(2,1)S(1)}, u32[]{:S(2)}, u32[]{:S(2)}) %collective-permute-start.9) | collective-permute-done | bytes 163872 | tf_op jit(solution)/shard_map/ppermute | solution.py:78
  58.4 7.0 %project.3 = (bf16[3840,512]{1,0:T(8,128)(2,1)S(1)}, f32[32,128]{1,0:T(8,128)S(1)}, bf16[512,1280]{1,0:T(8,128)(2,1)S(1)}) custom-call(bf16[1,64,1280]{2,1,0:T(8,128)(2,1)S(1)} %get-tuple-element.39.refs_0_, bf16[1,64,1280]{2,1,0:T(8,128)(2,1)} %collective-permute-done.3.refs_1_, bf16[1,64,1280]{2,1,0:T(8,128)(2,1)} %collective-permute-done.4.refs_2_, ...), custom_call_target="tpu_custom_call" | custom-call | tf_op jit(solution)/shard_map/project/pallas_call | solution.py:155
  65.4 3.3 %project.5 = (bf16[3840,256]{1,0:T(8,128)(2,1)S(1)}, f32[32,128]{1,0:T(8,128)S(1)}, bf16[256,1280]{1,0:T(8,128)(2,1)S(1)}) custom-call(bf16[4,64,1280]{2,1,0:T(8,128)(2,1)S(1)} %collective-permute-done.14.refs_0_, f32[1,1280]{1,0:T(1,128)S(1)} %fusion.2.refs_8_.refs_4_.refs_1_.refs_9_, bf16[1,1280]{1,0:T(2,128)(2,1)S(1)} %broadcast_in_dim.22.refs_9_.refs_5_.refs_2_, ...), custom_call_target="tpu_custom_call" | custom-call | tf_op jit(solution)/shard_map/project/pallas_call | solution.py:155
  68.8 34.7 %encode.1 = (bf16[256,256]{1,0:T(8,128)(2,1)S(1)}, bf16[48,256]{1,0:T(8,128)(2,1)S(1)}, bf16[48,256]{1,0:T(8,128)(2,1)}) custom-call(s32[3]{0:T(128)S(1)} %copy-done.15, bf16[3840,512]{1,0:T(8,128)(2,1)S(1)} %get-tuple-element.55.refs_0_, bf16[3840,256]{1,0:T(8,128)(2,1)S(1)} %get-tuple-element.59.refs_1_, bf16[3840,256]{1,0:T(8,128)(2,1)S(1)} %get-tuple-element.61.refs_2_, ...), custom_call_target="tpu_custom_call" | custom-call | tf_op jit(solution)/shard_map/encode/pallas_call | solution.py:262
  103.5 1.6 %collective-permute-start.15 = (bf16[48,256]{1,0:T(8,128)(2,1)S(1)}, bf16[48,256]{1,0:T(8,128)(2,1)S(1)}, u32[]{:S(2)}, u32[]{:S(2)}) collective-permute-start(bf16[48,256]{1,0:T(8,128)(2,1)S(1)} %get-tuple-element.70), channel_id=1, source_target_pairs={{0,1},{1,0},{2,3},{3,2},{4,5},{5,4},{6,7},{7,6},{8,9},{9,8},{10,11... | collective-permute-start | bytes 73736 | tf_op jit(solution)/shard_map/ppermute | solution.py:78
  105.1 2.2 %collective-permute-done.15 = bf16[48,256]{1,0:T(8,128)(2,1)S(1)} collective-permute-done((bf16[48,256]{1,0:T(8,128)(2,1)S(1)}, bf16[48,256]{1,0:T(8,128)(2,1)S(1)}, u32[]{:S(2)}, u32[]{:S(2)}) %collective-permute-start.15) | collective-permute-done | bytes 24608 | tf_op jit(solution)/shard_map/ppermute | solution.py:78
  107.4 8.3 %collective-permute-start.16 = (bf16[48,256]{1,0:T(8,128)(2,1)S(1)}, bf16[48,256]{1,0:T(8,128)(2,1)S(1)}, u32[]{:S(2)}, u32[]{:S(2)}) collective-permute-start(bf16[48,256]{1,0:T(8,128)(2,1)S(1)} %concatenate.12), channel_id=1, source_target_pairs={{0,2},{2,4},{4,6},{6,8},{8,10},{10,12},{12,14},{14,16},{16,18},{18... | collective-permute-start | bytes 73736 | tf_op jit(solution)/shard_map/ppermute | solution.py:587
  115.8 1.3 collective-permute-start.17
  117.1 0.1 collective-permute-done.16.above_ref
  117.3 4.3 %collective-permute-done.17.below_ref = bf16[48,256]{1,0:T(8,128)(2,1)S(1)} collective-permute-done((bf16[48,256]{1,0:T(8,128)(2,1)S(1)}, bf16[48,256]{1,0:T(8,128)(2,1)S(1)}, u32[]{:S(2)}, u32[]{:S(2)}) %collective-permute-start.17) | collective-permute-done | bytes 24608 | tf_op jit(solution)/shard_map/ppermute | solution.py:588
  121.6 7.6 %compose.1 = f32[13,192,192]{2,1,0:T(8,128)} custom-call(bf16[256,256]{1,0:T(8,128)(2,1)S(1)} %get-tuple-element.69.own_ref, bf16[48,256]{1,0:T(8,128)(2,1)S(1)} %get-tuple-element.98.before_ref, bf16[48,256]{1,0:T(8,128)(2,1)S(1)} %get-tuple-element.97.after_ref, bf16[48,256]{1,0:T(8,128)(2,1)S(1)} %collective-permute-done.16.above_ref, ...), custom_call_target="tpu_custom_call" | custom-call | tf_op jit(solution)/shard_map/compose/pallas_call | solution.py:597
  (66 shorter events, 0.4 us)
Async XLA Ops:
  0.0 33.0 %copy-start = (bf16[16,1280]{1,0:T(8,128)(2,1)S(1)}, bf16[16,1280]{1,0:T(8,128)(2,1)}, u32[]{:S(2)}) copy-start(bf16[16,1280]{1,0:T(8,128)(2,1)} %param.27) | copy-start | bytes 122884
  0.0 13.7 %copy-start.23 = (bf16[256]{0:T(256)(128)(2,1)S(1)}, bf16[256]{0:T(256)(128)(2,1)}, u32[]{:S(2)}) copy-start(bf16[256]{0:T(256)(128)(2,1)} %param.33) | copy-start | bytes 1540
  0.0 1.8 %copy-start.3 = (bf16[1,16,1,1,4,16,1280]{6,5,4,3,2,1,0:T(8,128)(2,1)S(1)}, bf16[1,16,1,1,4,16,1280]{6,5,4,3,2,1,0:T(8,128)(2,1)}, u32[]{:S(2)}) copy-start(bf16[1,16,1,1,4,16,1280]{6,5,4,3,2,1,0:T(8,128)(2,1)} %param.22) | copy-start | bytes 7864324
  1.8 0.7 copy-start.17
  2.4 10.6 %copy-start.21 = (bf16[1280]{0:T(1024)(128)(2,1)S(1)}, bf16[1280]{0:T(1024)(128)(2,1)}, u32[]{:S(2)}) copy-start(bf16[1280]{0:T(1024)(128)(2,1)} %param.28) | copy-start | bytes 7684
  2.4 10.7 %copy-start.22 = (bf16[1280]{0:T(1024)(128)(2,1)S(1)}, bf16[1280]{0:T(1024)(128)(2,1)}, u32[]{:S(2)}) copy-start(bf16[1280]{0:T(1024)(128)(2,1)} %param.31) | copy-start | bytes 7684
  4.3 0.7 copy-start.18
  4.9 19.7 %copy-start.5 = (bf16[3,256,224]{2,1,0:T(8,128)(2,1)S(1)}, bf16[3,256,224]{2,1,0:T(8,128)(2,1)}, u32[]{:S(2)}) copy-start(bf16[3,256,224]{2,1,0:T(8,128)(2,1)} %constant.34.clone.meet_ref) | copy-start | bytes 1032196
  4.9 33.1 %collective-permute-start.10 = (bf16[4,64,1280]{2,1,0:T(8,128)(2,1)}, bf16[4,64,1280]{2,1,0:T(8,128)(2,1)S(1)}, u32[]{:S(2)}, u32[]{:S(2)}) collective-permute-start(bf16[4,64,1280]{2,1,0:T(8,128)(2,1)} %get-tuple-element.56), channel_id=1, source_target_pairs={{0,4},{2,6},{4,0},{6,2},{1,5},{3,7},{5,1},{7,3},{8,12},{10,14},{12... | collective-permute-start | bytes 1966088 | tf_op jit(solution)/shard_map/ppermute | solution.py:78
  9.0 6.6 %collective-permute-start.2 = (bf16[1,64,1280]{2,1,0:T(8,128)(2,1)S(1)}, bf16[1,64,1280]{2,1,0:T(8,128)(2,1)S(1)}, u32[]{:S(2)}, u32[]{:S(2)}) collective-permute-start(bf16[1,64,1280]{2,1,0:T(8,128)(2,1)S(1)} %get-tuple-element.46), channel_id=1, source_target_pairs={{0,24},{8,16},{16,8},{24,0},{1,25},{9,17},{17,9},{25,1},{2,26},{10... | collective-permute-start | bytes 491528 | tf_op jit(solution)/shard_map/ppermute | solution.py:78
  9.6 9.4 %collective-permute-start.1 = (bf16[1,64,1280]{2,1,0:T(8,128)(2,1)S(1)}, bf16[1,64,1280]{2,1,0:T(8,128)(2,1)S(1)}, u32[]{:S(2)}, u32[]{:S(2)}) collective-permute-start(bf16[1,64,1280]{2,1,0:T(8,128)(2,1)S(1)} %get-tuple-element.45), channel_id=1, source_target_pairs={{0,16},{8,24},{16,0},{24,8},{1,17},{9,25},{17,1},{25,9},{2,18},{10... | collective-permute-start | bytes 491528 | tf_op jit(solution)/shard_map/ppermute | solution.py:78
  10.5 8.5 %collective-permute-start = (bf16[1,64,1280]{2,1,0:T(8,128)(2,1)S(1)}, bf16[1,64,1280]{2,1,0:T(8,128)(2,1)S(1)}, u32[]{:S(2)}, u32[]{:S(2)}) collective-permute-start(bf16[1,64,1280]{2,1,0:T(8,128)(2,1)S(1)} %get-tuple-element.44), channel_id=1, source_target_pairs={{0,8},{8,0},{16,24},{24,16},{1,9},{9,1},{17,25},{25,17},{2,10},{10... | collective-permute-start | bytes 491528 | tf_op jit(solution)/shard_map/ppermute | solution.py:78
  10.8 29.9 %collective-permute-start.6 = (bf16[4,64,1280]{2,1,0:T(8,128)(2,1)}, bf16[4,64,1280]{2,1,0:T(8,128)(2,1)S(1)}, u32[]{:S(2)}, u32[]{:S(2)}) collective-permute-start(bf16[4,64,1280]{2,1,0:T(8,128)(2,1)} %get-tuple-element.50), channel_id=1, source_target_pairs={{0,2},{2,0},{4,6},{6,4},{1,3},{3,1},{5,7},{7,5},{8,10},{10,8},{12,... | collective-permute-start | bytes 1966088 | tf_op jit(solution)/shard_map/ppermute | solution.py:78
  19.9 19.9 %collective-permute-start.3 = (bf16[1,64,1280]{2,1,0:T(8,128)(2,1)}, bf16[1,64,1280]{2,1,0:T(8,128)(2,1)}, u32[]{:S(2)}, u32[]{:S(2)}) collective-permute-start(bf16[1,64,1280]{2,1,0:T(8,128)(2,1)} %get-tuple-element.47), channel_id=1, source_target_pairs={{0,8},{8,0},{16,24},{24,16},{1,9},{9,1},{17,25},{25,17},{2,10},{10... | collective-permute-start | bytes 491528 | tf_op jit(solution)/shard_map/ppermute | solution.py:78
  20.0 23.6 %collective-permute-start.4 = (bf16[1,64,1280]{2,1,0:T(8,128)(2,1)}, bf16[1,64,1280]{2,1,0:T(8,128)(2,1)}, u32[]{:S(2)}, u32[]{:S(2)}) collective-permute-start(bf16[1,64,1280]{2,1,0:T(8,128)(2,1)} %get-tuple-element.48), channel_id=1, source_target_pairs={{0,16},{8,24},{16,0},{24,8},{1,17},{9,25},{17,1},{25,9},{2,18},{10... | collective-permute-start | bytes 491528 | tf_op jit(solution)/shard_map/ppermute | solution.py:78
  24.7 0.8 copy-start.10
  25.5 0.8 copy-start.11
  26.3 0.7 copy-start.14
  27.0 13.8 %copy-start.20 = (bf16[4,64,1280]{2,1,0:T(8,128)(2,1)S(1)}, bf16[4,64,1280]{2,1,0:T(8,128)(2,1)}, u32[]{:S(2)}) copy-start(bf16[4,64,1280]{2,1,0:T(8,128)(2,1)} %pad_maximum_fusion) | copy-start | bytes 1966084
  27.0 16.7 %copy-start.19 = (bf16[1,64,1280]{2,1,0:T(8,128)(2,1)S(1)}, bf16[1,64,1280]{2,1,0:T(8,128)(2,1)}, u32[]{:S(2)}) copy-start(bf16[1,64,1280]{2,1,0:T(8,128)(2,1)} %copy-done.18) | copy-start | bytes 491524
  31.6 1.3 %copy-start.4 = (bf16[16,256,256]{2,1,0:T(8,128)(2,1)}, bf16[16,256,256]{2,1,0:T(8,128)(2,1)S(1)}, u32[]{:S(2)}) copy-start(bf16[16,256,256]{2,1,0:T(8,128)(2,1)S(1)} %get-tuple-element.71.m_ref) | copy-start | bytes 6291460
  33.0 20.2 %copy-start.8 = (bf16[2,256,256]{2,1,0:T(8,128)(2,1)}, bf16[2,256,256]{2,1,0:T(8,128)(2,1)S(1)}, u32[]{:S(2)}) copy-start(bf16[2,256,256]{2,1,0:T(8,128)(2,1)S(1)} %get-tuple-element.72.edge_ref) | copy-start | bytes 786436
  38.1 6.8 %collective-permute-start.11 = (bf16[1,64,1280]{2,1,0:T(8,128)(2,1)S(1)}, bf16[1,64,1280]{2,1,0:T(8,128)(2,1)S(1)}, u32[]{:S(2)}, u32[]{:S(2)}) collective-permute-start(bf16[1,64,1280]{2,1,0:T(8,128)(2,1)S(1)} %get-tuple-element.75), channel_id=1, source_target_pairs={{0,8},{8,0},{16,24},{24,16},{1,9},{9,1},{17,25},{25,17},{2,10},{10... | collective-permute-start | bytes 491528 | tf_op jit(solution)/shard_map/ppermute | solution.py:78
  38.2 7.2 %collective-permute-start.12 = (bf16[1,64,1280]{2,1,0:T(8,128)(2,1)S(1)}, bf16[1,64,1280]{2,1,0:T(8,128)(2,1)S(1)}, u32[]{:S(2)}, u32[]{:S(2)}) collective-permute-start(bf16[1,64,1280]{2,1,0:T(8,128)(2,1)S(1)} %get-tuple-element.74), channel_id=1, source_target_pairs={{0,16},{8,24},{16,0},{24,8},{1,17},{9,25},{17,1},{25,9},{2,18},{10... | collective-permute-start | bytes 491528 | tf_op jit(solution)/shard_map/ppermute | solution.py:78
  39.8 8.1 %collective-permute-start.13 = (bf16[1,64,1280]{2,1,0:T(8,128)(2,1)S(1)}, bf16[1,64,1280]{2,1,0:T(8,128)(2,1)S(1)}, u32[]{:S(2)}, u32[]{:S(2)}) collective-permute-start(bf16[1,64,1280]{2,1,0:T(8,128)(2,1)S(1)} %get-tuple-element.73), channel_id=1, source_target_pairs={{0,24},{8,16},{16,8},{24,0},{1,25},{9,17},{17,9},{25,1},{2,26},{10... | collective-permute-start | bytes 491528 | tf_op jit(solution)/shard_map/ppermute | solution.py:78
  40.7 24.7 %collective-permute-start.14 = (bf16[4,64,1280]{2,1,0:T(8,128)(2,1)S(1)}, bf16[4,64,1280]{2,1,0:T(8,128)(2,1)S(1)}, u32[]{:S(2)}, u32[]{:S(2)}) collective-permute-start(bf16[4,64,1280]{2,1,0:T(8,128)(2,1)S(1)} %copy-done.20), channel_id=1, source_target_pairs={{0,6},{2,4},{4,2},{6,0},{1,7},{3,5},{5,3},{7,1},{8,14},{10,12},{12... | collective-permute-start | bytes 1966088 | tf_op jit(solution)/shard_map/ppermute | solution.py:78
  43.6 9.5 %collective-permute-start.5 = (bf16[1,64,1280]{2,1,0:T(8,128)(2,1)S(1)}, bf16[1,64,1280]{2,1,0:T(8,128)(2,1)S(1)}, u32[]{:S(2)}, u32[]{:S(2)}) collective-permute-start(bf16[1,64,1280]{2,1,0:T(8,128)(2,1)S(1)} %copy-done.19), channel_id=1, source_target_pairs={{0,24},{8,16},{16,8},{24,0},{1,25},{9,17},{17,9},{25,1},{2,26},{10... | collective-permute-start | bytes 491528 | tf_op jit(solution)/shard_map/ppermute | solution.py:78
  44.9 8.3 %collective-permute-start.7 = (bf16[1,64,1280]{2,1,0:T(8,128)(2,1)S(1)}, bf16[1,64,1280]{2,1,0:T(8,128)(2,1)S(1)}, u32[]{:S(2)}, u32[]{:S(2)}) collective-permute-start(bf16[1,64,1280]{2,1,0:T(8,128)(2,1)S(1)} %get-tuple-element.78), channel_id=1, source_target_pairs={{0,8},{8,0},{16,24},{24,16},{1,9},{9,1},{17,25},{25,17},{2,10},{10... | collective-permute-start | bytes 491528 | tf_op jit(solution)/shard_map/ppermute | solution.py:78
  45.3 10.4 %collective-permute-start.8 = (bf16[1,64,1280]{2,1,0:T(8,128)(2,1)S(1)}, bf16[1,64,1280]{2,1,0:T(8,128)(2,1)S(1)}, u32[]{:S(2)}, u32[]{:S(2)}) collective-permute-start(bf16[1,64,1280]{2,1,0:T(8,128)(2,1)S(1)} %get-tuple-element.77), channel_id=1, source_target_pairs={{0,16},{8,24},{16,0},{24,8},{1,17},{9,25},{17,1},{25,9},{2,18},{10... | collective-permute-start | bytes 491528 | tf_op jit(solution)/shard_map/ppermute | solution.py:78
  47.8 10.5 %collective-permute-start.9 = (bf16[1,64,1280]{2,1,0:T(8,128)(2,1)S(1)}, bf16[1,64,1280]{2,1,0:T(8,128)(2,1)S(1)}, u32[]{:S(2)}, u32[]{:S(2)}) collective-permute-start(bf16[1,64,1280]{2,1,0:T(8,128)(2,1)S(1)} %get-tuple-element.76), channel_id=1, source_target_pairs={{0,24},{8,16},{16,8},{24,0},{1,25},{9,17},{17,9},{25,1},{2,26},{10... | collective-permute-start | bytes 491528 | tf_op jit(solution)/shard_map/ppermute | solution.py:78
  65.4 3.4 %copy-start.1 = (bf16[1280,1280]{1,0:T(8,128)(2,1)S(1)}, bf16[1280,1280]{1,0:T(8,128)(2,1)}, u32[]{:S(2)}) copy-start(bf16[1280,1280]{1,0:T(8,128)(2,1)} %refs_10_.1) | copy-start | bytes 9830404
  65.4 3.4 %copy-start.2 = (bf16[5120,256]{1,0:T(8,128)(2,1)S(1)}, bf16[5120,256]{1,0:T(8,128)(2,1)}, u32[]{:S(2)}) copy-start(bf16[5120,256]{1,0:T(8,128)(2,1)} %param.32) | copy-start | bytes 7864324
  65.4 3.4 %copy-start.13 = (bf16[1,1280]{1,0:T(2,128)(2,1)S(1)}, bf16[1,1280]{1,0:T(2,128)(2,1)}, u32[]{:S(2)}) copy-start(bf16[1,1280]{1,0:T(2,128)(2,1)} %broadcast_in_dim.23.refs_11_) | copy-start | bytes 7684
  65.4 3.4 %copy-start.15 = (s32[3]{0:T(128)S(1)}, s32[3]{0:T(128)}, u32[]{:S(2)}) copy-start(s32[3]{0:T(128)} %pad_add_fusion.place_ref) | copy-start | bytes 40
  65.4 3.4 %copy-start.16 = (bf16[1,256]{1,0:T(2,128)(2,1)S(1)}, bf16[1,256]{1,0:T(2,128)(2,1)}, u32[]{:S(2)}) copy-start(bf16[1,256]{1,0:T(2,128)(2,1)} %broadcast_in_dim.24.refs_13_) | copy-start | bytes 1540
  68.8 48.4 %copy-start.24 = (bf16[13]{0:T(256)(128)(2,1)S(1)}, bf16[13]{0:T(256)(128)(2,1)}, u32[]{:S(2)}) copy-start(bf16[13]{0:T(256)(128)(2,1)} %param.36) | copy-start | bytes 82
  68.8 52.8 %copy-start.6 = (bf16[3,256,192]{2,1,0:T(8,128)(2,1)S(1)}, bf16[3,256,192]{2,1,0:T(8,128)(2,1)}, u32[]{:S(2)}) copy-start(bf16[3,256,192]{2,1,0:T(8,128)(2,1)} %constant.36.clone.window_ref) | copy-start | bytes 884740
  68.8 52.7 %copy-start.7 = (bf16[3,256,192]{2,1,0:T(8,128)(2,1)S(1)}, bf16[3,256,192]{2,1,0:T(8,128)(2,1)}, u32[]{:S(2)}) copy-start(bf16[3,256,192]{2,1,0:T(8,128)(2,1)} %constant.37.clone.place_ref) | copy-start | bytes 884740
  68.8 52.7 %copy-start.9 = (bf16[2,256,256]{2,1,0:T(8,128)(2,1)S(1)}, bf16[2,256,256]{2,1,0:T(8,128)(2,1)}, u32[]{:S(2)}) copy-start(bf16[2,256,256]{2,1,0:T(8,128)(2,1)} %copy-done.8) | copy-start | bytes 786436
  68.8 52.7 %copy-start.12 = (bf16[3,16,192]{2,1,0:T(8,128)(2,1)S(1)}, bf16[3,16,192]{2,1,0:T(8,128)(2,1)}, u32[]{:S(2)}) copy-start(bf16[3,16,192]{2,1,0:T(8,128)(2,1)} %constant.38.clone.side_ref) | copy-start | bytes 55300
  103.5 3.8 %collective-permute-start.15 = (bf16[48,256]{1,0:T(8,128)(2,1)S(1)}, bf16[48,256]{1,0:T(8,128)(2,1)S(1)}, u32[]{:S(2)}, u32[]{:S(2)}) collective-permute-start(bf16[48,256]{1,0:T(8,128)(2,1)S(1)} %get-tuple-element.70), channel_id=1, source_target_pairs={{0,1},{1,0},{2,3},{3,2},{4,5},{5,4},{6,7},{7,6},{8,9},{9,8},{10,11... | collective-permute-start | bytes 73736 | tf_op jit(solution)/shard_map/ppermute | solution.py:78
  107.4 9.8 %collective-permute-start.16 = (bf16[48,256]{1,0:T(8,128)(2,1)S(1)}, bf16[48,256]{1,0:T(8,128)(2,1)S(1)}, u32[]{:S(2)}, u32[]{:S(2)}) collective-permute-start(bf16[48,256]{1,0:T(8,128)(2,1)S(1)} %concatenate.12), channel_id=1, source_target_pairs={{0,2},{2,4},{4,6},{6,8},{8,10},{10,12},{12,14},{14,16},{16,18},{18... | collective-permute-start | bytes 73736 | tf_op jit(solution)/shard_map/ppermute | solution.py:587
  115.8 5.7 %collective-permute-start.17 = (bf16[48,256]{1,0:T(8,128)(2,1)S(1)}, bf16[48,256]{1,0:T(8,128)(2,1)S(1)}, u32[]{:S(2)}, u32[]{:S(2)}) collective-permute-start(bf16[48,256]{1,0:T(8,128)(2,1)S(1)} %concatenate.13), channel_id=1, source_target_pairs={{2,0},{4,2},{6,4},{8,6},{10,8},{12,10},{14,12},{16,14},{18,16},{20... | collective-permute-start | bytes 73736 | tf_op jit(solution)/shard_map/ppermute | solution.py:588

commit v6 on v5

--- a/solution.py
+++ b/solution.py
@@ -26,7 +26,7 @@
 
 EXPONENT_BOUND = 100.0
 SUM_ROWS = 16
-PAIR = 4
+PAIR = 8
 GROUP = 256
 
 norm_eps = 1e-06
@@ -66,7 +66,7 @@
         functools.partial(gather_kernel, dates, slots // dates, routes),
         in_specs=[pl.BlockSpec(memory_space=pltpu.SMEM), whole],
         out_specs=[whole] * len(groups),
-        out_shape=[pltpu.VMEM((len(group), strip, width), bf16) for group in groups],
+        out_shape=[jax.ShapeDtypeStruct((len(group), strip, width), bf16) for group in groups],
         scratch_shapes=[pltpu.SMEM((slots,), jnp.int32)],
         compiler_params=pltpu.CompilerParams(vmem_limit_bytes=12 * 2**20),
         cost_estimate=pl.CostEstimate(flops=0, bytes_accessed=0, transcendentals=0),

time: 130 us -> 130 us (level)
  no operation moved by 1% of the time
where the time goes in v6:
time: 130 us; the launch traced here: 129 us
  Pallas kernels  62.1 us (48%)
  starting transfers between devices  30.1 us (23%)
  waiting for transfers between devices  22 us (17%)
  local copies, waits for them, and re-layouts  10.9 us (8%)
  other arithmetic  2.31 us (2%)
  between operations  1.84 us (1%)
    pallas_call x1, Pallas kernels, encode(): pl.pallas_call(functools.partial(encode_kernel, len(packed)), in_specs=[p...  34.7 us
    ppermute x16, starting transfers between devices, swap(): lax.ppermute(value, axis, [(i, i ^ mask) for i in range(lax.axis_size(axi...  20.5 us
    ppermute x16, waiting for transfers between devices, swap(): lax.ppermute(value, axis, [(i, i ^ mask) for i in range(lax.axis_size(axi...  17.6 us
    pallas_call x3, Pallas kernels, project(): pl.pallas_call(functools.partial(project_kernel, [n for _, n in pieces]),...  13.4 us
    ppermute x1, starting transfers between devices, exchange_rims(): above = lax.ppermute(lines(UPPER), ('date', 'tile'), forward(rows))  8.32 us
    pallas_call x1, Pallas kernels, compose(): pl.pallas_call(functools.partial(compose_kernel, classes), in_specs=[whol...  7.6 us
    unnamed x50, local copies, waits for them, and re-layouts  6.81 us
    pallas_call x1, Pallas kernels, prepare_weights(): pl.pallas_call(prepare_kernel, in_specs=[whole] * 5 + [pl.BlockSpec(memor...  4.63 us
  transfers between devices with their start and end apart: 18, of which 9 were waited for; matrix products, arithmetic and copies ran while one was open for 5% of the time, Pallas kernels for 11%

profile of v6, /device:TPU:0, one launch (start us, length us, event | category | flops | bytes accessed | tf_op | source)
XLA Modules:
  0.0 129.3 jit_solution(17786821995657784397)
XLA Ops:
  0.0 1.8 %copy-done.3 = bf16[1,16,1,1,4,16,1280]{6,5,4,3,2,1,0:T(8,128)(2,1)S(1)} copy-done((bf16[1,16,1,1,4,16,1280]{6,5,4,3,2,1,0:T(8,128)(2,1)S(1)}, bf16[1,16,1,1,4,16,1280]{6,5,4,3,2,1,0:T(8,128)(2,1)}, u32[]{:S(2)}) %copy-start.3) | copy-done | bytes 2621464
  1.8 0.7 copy-done.17
  2.4 1.8 %gather_pieces.1 = (bf16[4,64,1280]{2,1,0:T(8,128)(2,1)}, bf16[4,64,1280]{2,1,0:T(8,128)(2,1)}, bf16[1,64,1280]{2,1,0:T(8,128)(2,1)S(1)}, bf16[1,64,1280]{2,1,0:...) custom-call(s32[16]{0:T(128)S(1)} %bitcast.20, ...), custom_call_target="tpu_custom_call" | custom-call | tf_op jit(solution)/shard_map/gather_pieces/pallas_call | solution.py:65
  4.3 0.7 copy-done.18
  4.9 4.0 %collective-permute-start.10 = (bf16[4,64,1280]{2,1,0:T(8,128)(2,1)}, bf16[4,64,1280]{2,1,0:T(8,128)(2,1)S(1)}, u32[]{:S(2)}, u32[]{:S(2)}) collective-permute-start(bf16[4,64,1280]{2,1,0:T(8,128)(2,1)} %get-tuple-element.56), channel_id=1, source_target_pairs={{0,4},{2,6},{4,0},{6,2},{1,5},{3,7},{5,1},{7,3},{8,12},{10,14},{12... | collective-permute-start | bytes 1966088 | tf_op jit(solution)/shard_map/ppermute | solution.py:78
  9.0 0.7 collective-permute-start.2
  9.6 0.9 collective-permute-start.1
  10.5 0.3 collective-permute-start
  10.8 1.6 %collective-permute-start.6 = (bf16[4,64,1280]{2,1,0:T(8,128)(2,1)}, bf16[4,64,1280]{2,1,0:T(8,128)(2,1)S(1)}, u32[]{:S(2)}, u32[]{:S(2)}) collective-permute-start(bf16[4,64,1280]{2,1,0:T(8,128)(2,1)} %get-tuple-element.50), channel_id=1, source_target_pairs={{0,2},{2,0},{4,6},{6,4},{1,3},{3,1},{5,7},{7,5},{8,10},{10,8},{12,... | collective-permute-start | bytes 1966088 | tf_op jit(solution)/shard_map/ppermute | solution.py:78
  13.1 0.6 broadcast_in_dim.23.refs_11_
  13.7 0.6 broadcast_in_dim.24.refs_13_
  14.9 0.7 pad_add_fusion.place_ref
  15.6 3.4 %collective-permute-done.1 = bf16[1,64,1280]{2,1,0:T(8,128)(2,1)S(1)} collective-permute-done((bf16[1,64,1280]{2,1,0:T(8,128)(2,1)S(1)}, bf16[1,64,1280]{2,1,0:T(8,128)(2,1)S(1)}, u32[]{:S(2)}, u32[]{:S(2)}) %collective-permute-start.1) | collective-permute-done | bytes 163872 | tf_op jit(solution)/shard_map/ppermute | solution.py:78
  19.0 0.9 pad_maximum_fusion
  19.9 0.1 collective-permute-start.3
  20.0 1.3 collective-permute-start.4
  21.3 2.7 %copy.23.up_ref = bf16[256,3136]{1,0:T(8,128)(2,1)S(1)} copy(bf16[256,3136]{0,1:T(8,128)(2,1)} %param.34) | data formatting | bytes 3211264 | tf_op jit(solution)/shard_map/optimization_barrier | solution.py:641
  24.0 0.7 convert_element_type.18
  24.7 0.8 copy-done.10
  25.5 0.8 copy-done.11
  26.3 0.7 copy-done.14
  27.0 4.6 %prepare_weights.1 = (bf16[16,256,256]{2,1,0:T(8,128)(2,1)S(1)}, bf16[2,256,256]{2,1,0:T(8,128)(2,1)S(1)}, bf16[1280,3840]{1,0:T(8,128)(2,1)S(1)}) custom-call(bf16[256,3136]{1,0:T(8,128)(2,1)S(1)} %copy.23.up_ref, bf16[9,13,16]{2,1,0:T(8,128)(2,1)S(1)} %copy-done.11, bf16[256,13]{1,0:T(8,128)(2,1)S(1)} %copy-done.10, bf16[16,224]{1,0:T(8,128)(2,1)S(1)} %copy-done.14, ...), custom_call_target="tpu_custom_call" | custom-call | tf_op jit(solution)/shard_map/prepare_weights/pallas_call | solution.py:406
  31.6 1.3 %copy-done.4 = bf16[16,256,256]{2,1,0:T(8,128)(2,1)} copy-done((bf16[16,256,256]{2,1,0:T(8,128)(2,1)}, bf16[16,256,256]{2,1,0:T(8,128)(2,1)S(1)}, u32[]{:S(2)}) %copy-start.4) | copy-done | bytes 2097176
  33.0 0.1 fusion.2.refs_8_.refs_4_.refs_1_.refs_9_
  33.1 5.0 %collective-permute-done.10.refs_0_ = bf16[4,64,1280]{2,1,0:T(8,128)(2,1)S(1)} collective-permute-done((bf16[4,64,1280]{2,1,0:T(8,128)(2,1)}, bf16[4,64,1280]{2,1,0:T(8,128)(2,1)S(1)}, u32[]{:S(2)}, u32[]{:S(2)}) %collective-permute-start.10) | collective-permute-done | bytes 655392 | tf_op jit(solution)/shard_map/ppermute | solution.py:78
  38.1 0.1 collective-permute-start.11
  38.2 1.6 %collective-permute-start.12 = (bf16[1,64,1280]{2,1,0:T(8,128)(2,1)S(1)}, bf16[1,64,1280]{2,1,0:T(8,128)(2,1)S(1)}, u32[]{:S(2)}, u32[]{:S(2)}) collective-permute-start(bf16[1,64,1280]{2,1,0:T(8,128)(2,1)S(1)} %get-tuple-element.74), channel_id=1, source_target_pairs={{0,16},{8,24},{16,0},{24,8},{1,17},{9,25},{17,1},{25,9},{2,18},{10... | collective-permute-start | bytes 491528 | tf_op jit(solution)/shard_map/ppermute | solution.py:78
  39.8 0.3 collective-permute-start.13
  40.0 0.7 collective-permute-done.6.refs_4_
  40.7 2.9 %collective-permute-start.14 = (bf16[4,64,1280]{2,1,0:T(8,128)(2,1)S(1)}, bf16[4,64,1280]{2,1,0:T(8,128)(2,1)S(1)}, u32[]{:S(2)}, u32[]{:S(2)}) collective-permute-start(bf16[4,64,1280]{2,1,0:T(8,128)(2,1)S(1)} %copy-done.20), channel_id=1, source_target_pairs={{0,6},{2,4},{4,2},{6,0},{1,7},{3,5},{5,3},{7,1},{8,14},{10,12},{12... | collective-permute-start | bytes 1966088 | tf_op jit(solution)/shard_map/ppermute | solution.py:78
  43.6 1.2 collective-permute-start.5
  44.9 0.4 collective-permute-start.7
  45.3 1.5 %collective-permute-start.8 = (bf16[1,64,1280]{2,1,0:T(8,128)(2,1)S(1)}, bf16[1,64,1280]{2,1,0:T(8,128)(2,1)S(1)}, u32[]{:S(2)}, u32[]{:S(2)}) collective-permute-start(bf16[1,64,1280]{2,1,0:T(8,128)(2,1)S(1)} %get-tuple-element.77), channel_id=1, source_target_pairs={{0,16},{8,24},{16,0},{24,8},{1,17},{9,25},{17,1},{25,9},{2,18},{10... | collective-permute-start | bytes 491528 | tf_op jit(solution)/shard_map/ppermute | solution.py:78
  46.8 1.1 collective-permute-done.13.refs_3_
  47.8 2.2 %collective-permute-start.9 = (bf16[1,64,1280]{2,1,0:T(8,128)(2,1)S(1)}, bf16[1,64,1280]{2,1,0:T(8,128)(2,1)S(1)}, u32[]{:S(2)}, u32[]{:S(2)}) collective-permute-start(bf16[1,64,1280]{2,1,0:T(8,128)(2,1)S(1)} %get-tuple-element.76), channel_id=1, source_target_pairs={{0,24},{8,16},{16,8},{24,0},{1,25},{9,17},{17,9},{25,1},{2,26},{10... | collective-permute-start | bytes 491528 | tf_op jit(solution)/shard_map/ppermute | solution.py:78
  50.0 3.1 %project.4 = (bf16[3840,256]{1,0:T(8,128)(2,1)S(1)}, f32[32,128]{1,0:T(8,128)S(1)}, bf16[256,1280]{1,0:T(8,128)(2,1)S(1)}) custom-call(bf16[4,64,1280]{2,1,0:T(8,128)(2,1)S(1)} %collective-permute-done.10.refs_0_, bf16[1,64,1280]{2,1,0:T(8,128)(2,1)S(1)} %collective-permute-done.11.refs_1_, bf16[1,64,1280]{2,1,0:T(8,128)(2,1)S(1)} %collective-permute-done.12.refs_2_, ...), custom_call_target="tpu_custom_call" | custom-call | tf_op jit(solution)/shard_map/project/pallas_call | solution.py:155
  53.2 2.6 %collective-permute-done.8.refs_6_ = bf16[1,64,1280]{2,1,0:T(8,128)(2,1)S(1)} collective-permute-done((bf16[1,64,1280]{2,1,0:T(8,128)(2,1)S(1)}, bf16[1,64,1280]{2,1,0:T(8,128)(2,1)S(1)}, u32[]{:S(2)}, u32[]{:S(2)}) %collective-permute-start.8) | collective-permute-done | bytes 163872 | tf_op jit(solution)/shard_map/ppermute | solution.py:78
  55.8 2.6 %collective-permute-done.9.refs_7_ = bf16[1,64,1280]{2,1,0:T(8,128)(2,1)S(1)} collective-permute-done((bf16[1,64,1280]{2,1,0:T(8,128)(2,1)S(1)}, bf16[1,64,1280]{2,1,0:T(8,128)(2,1)S(1)}, u32[]{:S(2)}, u32[]{:S(2)}) %collective-permute-start.9) | collective-permute-done | bytes 163872 | tf_op jit(solution)/shard_map/ppermute | solution.py:78
  58.4 7.0 %project.3 = (bf16[3840,512]{1,0:T(8,128)(2,1)S(1)}, f32[32,128]{1,0:T(8,128)S(1)}, bf16[512,1280]{1,0:T(8,128)(2,1)S(1)}) custom-call(bf16[1,64,1280]{2,1,0:T(8,128)(2,1)S(1)} %get-tuple-element.39.refs_0_, bf16[1,64,1280]{2,1,0:T(8,128)(2,1)} %collective-permute-done.3.refs_1_, bf16[1,64,1280]{2,1,0:T(8,128)(2,1)} %collective-permute-done.4.refs_2_, ...), custom_call_target="tpu_custom_call" | custom-call | tf_op jit(solution)/shard_map/project/pallas_call | solution.py:155
  65.4 3.3 %project.5 = (bf16[3840,256]{1,0:T(8,128)(2,1)S(1)}, f32[32,128]{1,0:T(8,128)S(1)}, bf16[256,1280]{1,0:T(8,128)(2,1)S(1)}) custom-call(bf16[4,64,1280]{2,1,0:T(8,128)(2,1)S(1)} %collective-permute-done.14.refs_0_, f32[1,1280]{1,0:T(1,128)S(1)} %fusion.2.refs_8_.refs_4_.refs_1_.refs_9_, bf16[1,1280]{1,0:T(2,128)(2,1)S(1)} %broadcast_in_dim.22.refs_9_.refs_5_.refs_2_, ...), custom_call_target="tpu_custom_call" | custom-call | tf_op jit(solution)/shard_map/project/pallas_call | solution.py:155
  68.8 34.7 %encode.1 = (bf16[256,256]{1,0:T(8,128)(2,1)S(1)}, bf16[48,256]{1,0:T(8,128)(2,1)S(1)}, bf16[48,256]{1,0:T(8,128)(2,1)}) custom-call(s32[3]{0:T(128)S(1)} %copy-done.15, bf16[3840,512]{1,0:T(8,128)(2,1)S(1)} %get-tuple-element.55.refs_0_, bf16[3840,256]{1,0:T(8,128)(2,1)S(1)} %get-tuple-element.59.refs_1_, bf16[3840,256]{1,0:T(8,128)(2,1)S(1)} %get-tuple-element.61.refs_2_, ...), custom_call_target="tpu_custom_call" | custom-call | tf_op jit(solution)/shard_map/encode/pallas_call | solution.py:262
  103.5 1.6 %collective-permute-start.15 = (bf16[48,256]{1,0:T(8,128)(2,1)S(1)}, bf16[48,256]{1,0:T(8,128)(2,1)S(1)}, u32[]{:S(2)}, u32[]{:S(2)}) collective-permute-start(bf16[48,256]{1,0:T(8,128)(2,1)S(1)} %get-tuple-element.70), channel_id=1, source_target_pairs={{0,1},{1,0},{2,3},{3,2},{4,5},{5,4},{6,7},{7,6},{8,9},{9,8},{10,11... | collective-permute-start | bytes 73736 | tf_op jit(solution)/shard_map/ppermute | solution.py:78
  105.1 2.2 %collective-permute-done.15 = bf16[48,256]{1,0:T(8,128)(2,1)S(1)} collective-permute-done((bf16[48,256]{1,0:T(8,128)(2,1)S(1)}, bf16[48,256]{1,0:T(8,128)(2,1)S(1)}, u32[]{:S(2)}, u32[]{:S(2)}) %collective-permute-start.15) | collective-permute-done | bytes 24608 | tf_op jit(solution)/shard_map/ppermute | solution.py:78
  107.4 8.3 %collective-permute-start.16 = (bf16[48,256]{1,0:T(8,128)(2,1)S(1)}, bf16[48,256]{1,0:T(8,128)(2,1)S(1)}, u32[]{:S(2)}, u32[]{:S(2)}) collective-permute-start(bf16[48,256]{1,0:T(8,128)(2,1)S(1)} %concatenate.12), channel_id=1, source_target_pairs={{0,2},{2,4},{4,6},{6,8},{8,10},{10,12},{12,14},{14,16},{16,18},{18... | collective-permute-start | bytes 73736 | tf_op jit(solution)/shard_map/ppermute | solution.py:587
  115.8 1.3 collective-permute-start.17
  117.1 0.1 collective-permute-done.16.above_ref
  117.3 4.3 %collective-permute-done.17.below_ref = bf16[48,256]{1,0:T(8,128)(2,1)S(1)} collective-permute-done((bf16[48,256]{1,0:T(8,128)(2,1)S(1)}, bf16[48,256]{1,0:T(8,128)(2,1)S(1)}, u32[]{:S(2)}, u32[]{:S(2)}) %collective-permute-start.17) | collective-permute-done | bytes 24608 | tf_op jit(solution)/shard_map/ppermute | solution.py:588
  121.6 7.6 %compose.1 = f32[13,192,192]{2,1,0:T(8,128)} custom-call(bf16[256,256]{1,0:T(8,128)(2,1)S(1)} %get-tuple-element.69.own_ref, bf16[48,256]{1,0:T(8,128)(2,1)S(1)} %get-tuple-element.98.before_ref, bf16[48,256]{1,0:T(8,128)(2,1)S(1)} %get-tuple-element.97.after_ref, bf16[48,256]{1,0:T(8,128)(2,1)S(1)} %collective-permute-done.16.above_ref, ...), custom_call_target="tpu_custom_call" | custom-call | tf_op jit(solution)/shard_map/compose/pallas_call | solution.py:597
  (66 shorter events, 0.4 us)
Async XLA Ops:
  0.0 33.0 %copy-start = (bf16[16,1280]{1,0:T(8,128)(2,1)S(1)}, bf16[16,1280]{1,0:T(8,128)(2,1)}, u32[]{:S(2)}) copy-start(bf16[16,1280]{1,0:T(8,128)(2,1)} %param.27) | copy-start | bytes 122884
  0.0 13.7 %copy-start.23 = (bf16[256]{0:T(256)(128)(2,1)S(1)}, bf16[256]{0:T(256)(128)(2,1)}, u32[]{:S(2)}) copy-start(bf16[256]{0:T(256)(128)(2,1)} %param.33) | copy-start | bytes 1540
  0.0 1.8 %copy-start.3 = (bf16[1,16,1,1,4,16,1280]{6,5,4,3,2,1,0:T(8,128)(2,1)S(1)}, bf16[1,16,1,1,4,16,1280]{6,5,4,3,2,1,0:T(8,128)(2,1)}, u32[]{:S(2)}) copy-start(bf16[1,16,1,1,4,16,1280]{6,5,4,3,2,1,0:T(8,128)(2,1)} %param.22) | copy-start | bytes 7864324
  1.8 0.7 copy-start.17
  2.4 10.6 %copy-start.21 = (bf16[1280]{0:T(1024)(128)(2,1)S(1)}, bf16[1280]{0:T(1024)(128)(2,1)}, u32[]{:S(2)}) copy-start(bf16[1280]{0:T(1024)(128)(2,1)} %param.28) | copy-start | bytes 7684
  2.4 10.7 %copy-start.22 = (bf16[1280]{0:T(1024)(128)(2,1)S(1)}, bf16[1280]{0:T(1024)(128)(2,1)}, u32[]{:S(2)}) copy-start(bf16[1280]{0:T(1024)(128)(2,1)} %param.31) | copy-start | bytes 7684
  4.3 0.7 copy-start.18
  4.9 19.7 %copy-start.5 = (bf16[3,256,224]{2,1,0:T(8,128)(2,1)S(1)}, bf16[3,256,224]{2,1,0:T(8,128)(2,1)}, u32[]{:S(2)}) copy-start(bf16[3,256,224]{2,1,0:T(8,128)(2,1)} %constant.34.clone.meet_ref) | copy-start | bytes 1032196
  4.9 33.1 %collective-permute-start.10 = (bf16[4,64,1280]{2,1,0:T(8,128)(2,1)}, bf16[4,64,1280]{2,1,0:T(8,128)(2,1)S(1)}, u32[]{:S(2)}, u32[]{:S(2)}) collective-permute-start(bf16[4,64,1280]{2,1,0:T(8,128)(2,1)} %get-tuple-element.56), channel_id=1, source_target_pairs={{0,4},{2,6},{4,0},{6,2},{1,5},{3,7},{5,1},{7,3},{8,12},{10,14},{12... | collective-permute-start | bytes 1966088 | tf_op jit(solution)/shard_map/ppermute | solution.py:78
  9.0 6.6 %collective-permute-start.2 = (bf16[1,64,1280]{2,1,0:T(8,128)(2,1)S(1)}, bf16[1,64,1280]{2,1,0:T(8,128)(2,1)S(1)}, u32[]{:S(2)}, u32[]{:S(2)}) collective-permute-start(bf16[1,64,1280]{2,1,0:T(8,128)(2,1)S(1)} %get-tuple-element.46), channel_id=1, source_target_pairs={{0,24},{8,16},{16,8},{24,0},{1,25},{9,17},{17,9},{25,1},{2,26},{10... | collective-permute-start | bytes 491528 | tf_op jit(solution)/shard_map/ppermute | solution.py:78
  9.6 9.4 %collective-permute-start.1 = (bf16[1,64,1280]{2,1,0:T(8,128)(2,1)S(1)}, bf16[1,64,1280]{2,1,0:T(8,128)(2,1)S(1)}, u32[]{:S(2)}, u32[]{:S(2)}) collective-permute-start(bf16[1,64,1280]{2,1,0:T(8,128)(2,1)S(1)} %get-tuple-element.45), channel_id=1, source_target_pairs={{0,16},{8,24},{16,0},{24,8},{1,17},{9,25},{17,1},{25,9},{2,18},{10... | collective-permute-start | bytes 491528 | tf_op jit(solution)/shard_map/ppermute | solution.py:78
  10.5 8.5 %collective-permute-start = (bf16[1,64,1280]{2,1,0:T(8,128)(2,1)S(1)}, bf16[1,64,1280]{2,1,0:T(8,128)(2,1)S(1)}, u32[]{:S(2)}, u32[]{:S(2)}) collective-permute-start(bf16[1,64,1280]{2,1,0:T(8,128)(2,1)S(1)} %get-tuple-element.44), channel_id=1, source_target_pairs={{0,8},{8,0},{16,24},{24,16},{1,9},{9,1},{17,25},{25,17},{2,10},{10... | collective-permute-start | bytes 491528 | tf_op jit(solution)/shard_map/ppermute | solution.py:78
  10.8 29.9 %collective-permute-start.6 = (bf16[4,64,1280]{2,1,0:T(8,128)(2,1)}, bf16[4,64,1280]{2,1,0:T(8,128)(2,1)S(1)}, u32[]{:S(2)}, u32[]{:S(2)}) collective-permute-start(bf16[4,64,1280]{2,1,0:T(8,128)(2,1)} %get-tuple-element.50), channel_id=1, source_target_pairs={{0,2},{2,0},{4,6},{6,4},{1,3},{3,1},{5,7},{7,5},{8,10},{10,8},{12,... | collective-permute-start | bytes 1966088 | tf_op jit(solution)/shard_map/ppermute | solution.py:78
  19.9 19.9 %collective-permute-start.3 = (bf16[1,64,1280]{2,1,0:T(8,128)(2,1)}, bf16[1,64,1280]{2,1,0:T(8,128)(2,1)}, u32[]{:S(2)}, u32[]{:S(2)}) collective-permute-start(bf16[1,64,1280]{2,1,0:T(8,128)(2,1)} %get-tuple-element.47), channel_id=1, source_target_pairs={{0,8},{8,0},{16,24},{24,16},{1,9},{9,1},{17,25},{25,17},{2,10},{10... | collective-permute-start | bytes 491528 | tf_op jit(solution)/shard_map/ppermute | solution.py:78
  20.0 23.6 %collective-permute-start.4 = (bf16[1,64,1280]{2,1,0:T(8,128)(2,1)}, bf16[1,64,1280]{2,1,0:T(8,128)(2,1)}, u32[]{:S(2)}, u32[]{:S(2)}) collective-permute-start(bf16[1,64,1280]{2,1,0:T(8,128)(2,1)} %get-tuple-element.48), channel_id=1, source_target_pairs={{0,16},{8,24},{16,0},{24,8},{1,17},{9,25},{17,1},{25,9},{2,18},{10... | collective-permute-start | bytes 491528 | tf_op jit(solution)/shard_map/ppermute | solution.py:78
  24.7 0.8 copy-start.10
  25.5 0.8 copy-start.11
  26.3 0.7 copy-start.14
  27.0 13.8 %copy-start.20 = (bf16[4,64,1280]{2,1,0:T(8,128)(2,1)S(1)}, bf16[4,64,1280]{2,1,0:T(8,128)(2,1)}, u32[]{:S(2)}) copy-start(bf16[4,64,1280]{2,1,0:T(8,128)(2,1)} %pad_maximum_fusion) | copy-start | bytes 1966084
  27.0 16.7 %copy-start.19 = (bf16[1,64,1280]{2,1,0:T(8,128)(2,1)S(1)}, bf16[1,64,1280]{2,1,0:T(8,128)(2,1)}, u32[]{:S(2)}) copy-start(bf16[1,64,1280]{2,1,0:T(8,128)(2,1)} %copy-done.18) | copy-start | bytes 491524
  31.6 1.3 %copy-start.4 = (bf16[16,256,256]{2,1,0:T(8,128)(2,1)}, bf16[16,256,256]{2,1,0:T(8,128)(2,1)S(1)}, u32[]{:S(2)}) copy-start(bf16[16,256,256]{2,1,0:T(8,128)(2,1)S(1)} %get-tuple-element.71.m_ref) | copy-start | bytes 6291460
  33.0 20.2 %copy-start.8 = (bf16[2,256,256]{2,1,0:T(8,128)(2,1)}, bf16[2,256,256]{2,1,0:T(8,128)(2,1)S(1)}, u32[]{:S(2)}) copy-start(bf16[2,256,256]{2,1,0:T(8,128)(2,1)S(1)} %get-tuple-element.72.edge_ref) | copy-start | bytes 786436
  38.1 6.8 %collective-permute-start.11 = (bf16[1,64,1280]{2,1,0:T(8,128)(2,1)S(1)}, bf16[1,64,1280]{2,1,0:T(8,128)(2,1)S(1)}, u32[]{:S(2)}, u32[]{:S(2)}) collective-permute-start(bf16[1,64,1280]{2,1,0:T(8,128)(2,1)S(1)} %get-tuple-element.75), channel_id=1, source_target_pairs={{0,8},{8,0},{16,24},{24,16},{1,9},{9,1},{17,25},{25,17},{2,10},{10... | collective-permute-start | bytes 491528 | tf_op jit(solution)/shard_map/ppermute | solution.py:78
  38.2 7.2 %collective-permute-start.12 = (bf16[1,64,1280]{2,1,0:T(8,128)(2,1)S(1)}, bf16[1,64,1280]{2,1,0:T(8,128)(2,1)S(1)}, u32[]{:S(2)}, u32[]{:S(2)}) collective-permute-start(bf16[1,64,1280]{2,1,0:T(8,128)(2,1)S(1)} %get-tuple-element.74), channel_id=1, source_target_pairs={{0,16},{8,24},{16,0},{24,8},{1,17},{9,25},{17,1},{25,9},{2,18},{10... | collective-permute-start | bytes 491528 | tf_op jit(solution)/shard_map/ppermute | solution.py:78
  39.8 8.1 %collective-permute-start.13 = (bf16[1,64,1280]{2,1,0:T(8,128)(2,1)S(1)}, bf16[1,64,1280]{2,1,0:T(8,128)(2,1)S(1)}, u32[]{:S(2)}, u32[]{:S(2)}) collective-permute-start(bf16[1,64,1280]{2,1,0:T(8,128)(2,1)S(1)} %get-tuple-element.73), channel_id=1, source_target_pairs={{0,24},{8,16},{16,8},{24,0},{1,25},{9,17},{17,9},{25,1},{2,26},{10... | collective-permute-start | bytes 491528 | tf_op jit(solution)/shard_map/ppermute | solution.py:78
  40.7 24.7 %collective-permute-start.14 = (bf16[4,64,1280]{2,1,0:T(8,128)(2,1)S(1)}, bf16[4,64,1280]{2,1,0:T(8,128)(2,1)S(1)}, u32[]{:S(2)}, u32[]{:S(2)}) collective-permute-start(bf16[4,64,1280]{2,1,0:T(8,128)(2,1)S(1)} %copy-done.20), channel_id=1, source_target_pairs={{0,6},{2,4},{4,2},{6,0},{1,7},{3,5},{5,3},{7,1},{8,14},{10,12},{12... | collective-permute-start | bytes 1966088 | tf_op jit(solution)/shard_map/ppermute | solution.py:78
  43.6 9.5 %collective-permute-start.5 = (bf16[1,64,1280]{2,1,0:T(8,128)(2,1)S(1)}, bf16[1,64,1280]{2,1,0:T(8,128)(2,1)S(1)}, u32[]{:S(2)}, u32[]{:S(2)}) collective-permute-start(bf16[1,64,1280]{2,1,0:T(8,128)(2,1)S(1)} %copy-done.19), channel_id=1, source_target_pairs={{0,24},{8,16},{16,8},{24,0},{1,25},{9,17},{17,9},{25,1},{2,26},{10... | collective-permute-start | bytes 491528 | tf_op jit(solution)/shard_map/ppermute | solution.py:78
  44.9 8.3 %collective-permute-start.7 = (bf16[1,64,1280]{2,1,0:T(8,128)(2,1)S(1)}, bf16[1,64,1280]{2,1,0:T(8,128)(2,1)S(1)}, u32[]{:S(2)}, u32[]{:S(2)}) collective-permute-start(bf16[1,64,1280]{2,1,0:T(8,128)(2,1)S(1)} %get-tuple-element.78), channel_id=1, source_target_pairs={{0,8},{8,0},{16,24},{24,16},{1,9},{9,1},{17,25},{25,17},{2,10},{10... | collective-permute-start | bytes 491528 | tf_op jit(solution)/shard_map/ppermute | solution.py:78
  45.3 10.4 %collective-permute-start.8 = (bf16[1,64,1280]{2,1,0:T(8,128)(2,1)S(1)}, bf16[1,64,1280]{2,1,0:T(8,128)(2,1)S(1)}, u32[]{:S(2)}, u32[]{:S(2)}) collective-permute-start(bf16[1,64,1280]{2,1,0:T(8,128)(2,1)S(1)} %get-tuple-element.77), channel_id=1, source_target_pairs={{0,16},{8,24},{16,0},{24,8},{1,17},{9,25},{17,1},{25,9},{2,18},{10... | collective-permute-start | bytes 491528 | tf_op jit(solution)/shard_map/ppermute | solution.py:78
  47.8 10.5 %collective-permute-start.9 = (bf16[1,64,1280]{2,1,0:T(8,128)(2,1)S(1)}, bf16[1,64,1280]{2,1,0:T(8,128)(2,1)S(1)}, u32[]{:S(2)}, u32[]{:S(2)}) collective-permute-start(bf16[1,64,1280]{2,1,0:T(8,128)(2,1)S(1)} %get-tuple-element.76), channel_id=1, source_target_pairs={{0,24},{8,16},{16,8},{24,0},{1,25},{9,17},{17,9},{25,1},{2,26},{10... | collective-permute-start | bytes 491528 | tf_op jit(solution)/shard_map/ppermute | solution.py:78
  65.4 3.4 %copy-start.1 = (bf16[1280,1280]{1,0:T(8,128)(2,1)S(1)}, bf16[1280,1280]{1,0:T(8,128)(2,1)}, u32[]{:S(2)}) copy-start(bf16[1280,1280]{1,0:T(8,128)(2,1)} %refs_10_.1) | copy-start | bytes 9830404
  65.4 3.4 %copy-start.2 = (bf16[5120,256]{1,0:T(8,128)(2,1)S(1)}, bf16[5120,256]{1,0:T(8,128)(2,1)}, u32[]{:S(2)}) copy-start(bf16[5120,256]{1,0:T(8,128)(2,1)} %param.32) | copy-start | bytes 7864324
  65.4 3.4 %copy-start.13 = (bf16[1,1280]{1,0:T(2,128)(2,1)S(1)}, bf16[1,1280]{1,0:T(2,128)(2,1)}, u32[]{:S(2)}) copy-start(bf16[1,1280]{1,0:T(2,128)(2,1)} %broadcast_in_dim.23.refs_11_) | copy-start | bytes 7684
  65.4 3.4 %copy-start.15 = (s32[3]{0:T(128)S(1)}, s32[3]{0:T(128)}, u32[]{:S(2)}) copy-start(s32[3]{0:T(128)} %pad_add_fusion.place_ref) | copy-start | bytes 40
  65.4 3.4 %copy-start.16 = (bf16[1,256]{1,0:T(2,128)(2,1)S(1)}, bf16[1,256]{1,0:T(2,128)(2,1)}, u32[]{:S(2)}) copy-start(bf16[1,256]{1,0:T(2,128)(2,1)} %broadcast_in_dim.24.refs_13_) | copy-start | bytes 1540
  68.8 48.3 %copy-start.24 = (bf16[13]{0:T(256)(128)(2,1)S(1)}, bf16[13]{0:T(256)(128)(2,1)}, u32[]{:S(2)}) copy-start(bf16[13]{0:T(256)(128)(2,1)} %param.36) | copy-start | bytes 82
  68.8 52.8 %copy-start.6 = (bf16[3,256,192]{2,1,0:T(8,128)(2,1)S(1)}, bf16[3,256,192]{2,1,0:T(8,128)(2,1)}, u32[]{:S(2)}) copy-start(bf16[3,256,192]{2,1,0:T(8,128)(2,1)} %constant.36.clone.window_ref) | copy-start | bytes 884740
  68.8 52.7 %copy-start.7 = (bf16[3,256,192]{2,1,0:T(8,128)(2,1)S(1)}, bf16[3,256,192]{2,1,0:T(8,128)(2,1)}, u32[]{:S(2)}) copy-start(bf16[3,256,192]{2,1,0:T(8,128)(2,1)} %constant.37.clone.place_ref) | copy-start | bytes 884740
  68.8 52.7 %copy-start.9 = (bf16[2,256,256]{2,1,0:T(8,128)(2,1)S(1)}, bf16[2,256,256]{2,1,0:T(8,128)(2,1)}, u32[]{:S(2)}) copy-start(bf16[2,256,256]{2,1,0:T(8,128)(2,1)} %copy-done.8) | copy-start | bytes 786436
  68.8 52.7 %copy-start.12 = (bf16[3,16,192]{2,1,0:T(8,128)(2,1)S(1)}, bf16[3,16,192]{2,1,0:T(8,128)(2,1)}, u32[]{:S(2)}) copy-start(bf16[3,16,192]{2,1,0:T(8,128)(2,1)} %constant.38.clone.side_ref) | copy-start | bytes 55300
  103.5 3.8 %collective-permute-start.15 = (bf16[48,256]{1,0:T(8,128)(2,1)S(1)}, bf16[48,256]{1,0:T(8,128)(2,1)S(1)}, u32[]{:S(2)}, u32[]{:S(2)}) collective-permute-start(bf16[48,256]{1,0:T(8,128)(2,1)S(1)} %get-tuple-element.70), channel_id=1, source_target_pairs={{0,1},{1,0},{2,3},{3,2},{4,5},{5,4},{6,7},{7,6},{8,9},{9,8},{10,11... | collective-permute-start | bytes 73736 | tf_op jit(solution)/shard_map/ppermute | solution.py:78
  107.4 9.8 %collective-permute-start.16 = (bf16[48,256]{1,0:T(8,128)(2,1)S(1)}, bf16[48,256]{1,0:T(8,128)(2,1)S(1)}, u32[]{:S(2)}, u32[]{:S(2)}) collective-permute-start(bf16[48,256]{1,0:T(8,128)(2,1)S(1)} %concatenate.12), channel_id=1, source_target_pairs={{0,2},{2,4},{4,6},{6,8},{8,10},{10,12},{12,14},{14,16},{16,18},{18... | collective-permute-start | bytes 73736 | tf_op jit(solution)/shard_map/ppermute | solution.py:587
  115.8 5.7 %collective-permute-start.17 = (bf16[48,256]{1,0:T(8,128)(2,1)S(1)}, bf16[48,256]{1,0:T(8,128)(2,1)S(1)}, u32[]{:S(2)}, u32[]{:S(2)}) collective-permute-start(bf16[48,256]{1,0:T(8,128)(2,1)S(1)} %concatenate.13), channel_id=1, source_target_pairs={{2,0},{4,2},{6,4},{8,6},{10,8},{12,10},{14,12},{16,14},{18,16},{20... | collective-permute-start | bytes 73736 | tf_op jit(solution)/shard_map/ppermute | solution.py:588
